TPU v7x, 32 devices: a whole 2x2x4 slice. The times are simulated.
32 devices in a mesh: row: 4 (over y, core), col: 8 (over z, x).
Axes of the slice: x: 2, y: 2, z: 4, core: 2. Of those that a mesh axis runs over, the one named last changes fastest.
Arguments:
- latents: bfloat16 [16384, 1152], P(('row', 'col')), may hold values from -6 to 6
- condition: bfloat16 [16, 1152], P('row'), may hold values from -6 to 6
- ada_weight: bfloat16 [1152, 6, 1152], P('row', None, 'col'), may hold values from -0.1875 to 0.1875
- ada_bias: bfloat16 [6, 1152], P(None, 'col'), may hold values from -3 to 3
- qkv_weight: bfloat16 [1152, 3, 1152], P('row', None, 'col'), may hold values from -0.1875 to 0.1875
- qv_bias: bfloat16 [2, 1152], P(None, 'col'), may hold values from -3 to 3
- proj_weight: bfloat16 [1152, 1152], P('col', 'row'), may hold values from -0.75 to 0.75
- proj_bias: bfloat16 [1152], P('col'), may hold values from -2 to 2
- fc1_weight: bfloat16 [1152, 4608], P('row', 'col'), may hold values from -0.1875 to 0.1875
- fc1_bias: bfloat16 [4608], P('col'), may hold values from -3 to 3
- fc2_weight: bfloat16 [4608, 1152], P('col', 'row'), may hold values from -0.125 to 0.125
- fc2_bias: bfloat16 [1152], P('col'), may hold values from -2 to 2
- cotangent: bfloat16 [16384, 1152], P(('row', 'col')), may hold values from -6 to 6
Outputs:
- output: bfloat16 [16384, 1152], P(('row', 'col'))
- latents_grad: float32 [16384, 1152], P(('row', 'col'))
- condition_grad: float32 [16, 1152], P('row')
- ada_weight_grad: float32 [1152, 6, 1152], P('row', None, 'col')
- ada_bias_grad: float32 [6, 1152], P(None, 'col')
- qkv_weight_grad: float32 [1152, 3, 1152], P('row', None, 'col')
- qv_bias_grad: float32 [2, 1152], P(None, 'col')
- proj_weight_grad: float32 [1152, 1152], P('col', 'row')
- proj_bias_grad: float32 [1152], P('col')
- fc1_weight_grad: float32 [1152, 4608], P('row', 'col')
- fc1_bias_grad: float32 [4608], P('col')
- fc2_weight_grad: float32 [4608, 1152], P('col', 'row')
- fc2_bias_grad: float32 [1152], P('col')
All inputs are finite; a program needn't handle non-finite values.
Results may differ from a plain program's by a relative error of at most 0.02.
Values may be sent and summed in bfloat16 or wider, within the bound.
A program may use at most 256 MiB of HBM per device.

v0:
```python
import jax
import jax.numpy as jnp
from jax import lax
from jax.sharding import PartitionSpec as P

HEAD_DIM = 72
SEQ = 1024


norm_eps = 1e-06
highest = lax.Precision.HIGHEST


def shards(
    latents,
    condition,
    ada_weight,
    ada_bias,
    qkv_weight,
    qv_bias,
    proj_weight,
    proj_bias,
    fc1_weight,
    fc1_bias,
    fc2_weight,
    fc2_bias,
    cotangent,
):
    lat_count = condition.shape[0]
    local_rows = latents.shape[0]
    full_width = latents.shape[1]
    col_count = lax.axis_size("col")
    tok_rows = local_rows * col_count
    head_count = qkv_weight.shape[2] // HEAD_DIM
    scale_factor = HEAD_DIM ** (-0.5)
    first_row = lax.axis_index("col") * local_rows
    owner = (first_row + jnp.arange(local_rows, dtype=jnp.int32)) // SEQ
    picker = (owner[:, None] == jnp.arange(lat_count, dtype=jnp.int32)[None, :]).astype(jnp.float32)

    def per_latent(rows):
        return lax.dot_general(
            picker,
            rows,
            (((0,), (0,)), ((), ())),
            precision=highest,
            preferred_element_type=jnp.float32,
        )

    ada_full, qkv_full, proj_full, fc1_full, fc2_full = (
        lax.all_gather(ada_weight, "row", axis=0, tiled=True),
        lax.all_gather(qkv_weight, "row", axis=0, tiled=True),
        lax.all_gather(proj_weight, "row", axis=1, tiled=True),
        lax.all_gather(fc1_weight, "row", axis=0, tiled=True),
        lax.all_gather(fc2_weight, "row", axis=1, tiled=True),
    )
    cond_float = condition.astype(jnp.float32)
    cond_act = jax.nn.silu(cond_float).astype(jnp.bfloat16)
    mod_block = jnp.einsum(
        "bd,dkc->bkc", cond_act, ada_full, preferred_element_type=jnp.float32
    ) + ada_bias.astype(jnp.float32)
    modulation, proj_bias_full, fc2_bias_full = (
        lax.all_gather(mod_block, "col", axis=2, tiled=True),
        lax.all_gather(proj_bias.astype(jnp.float32), "col", axis=0, tiled=True),
        lax.all_gather(fc2_bias.astype(jnp.float32), "col", axis=0, tiled=True),
    )
    mod_rows = jnp.dot(
        picker,
        modulation.reshape(lat_count, 6 * full_width),
        precision=highest,
        preferred_element_type=jnp.float32,
    ).reshape(local_rows, 6, full_width)
    shift_one = mod_rows[:, 0]
    scale_one = mod_rows[:, 1]
    gate_one = mod_rows[:, 2]
    shift_two = mod_rows[:, 3]
    scale_two = mod_rows[:, 4]
    gate_two = mod_rows[:, 5]

    def normed(values, shift, scale):
        mean = jnp.mean(values, axis=-1, keepdims=True)
        centred = values - mean
        inverse = lax.rsqrt(jnp.mean(centred * centred, axis=-1, keepdims=True) + norm_eps)
        normal = centred * inverse
        rows = (normal * (1.0 + scale) + shift).astype(jnp.bfloat16)
        gathered = lax.all_gather(rows, "col", axis=0, tiled=True)
        return (gathered, normal, inverse)

    def spread(grad_rows):
        return lax.all_gather(grad_rows.astype(jnp.bfloat16), "col", axis=0, tiled=True)

    def back_summed(term):
        return lax.psum_scatter(
            term.astype(jnp.bfloat16), "col", scatter_dimension=0, tiled=True
        ).astype(jnp.float32)

    def norm_back(rows_grad, normal, inverse, scale):
        shift_grad = per_latent(rows_grad)
        scale_grad = per_latent(rows_grad * normal)
        normal_grad = rows_grad * (1.0 + scale)
        first = jnp.mean(normal_grad, axis=-1, keepdims=True)
        second = jnp.mean(normal_grad * normal, axis=-1, keepdims=True)
        value_grad = inverse * (normal_grad - first - normal * second)
        return (value_grad, shift_grad, scale_grad)

    values = latents.astype(jnp.float32)
    normed_one, normal_one, inverse_one = normed(values, shift_one, scale_one)
    projected = jnp.einsum("td,dkc->tkc", normed_one, qkv_full, preferred_element_type=jnp.float32)
    qv_float = qv_bias.astype(jnp.float32)
    query = (
        (projected[:, 0] + qv_float[0])
        .astype(jnp.bfloat16)
        .reshape(lat_count, SEQ, head_count, HEAD_DIM)
    )
    key_vec = projected[:, 1].astype(jnp.bfloat16).reshape(lat_count, SEQ, head_count, HEAD_DIM)
    value_vec = (
        (projected[:, 2] + qv_float[1])
        .astype(jnp.bfloat16)
        .reshape(lat_count, SEQ, head_count, HEAD_DIM)
    )

    def attend(triple):
        query_blk, key_blk, value_blk = triple
        scores = (
            jnp.einsum("qhe,khe->hqk", query_blk, key_blk, preferred_element_type=jnp.float32)
            * scale_factor
        )
        top = jnp.max(scores, axis=-1, keepdims=True)
        expo = jnp.exp(scores - top)
        total = jnp.sum(expo, axis=-1, keepdims=True)
        probs = (expo / total).astype(jnp.bfloat16)
        result = jnp.einsum("hqk,khe->qhe", probs, value_blk, preferred_element_type=jnp.float32)
        return (result.astype(jnp.bfloat16), top + jnp.log(total))

    attended, log_total = lax.map(attend, (query, key_vec, value_vec))
    attended_flat = attended.reshape(tok_rows, head_count * HEAD_DIM)
    branch_a = lax.psum_scatter(
        jnp.dot(attended_flat, proj_full, preferred_element_type=jnp.float32).astype(jnp.bfloat16),
        "col",
        scatter_dimension=0,
        tiled=True,
    ).astype(jnp.float32)
    branch_a = branch_a + proj_bias_full
    middle = values + gate_one * branch_a
    normed_two, normal_two, inverse_two = normed(middle, shift_two, scale_two)
    pre_act = jnp.dot(normed_two, fc1_full, preferred_element_type=jnp.float32) + fc1_bias.astype(
        jnp.float32
    )
    hidden = jax.nn.gelu(pre_act, approximate=True).astype(jnp.bfloat16)
    branch_m = lax.psum_scatter(
        jnp.dot(hidden, fc2_full, preferred_element_type=jnp.float32).astype(jnp.bfloat16),
        "col",
        scatter_dimension=0,
        tiled=True,
    ).astype(jnp.float32)
    branch_m = branch_m + fc2_bias_full
    output = (middle + gate_two * branch_m).astype(jnp.bfloat16)
    grad_out = cotangent.astype(jnp.float32)
    gate_two_grad = per_latent(grad_out * branch_m)
    m_grad = grad_out * gate_two
    fc2_bias_part = jnp.sum(m_grad, axis=0)
    m_full = spread(m_grad)
    hidden_grad = lax.dot_general(
        m_full, fc2_full, (((1,), (1,)), ((), ())), preferred_element_type=jnp.float32
    )
    fc2_wgrad = lax.dot_general(
        hidden, m_full, (((0,), (0,)), ((), ())), preferred_element_type=jnp.float32
    )
    gelu_value, gelu_pull = jax.vjp(lambda inner: jax.nn.gelu(inner, approximate=True), pre_act)
    pre_grad = gelu_pull(hidden_grad)[0]
    fc1_bias_part = jnp.sum(pre_grad, axis=0)
    pre_low = pre_grad.astype(jnp.bfloat16)
    fc1_wgrad = lax.dot_general(
        normed_two, pre_low, (((0,), (0,)), ((), ())), preferred_element_type=jnp.float32
    )
    normed_two_grad = back_summed(
        lax.dot_general(
            pre_low, fc1_full, (((1,), (1,)), ((), ())), preferred_element_type=jnp.float32
        )
    )
    middle_part, shift_two_grad, scale_two_grad = norm_back(
        normed_two_grad, normal_two, inverse_two, scale_two
    )
    middle_grad = grad_out + middle_part
    gate_one_grad = per_latent(middle_grad * branch_a)
    a_grad = middle_grad * gate_one
    proj_bias_part = jnp.sum(a_grad, axis=0)
    a_full = spread(a_grad)
    attended_grad = lax.dot_general(
        a_full, proj_full, (((1,), (1,)), ((), ())), preferred_element_type=jnp.float32
    ).astype(jnp.bfloat16)
    proj_wgrad = lax.dot_general(
        attended_flat, a_full, (((0,), (0,)), ((), ())), preferred_element_type=jnp.float32
    )

    def attend_back(items):
        query_blk, key_blk, value_blk, log_blk, out_grad = items
        scores = (
            jnp.einsum("qhe,khe->hqk", query_blk, key_blk, preferred_element_type=jnp.float32)
            * scale_factor
        )
        probs = jnp.exp(scores - log_blk)
        value_grad = jnp.einsum(
            "hqk,qhe->khe", probs.astype(jnp.bfloat16), out_grad, preferred_element_type=jnp.float32
        )
        probs_grad = jnp.einsum(
            "qhe,khe->hqk", out_grad, value_blk, preferred_element_type=jnp.float32
        )
        inner = jnp.sum(probs * probs_grad, axis=-1, keepdims=True)
        scores_grad = (probs * (probs_grad - inner) * scale_factor).astype(jnp.bfloat16)
        query_grad = jnp.einsum(
            "hqk,khe->qhe", scores_grad, key_blk, preferred_element_type=jnp.float32
        )
        key_grad = jnp.einsum(
            "hqk,qhe->khe", scores_grad, query_blk, preferred_element_type=jnp.float32
        )
        return (query_grad, key_grad, value_grad)

    attended_grad4 = attended_grad.reshape(lat_count, SEQ, head_count, HEAD_DIM)
    query_grad, key_grad, value_grad = lax.map(
        attend_back, (query, key_vec, value_vec, log_total, attended_grad4)
    )
    query_grad = query_grad.reshape(tok_rows, head_count * HEAD_DIM)
    key_grad = key_grad.reshape(tok_rows, head_count * HEAD_DIM)
    value_grad = value_grad.reshape(tok_rows, head_count * HEAD_DIM)
    qv_bias_part = jnp.stack([jnp.sum(query_grad, axis=0), jnp.sum(value_grad, axis=0)], axis=0)
    qkv_low = jnp.stack([query_grad, key_grad, value_grad], axis=1).astype(jnp.bfloat16)
    qkv_wgrad = jnp.einsum("td,tkc->dkc", normed_one, qkv_low, preferred_element_type=jnp.float32)
    normed_one_grad = back_summed(
        jnp.einsum("tkc,dkc->td", qkv_low, qkv_full, preferred_element_type=jnp.float32)
    )
    input_part, shift_one_grad, scale_one_grad = norm_back(
        normed_one_grad, normal_one, inverse_one, scale_one
    )
    latents_grad = middle_grad + input_part
    mod_grad = jnp.stack(
        [
            shift_one_grad,
            scale_one_grad,
            gate_one_grad,
            shift_two_grad,
            scale_two_grad,
            gate_two_grad,
        ],
        axis=1,
    )
    mod_block_grad, out_bias_cols = (
        lax.psum_scatter(
            mod_grad.astype(jnp.bfloat16), "col", scatter_dimension=2, tiled=True
        ).astype(jnp.float32),
        lax.psum_scatter(
            jnp.stack([proj_bias_part, fc2_bias_part], axis=0).astype(jnp.bfloat16),
            "col",
            scatter_dimension=1,
            tiled=True,
        ).astype(jnp.float32),
    )
    ada_bias_part = jnp.sum(mod_block_grad, axis=0)
    mod_low = mod_block_grad.astype(jnp.bfloat16)
    ada_wgrad = jnp.einsum("bd,bkc->dkc", cond_act, mod_low, preferred_element_type=jnp.float32)
    cond_part = jnp.einsum("bkc,dkc->bd", mod_low, ada_full, preferred_element_type=jnp.float32)
    cond_summed = lax.psum(cond_part, "col")
    silu_value, silu_pull = jax.vjp(jax.nn.silu, cond_float)
    condition_grad = silu_pull(cond_summed)[0]
    ada_wsum, qkv_wsum, proj_wsum, fc1_wsum, fc2_wsum = (
        lax.psum_scatter(
            ada_wgrad.astype(jnp.bfloat16), "row", scatter_dimension=0, tiled=True
        ).astype(jnp.float32),
        lax.psum_scatter(
            qkv_wgrad.astype(jnp.bfloat16), "row", scatter_dimension=0, tiled=True
        ).astype(jnp.float32),
        lax.psum_scatter(
            proj_wgrad.astype(jnp.bfloat16), "row", scatter_dimension=1, tiled=True
        ).astype(jnp.float32),
        lax.psum_scatter(
            fc1_wgrad.astype(jnp.bfloat16), "row", scatter_dimension=0, tiled=True
        ).astype(jnp.float32),
        lax.psum_scatter(
            fc2_wgrad.astype(jnp.bfloat16), "row", scatter_dimension=1, tiled=True
        ).astype(jnp.float32),
    )
    ada_bsum, qv_bsum, proj_bsum, fc1_bsum, fc2_bsum = lax.psum(
        (ada_bias_part, qv_bias_part, out_bias_cols[0], fc1_bias_part, out_bias_cols[1]), "row"
    )
    return (
        output,
        latents_grad,
        condition_grad,
        ada_wsum,
        ada_bsum,
        qkv_wsum,
        qv_bsum,
        proj_wsum,
        proj_bsum,
        fc1_wsum,
        fc1_bsum,
        fc2_wsum,
        fc2_bsum,
    )


def solution(mesh):
    return jax.shard_map(
        shards,
        mesh=mesh,
        in_specs=(
            P(("row", "col"), None),
            P("row", None),
            P("row", None, "col"),
            P(None, "col"),
            P("row", None, "col"),
            P(None, "col"),
            P("col", "row"),
            P("col"),
            P("row", "col"),
            P("col"),
            P("col", "row"),
            P("col"),
            P(("row", "col"), None),
        ),
        out_specs=(
            P(("row", "col"), None),
            P(("row", "col"), None),
            P("row", None),
            P("row", None, "col"),
            P(None, "col"),
            P("row", None, "col"),
            P(None, "col"),
            P("col", "row"),
            P("col"),
            P("row", "col"),
            P("col"),
            P("col", "row"),
            P("col"),
        ),
        check_vma=False,
    )
```

profile of v0, /device:TPU:0, one launch (start us, length us, event | category | flops | bytes accessed | tf_op | source)
XLA Modules:
  0.0 2002.2 jit_solution(13960969873964941125)
XLA Ops:
  10.9 39.5 %all-gather.9.cloned.1.call-done = bf16[1152,6,144]{2,1,0:T(8,128)(2,1)} async-done(((bf16[288,6,144]{2,1,0:T(8,128)(2,1)}), bf16[1152,6,144]{2,1,0:T(8,128)(2,1)}) %all-gather.9.cloned.1.call-update) | async-done | bytes 1990672 | tf_op jit(solution)/shard_map/all_gather | solution.py:50
  50.4 5.5 copy.78
  56.8 50.3 %all_gather.37 = f32[4,6,1152]{1,0,2:T(4,128)} all-gather(f32[4,6,144]{1,0,2:T(4,128)S(1)} %copy.79), channel_id=1, replica_groups=mesh['row'=4,'col'=8] {'col'}, dimensions={2}, use_global_device_ids=true | all-gather | bytes 124416 | tf_op jit(solution)/shard_map/all_gather | solution.py:62
  109.3 5.7 fusion.156
  115.0 5.0 copy-done.1
  122.0 6.3 all-gather
  130.6 17.8 all_gather.39
  151.6 105.9 %all-gather.11.cloned.1.call-done = bf16[4096,1152]{1,0:T(8,128)(2,1)} async-done(((bf16[512,1152]{1,0:T(8,128)(2,1)}), bf16[4096,1152]{1,0:T(8,128)(2,1)}) %all-gather.11.cloned.1.call-update) | async-done | bytes 9437200 | tf_op jit(solution)/shard_map/all_gather | solution.py:85
  257.5 7.6 fusion.181
  273.9 4.0 squeeze.53
  283.4 27.6 %while.26 = (s32[]{:T(128)}, bf16[4,1024,2,72]{1,3,2,0:T(8,128)(2,1)}, f32[4,2,1024,1]{2,1,3,0:T(2,128)}, bf16[4,1024,2,72]{1,3,2,0:T(8,128)(2,1)}, bf16[4,1024,...) while((s32[]{:T(128)}, bf16[4,1024,2,72]{1,3,2,0:T(8,128)(2,1)}, ...), condition=%wide.region_5.6_spmd, body=%wide.region_2.5_spmd.sunk | while | flops 622999552 | bytes 26413144 | solution.py:134
  286.6 3.5 fusion.232
  293.3 3.5 fusion.232
  300.1 3.5 fusion.232
  306.9 3.5 fusion.232
  314.5 5.3 convolution_convert_fusion.2
  322.0 36.3 %all-reduce.2 = (f32[1152]{0:T(1024)S(1)}, f32[1152]{0:T(1024)S(1)}) all-reduce(f32[1152]{0:T(1024)S(1)} %convert_dynamic-update-slice_fusion.1, f32[1152]{0:T(1024)S(1)} %convert_dynamic-update-slice_fusion), channel_id=1, replica_groups=mesh['row'=4,'col'=8] {'col'}, use_global_device_ids=true, to_apply=%add | all-reduce | flops 2304 | bytes 18432
  358.4 124.0 %reduce-scatter.22.cloned.1.call-done = bf16[512,1152]{1,0:T(8,128)(2,1)} async-done(((bf16[4096,1152]{1,0:T(8,128)(2,1)}), bf16[512,1152]{1,0:T(8,128)(2,1)}) %reduce-scatter.22.cloned.1.call-update) | async-done | bytes 1179664 | tf_op jit(solution)/shard_map/reduce_scatter | solution.py:136
  486.2 5.1 fusion.137
  494.0 8.0 all-gather.15.cloned.1.call-done
  502.0 140.7 %all-gather.13.cloned.1.call-done = bf16[4096,1152]{1,0:T(8,128)(2,1)} async-done(((bf16[512,1152]{1,0:T(8,128)(2,1)}), bf16[4096,1152]{1,0:T(8,128)(2,1)}) %all-gather.13.cloned.1.call-update) | async-done | bytes 9437200 | tf_op jit(solution)/shard_map/all_gather | solution.py:85
  642.7 11.7 fusion.182
  654.3 7.1 all-gather.17.cloned.1.call-done
  661.4 140.8 %all-gather.19.cloned.1.call-done = bf16[4096,1152]{1,0:T(8,128)(2,1)} async-done(((bf16[512,1152]{1,0:T(8,128)(2,1)}), bf16[4096,1152]{1,0:T(8,128)(2,1)}) %all-gather.19.cloned.1.call-update) | async-done | bytes 9437200 | tf_op jit(solution)/shard_map/all_gather | solution.py:89
  802.3 17.9 fusion.172
  822.4 10.8 convolution_convert_fusion
  833.3 14.9 convolution_convert_fusion.1
  848.2 146.8 %reduce-scatter.26.cloned.1.call-done = bf16[512,1152]{1,0:T(8,128)(2,1)} async-done(((bf16[4096,1152]{1,0:T(8,128)(2,1)}), bf16[512,1152]{1,0:T(8,128)(2,1)}) %reduce-scatter.26.cloned.1.call-update) | async-done | bytes 1179664 | tf_op jit(solution)/shard_map/reduce_scatter | solution.py:92
  999.0 162.1 %reduce-scatter.24.cloned.1.call-done = bf16[512,1152]{1,0:T(8,128)(2,1)} async-done(((bf16[4096,1152]{1,0:T(8,128)(2,1)}), bf16[512,1152]{1,0:T(8,128)(2,1)}) %reduce-scatter.24.cloned.1.call-update) | async-done | bytes 1179664 | tf_op jit(solution)/shard_map/reduce_scatter | solution.py:149
  1161.1 6.0 fusion.145
  1167.2 137.2 %all-gather.21.cloned.1.call-done = bf16[4096,1152]{1,0:T(8,128)(2,1)} async-done(((bf16[512,1152]{1,0:T(8,128)(2,1)}), bf16[4096,1152]{1,0:T(8,128)(2,1)}) %all-gather.21.cloned.1.call-update) | async-done | bytes 9437200 | tf_op jit(solution)/shard_map/all_gather | solution.py:89
  1304.4 7.9 convolution_convert_fusion.3
  1312.3 4.1 reshape.153
  1319.2 177.2 %while.27 = (s32[]{:T(128)}, f32[4,1024,2,72]{1,3,2,0:T(8,128)}, bf16[4,1024,2,72]{1,3,2,0:T(8,128)(2,1)}, f32[4,1024,2,72]{1,3,2,0:T(8,128)}, bf16[4,1024,2,72]...) while((s32[]{:T(128)}, f32[4,1024,2,72]{1,3,2,0:T(8,128)}, ...), condition=%wide.region_15.16_spmd, body=%wide.region_13.15_spmd.sunk | while | flops 1553995776 | bytes 134444208 | solution.py:219
  1325.7 5.6 fusion.243
  1331.3 16.3 fusion.246
  1347.6 15.9 fusion.245
  1370.0 5.6 fusion.243
  1375.6 16.3 fusion.246
  1391.9 15.9 fusion.245
  1414.3 5.6 fusion.243
  1419.9 16.2 fusion.246
  1436.1 15.9 fusion.245
  1458.5 5.6 fusion.243
  1464.1 16.2 fusion.246
  1480.3 15.9 fusion.245
  1496.3 5.9 fusion.176
  1514.2 3.6 stack_reshape.13
  1521.4 8.1 bitcast_convert_fusion
  1529.7 161.4 %reduce-scatter.28.cloned.1.call-done = bf16[512,1152]{1,0:T(8,128)(2,1)} async-done(((bf16[4096,1152]{1,0:T(8,128)(2,1)}), bf16[512,1152]{1,0:T(8,128)(2,1)}) %reduce-scatter.28.cloned.1.call-update) | async-done | bytes 1179664 | tf_op jit(solution)/shard_map/reduce_scatter | solution.py:92
  1708.9 15.6 convolution_convert_fusion.6
  1725.0 12.2 convolution_convert_fusion.5
  1737.4 5.4 convolution_convert_fusion.7
  1743.9 9.5 fusion.183
  1757.1 5.0 fusion.144
  1772.2 4.1 copy.109
  1776.4 19.3 reduce-scatter.32.cloned.1.call-done
  1797.6 28.3 %reduce-scatter.30.cloned.1.call-done = bf16[288,576]{1,0:T(8,128)(2,1)} async-done(((bf16[1152,576]{1,0:T(8,128)(2,1)}), bf16[288,576]{1,0:T(8,128)(2,1)}) %reduce-scatter.30.cloned.1.call-update) | async-done | bytes 331792 | tf_op jit(solution)/shard_map/reduce_scatter | solution.py:274
  1831.7 19.2 reduce-scatter.40.cloned.1.call-done
  1854.2 25.5 %reduce-scatter.38.cloned.1.call-done = bf16[288,432]{1,0:T(8,128)(2,1)} async-done(((bf16[1152,432]{1,0:T(8,128)(2,1)}), bf16[288,432]{1,0:T(8,128)(2,1)}) %reduce-scatter.38.cloned.1.call-update) | async-done | bytes 248848
  1884.8 4.3 fusion.98
  1889.1 52.9 %reduce-scatter.42.cloned.1.call-done = bf16[144,2]{1,0:T(8,128)(2,1)} async-done(((bf16[1152,2]{1,0:T(8,128)(2,1)}), bf16[144,2]{1,0:T(8,128)(2,1)}) %reduce-scatter.42.cloned.1.call-update) | async-done | bytes 592
  1942.8 11.3 all-reduce.3
  1956.1 35.2 %psum.42 = f32[4,1152]{1,0:T(4,128)S(1)} all-reduce(f32[4,1152]{1,0:T(4,128)S(1)} %convolution_bitcast_fusion), channel_id=1, replica_groups=mesh['row'=4,'col'=8] {'col'}, use_global_device_ids=true, to_apply=%region_20.21 | all-reduce | flops 4608 | bytes 36864 | tf_op jit(solution)/shard_map/psum | solution.py:261
  (252 shorter events, 159.6 us)
Async XLA Ops:
  7.2 2.9 copy-start.36
  7.2 2.9 copy-start.2
  7.2 43.2 %all-gather.9.cloned.1.call-start = ((), (), s32[]{:S(2)}) async-start(), calls=%async_computation.11 | async-start | bytes 5898240 | tf_op jit(solution)/shard_map/all_gather | solution.py:50
  10.0 247.4 %all-gather.11.cloned.1.call-start = ((), (), s32[]{:S(2)}) async-start(), calls=%async_computation.12 | async-start | bytes 10616832 | tf_op jit(solution)/shard_map/all_gather | solution.py:85
  10.1 99.1 %copy-start.25 = (s32[512]{0:T(512)}, s32[512]{0:T(512)S(1)}, u32[]{:S(2)}) copy-start(s32[512]{0:T(512)S(1)} %add_select_fusion) | copy-start | bytes 6148
  10.4 104.6 %copy-start.28 = (f32[512]{0:T(512)}, f32[512]{0:T(512)S(1)}, u32[]{:S(2)}) copy-start(f32[512]{0:T(512)S(1)} %broadcast_multiply_fusion.5) | copy-start | bytes 6148
  10.8 104.2 %copy-start.34 = (f32[512]{0:T(512)}, f32[512]{0:T(512)S(1)}, u32[]{:S(2)}) copy-start(f32[512]{0:T(512)S(1)} %add_rsqrt_fusion.1) | copy-start | bytes 6148
  10.9 45.1 %copy-start.27 = (bf16[4,1152]{1,0:T(4,128)(2,1)S(1)}, bf16[4,1152]{1,0:T(4,128)(2,1)}, u32[]{:S(2)}) copy-start(bf16[4,1152]{1,0:T(4,128)(2,1)} %param.18) | copy-start | bytes 27652
  55.9 51.2 %copy-start.11 = (bf16[1152,6,144]{0,2,1:T(8,128)(2,1)}, bf16[1152,6,144]{0,2,1:T(8,128)(2,1)S(1)}, u32[]{:S(2)}) copy-start(bf16[1152,6,144]{0,2,1:T(8,128)(2,1)S(1)} %copy.78) | copy-start | bytes 5971972
  115.0 5.0 copy-start.1
  120.1 1.9 copy-start.24
  121.6 7.8 copy-start.23
  121.7 360.6 %reduce-scatter.22.cloned.1.call-start = ((), (), s32[]{:S(2)}) async-start(), calls=%async_computation.13 | async-start | bytes 10616832 | tf_op jit(solution)/shard_map/reduce_scatter | solution.py:136
  277.9 3.1 copy-start.16
  310.9 3.1 copy-start.12
  310.9 3.5 copy-start.15
  310.9 3.5 copy-start.20
  314.5 5.4 copy-start.6
  319.8 1.9 copy-start.39
  319.8 2.1 copy-start.40
  319.9 182.1 %all-gather.15.cloned.1.call-start = ((), (), s32[]{:S(2)}) async-start(), calls=%async_computation.15 | async-start | bytes 1843200 | tf_op jit(solution)/shard_map/all_gather | solution.py:53
  320.4 322.2 %all-gather.13.cloned.1.call-start = ((), (), s32[]{:S(2)}) async-start(), calls=%async_computation.14 | async-start | bytes 10616832 | tf_op jit(solution)/shard_map/all_gather | solution.py:85
  358.3 126.5 %copy-start.33 = (f32[1152]{0:T(1024)}, f32[1152]{0:T(1024)S(1)}, u32[]{:S(2)}) copy-start(f32[1152]{0:T(1024)S(1)} %get-tuple-element.200) | copy-start | bytes 13828
  358.3 802.8 %copy-start.31 = (f32[1152]{0:T(1024)}, f32[1152]{0:T(1024)S(1)}, u32[]{:S(2)}) copy-start(f32[1152]{0:T(1024)S(1)} %get-tuple-element.201) | copy-start | bytes 13828
  491.3 170.1 %all-gather.17.cloned.1.call-start = ((), (), s32[]{:S(2)}) async-start(), calls=%async_computation.16 | async-start | bytes 1843200 | tf_op jit(solution)/shard_map/all_gather | solution.py:54
  491.9 310.4 %all-gather.19.cloned.1.call-start = ((), (), s32[]{:S(2)}) async-start(), calls=%async_computation.18 | async-start | bytes 10616832 | tf_op jit(solution)/shard_map/all_gather | solution.py:89
  492.6 502.4 %reduce-scatter.26.cloned.1.call-start = ((), (), s32[]{:S(2)}) async-start(), calls=%async_computation.19 | async-start | bytes 10616832 | tf_op jit(solution)/shard_map/reduce_scatter | solution.py:92
  802.3 20.2 %copy-start.41 = (bf16[1152,576]{1,0:T(8,128)(2,1)S(1)}, bf16[1152,576]{1,0:T(8,128)(2,1)}, u32[]{:S(2)}) copy-start(bf16[1152,576]{1,0:T(8,128)(2,1)} %all-gather.15.cloned.1.call-done) | copy-start | bytes 3981316
  820.2 2.3 copy-start.43
  833.2 327.9 %reduce-scatter.24.cloned.1.call-start = ((), (), s32[]{:S(2)}) async-start(), calls=%async_computation.17 | async-start | bytes 10616832 | tf_op jit(solution)/shard_map/reduce_scatter | solution.py:149
  848.2 456.2 %all-gather.21.cloned.1.call-start = ((), (), s32[]{:S(2)}) async-start(), calls=%async_computation.20 | async-start | bytes 10616832 | tf_op jit(solution)/shard_map/all_gather | solution.py:89
  1167.1 524.0 %reduce-scatter.28.cloned.1.call-start = ((), (), s32[]{:S(2)}) async-start(), calls=%async_computation.21 | async-start | bytes 10616832 | tf_op jit(solution)/shard_map/reduce_scatter | solution.py:92
  1312.3 6.8 copy-start.13
  1319.9 2.4 copy-start.14
  1322.2 3.5 copy-start
  1364.2 2.4 copy-start.14
  1366.5 3.5 copy-start
  1408.5 2.4 copy-start.14
  1410.9 3.4 copy-start
  1452.7 2.4 copy-start.14
  1455.1 3.4 copy-start
  1519.4 2.0 copy-start.21
  1519.6 1.8 copy-start.22
  1529.4 161.7 %copy-start.26 = (s32[512]{0:T(512)S(1)}, s32[512]{0:T(512)}, u32[]{:S(2)}) copy-start(s32[512]{0:T(512)} %copy-done.25) | copy-start | bytes 6148
  1529.4 164.0 %copy-start.3 = (bf16[512,1152]{1,0:T(8,128)(2,1)S(1)}, bf16[512,1152]{1,0:T(8,128)(2,1)}, u32[]{:S(2)}) copy-start(bf16[512,1152]{1,0:T(8,128)(2,1)} %param.17) | copy-start | bytes 3538948
  1529.4 164.0 %copy-start.29 = (f32[512]{0:T(512)S(1)}, f32[512]{0:T(512)}, u32[]{:S(2)}) copy-start(f32[512]{0:T(512)} %copy-done.28) | copy-start | bytes 6148
  1529.5 237.1 %reduce-scatter.34.cloned.1.call-start = ((), (), s32[]{:S(2)}) async-start(), calls=%async_computation.24 | async-start | bytes 331776
  1691.2 5.5 copy-start.4
  1691.2 5.5 copy-start.18
  1696.6 2.5 copy-start.10
  1699.1 2.7 copy-start.9
  1699.1 2.7 copy-start.17
  1699.1 2.7 copy-start.32
  1703.6 5.2 copy-start.37
  1708.5 87.2 %reduce-scatter.32.cloned.1.call-start = ((), (), s32[]{:S(2)}) async-start(), calls=%async_computation.23 | async-start | bytes 1843200 | tf_op jit(solution)/shard_map/reduce_scatter | solution.py:277
  1724.5 12.8 copy-start.7
  1724.5 101.4 %reduce-scatter.30.cloned.1.call-start = ((), (), s32[]{:S(2)}) async-start(), calls=%async_computation.22 | async-start | bytes 1843200 | tf_op jit(solution)/shard_map/reduce_scatter | solution.py:274
  1737.3 113.7 %reduce-scatter.40.cloned.1.call-start = ((), (), s32[]{:S(2)}) async-start(), calls=%async_computation.27 | async-start | bytes 737280
  1743.8 135.9 %reduce-scatter.38.cloned.1.call-start = ((), (), s32[]{:S(2)}) async-start(), calls=%async_computation.26 | async-start | bytes 1474560
  1754.4 2.6 copy-start.5
  1754.4 2.6 copy-start.35
  1757.0 184.9 %reduce-scatter.42.cloned.1.call-start = ((), (), s32[]{:S(2)}) async-start(), calls=%async_computation.28 | async-start | bytes 331776
  1763.0 229.6 %reduce-scatter.36.cloned.1.call-start = ((), (), s32[]{:S(2)}) async-start(), calls=%async_computation.25 | async-start | bytes 2580480
  1776.4 108.4 %copy-start.30 = (f32[512]{0:T(512)S(1)}, f32[512]{0:T(512)}, u32[]{:S(2)}) copy-start(f32[512]{0:T(512)} %copy-done.28) | copy-start | bytes 6148
  (4 other events, 5.2 us)
Sparse Core Ops, SparseCore 0:
  10.2 40.1 all-gather.8
  121.8 135.6 all-gather.10
  320.0 162.2 reduce-scatter.21
  483.7 18.1 all-gather.14
  504.6 138.0 all-gather.12
  644.1 17.2 all-gather.16
  664.2 138.0 all-gather.18
  833.4 161.6 reduce-scatter.25
  998.7 162.4 reduce-scatter.23
  1167.3 137.1 all-gather.20
  1529.6 161.5 reduce-scatter.27
  1708.7 57.8 reduce-scatter.33
  1769.2 26.4 reduce-scatter.31
  1798.3 27.5 reduce-scatter.29
  1828.8 22.0 reduce-scatter.39
  1854.0 25.7 reduce-scatter.37
  1883.2 58.7 reduce-scatter.41
  1944.6 30.2 reduce-scatter.35
where the time goes:
time: 2010 us; the launch traced here: 2000 us
  waiting for transfers between devices  1320 us (66%)
  matrix products  341 us (17%)
  blocking collectives  157 us (8%)
  local copies, waits for them, and re-layouts  97.3 us (5%)
  other arithmetic  63.8 us (3%)
    reduce_scatter x2, waiting for transfers between devices, back_summed(): lax.psum_scatter(term.astype(jnp.bfloat16), 'col', scatter_dimension=0, t...  308 us
    all_gather x2, waiting for transfers between devices, spread(): lax.all_gather(grad_rows.astype(jnp.bfloat16), 'col', axis=0, tiled=True)  278 us
    all_gather x2, waiting for transfers between devices, normed(): gathered = lax.all_gather(rows, 'col', axis=0, tiled=True)  247 us
    reduce_scatter x1, waiting for transfers between devices, shards(): lax.psum_scatter(jnp.dot(hidden, fc2_full, preferred_element_type=jnp.flo...  162 us
    reduce_scatter x1, waiting for transfers between devices, shards(): lax.psum_scatter(jnp.dot(attended_flat, proj_full, preferred_element_type...  124 us
    unnamed x23, waiting for transfers between devices  103 us
    dot_general x4, matrix products, attend_back(): jnp.einsum('hqk,qhe->khe', scores_grad, query_blk, preferred_element_type...  65 us
    dot_general x4, matrix products, attend_back(): jnp.einsum('hqk,khe->qhe', scores_grad, key_blk, preferred_element_type=j...  63.6 us
  transfers between devices with their start and end apart: 18, of which 17 were waited for; matrix products, arithmetic and copies ran while one was open for 7% of the time, Pallas kernels for 0%

commit v1 on v0

v1 whole, which is shorter than its diff:
```python
import functools
import math
import jax
import jax.numpy as jnp
from jax import lax
from jax.experimental import pallas as pl
from jax.experimental.pallas import tpu as pltpu
from jax.sharding import PartitionSpec as P

HEAD_DIM = 72
SEQ = 1024
norm_eps = 1e-06
bf16, f32 = jnp.bfloat16, jnp.float32

MESH = pl.DeviceIdType.MESH
ANY = pl.BlockSpec(memory_space=pl.ANY)


class Place:
    def __init__(self):
        row, col = lax.axis_index("row"), lax.axis_index("col")
        self.row, self.col = row, col
        self.depth = lax.axis_size("col") // 2
        self.y, self.h = row // 2, row % 2
        self.z, self.x = col // 2, col % 2
        self.p = jnp.where(self.h == 0, self.y, self.x)
        self.q = jnp.where(self.h == 0, self.x, self.y)
        flip_x, flip_y = (row, col + 1 - 2 * self.x), (row + 2 - 4 * self.y, col)
        self.to_q = tuple(jnp.where(self.h == 0, a, b) for a, b in zip(flip_x, flip_y))
        self.to_p = tuple(jnp.where(self.h == 0, b, a) for a, b in zip(flip_x, flip_y))
        self.to_core = (row + 1 - 2 * self.h, col)

    def to_z(self, z):
        return (self.row, 2 * z + self.x)

    def yx(self, p, q):
        return jnp.where(self.h == 0, p, q), jnp.where(self.h == 0, q, p)

    def partners(self):
        near = [self.to_q, self.to_p, self.to_core]
        return near + [self.to_z((self.z + k) % self.depth) for k in range(1, self.depth)]


def greet(partners):
    barrier = pltpu.get_barrier_semaphore()
    for partner in partners:
        pl.semaphore_signal(barrier, inc=1, device_id=partner, device_id_type=MESH)
    pl.semaphore_wait(barrier, len(partners))


def block_at(ref, rows, lanes, r, c):
    return ref.at[pl.ds(pl.multiple_of(r * rows, 16), rows), pl.ds(pl.multiple_of(c * lanes, 128), lanes)]


class Gather:
    sems = (1, 2, 2, 4, 8)

    def __init__(self, place, ins, outs, sems):
        self.at, self.ins, self.outs = place, ins, outs
        self.local, self.zs, self.qs, self.ps, self.ks = sems

    @staticmethod
    def scratch(count, depth):
        dma = pltpu.SemaphoreType.DMA
        return [dma((count,)), dma((count, 2, depth)), dma((count, 2, depth)), dma((count, 2, depth, 2)), dma((count, 2, depth, 4))]

    def block(self, a, p, q, z, h=None):
        y, x = self.at.yx(p, q)
        rows, lanes = self.ins[a].shape
        h = self.at.h if h is None else h
        return block_at(self.outs[a], rows, lanes, 2 * y + h, 2 * z + x)

    def zc(self, t):
        return (self.at.z + self.at.depth - t) % self.at.depth

    def copy(self, src, dst, sems, index, to):
        return pltpu.make_async_remote_copy(
            src_ref=src, dst_ref=dst, send_sem=sems.at[(index[0], 0) + index[1:]], recv_sem=sems.at[(index[0], 1) + index[1:]],
            device_id=to, device_id_type=MESH)

    def own(self, a):
        return self.block(a, self.at.p, self.at.q, self.at.z)

    def c_local(self, a):
        return pltpu.make_async_copy(self.ins[a], self.own(a), self.local.at[a])

    def c_z(self, a, k):
        place = self.at
        return pltpu.make_async_remote_copy(
            src_ref=self.ins[a], dst_ref=self.own(a), send_sem=self.zs.at[a, 0, k], recv_sem=self.zs.at[a, 1, place.z],
            device_id=place.to_z((place.z + k) % place.depth), device_id_type=MESH)

    def r_z(self, a, t):
        place = self.at
        here = self.block(a, place.p, place.q, self.zc(t))
        return pltpu.make_async_remote_copy(
            src_ref=self.ins[a], dst_ref=here, send_sem=self.zs.at[a, 0, 0], recv_sem=self.zs.at[a, 1, self.zc(t)],
            device_id=place.to_z(place.z), device_id_type=MESH)

    def c_q(self, a, t):
        place = self.at
        spot = self.block(a, place.p, place.q, self.zc(t))
        return self.copy(self.ins[a] if t == 0 else spot, spot, self.qs, (a, self.zc(t)), place.to_q)

    def c_p(self, a, t, j):
        place = self.at
        spot = self.block(a, place.p, place.q if j == 0 else 1 - place.q, self.zc(t))
        return self.copy(self.ins[a] if t == 0 and j == 0 else spot, spot, self.ps, (a, self.zc(t), j), place.to_p)

    def c_k(self, a, t, j):
        place = self.at
        spot = self.block(a, place.p if j < 2 else 1 - place.p, place.q if j % 2 == 0 else 1 - place.q, self.zc(t))
        return self.copy(self.ins[a] if t == 0 and j == 0 else spot, spot, self.ks, (a, self.zc(t), j), place.to_core)

    def start(self, a):
        for k in range(1, self.at.depth):
            self.c_z(a, k).start()
        self.c_local(a).start()

    def stage(self, a, t, n):
        if n == 0:
            if t > 0:
                self.r_z(a, t).wait_recv()
            self.c_q(a, t).start()
            self.c_p(a, t, 0).start()
            self.c_k(a, t, 0).start()
        elif n == 1:
            self.c_q(a, t).wait_recv()
            self.c_p(a, t, 1).start()
            self.c_k(a, t, 1).start()
        elif n == 2:
            self.c_p(a, t, 0).wait_recv()
            self.c_k(a, t, 2).start()
        elif n == 3:
            self.c_p(a, t, 1).wait_recv()
            self.c_k(a, t, 3).start()
        else:
            for j in range(4):
                self.c_k(a, t, j).wait_recv()

    def finish(self, a):
        for k in range(1, self.at.depth):
            self.c_z(a, k).wait_send()
        self.c_local(a).wait()
        for t in range(self.at.depth):
            self.c_q(a, t).wait_send()
            for j in range(2):
                self.c_p(a, t, j).wait_send()
            for j in range(4):
                self.c_k(a, t, j).wait_send()


def gather_kernel(groups, *refs):
    count = sum(groups)
    ins, outs, sems = refs[:count], refs[count:2 * count], refs[2 * count:]
    place = Place()
    greet(place.partners())
    work = Gather(place, ins, outs, sems)
    for a in range(count):
        work.start(a)
    chunks, first = [], 0
    for size in groups:
        for t in range(place.depth):
            chunks.append([(a, t) for a in range(first, first + size)])
        first += size
    for s in range(len(chunks) + 4):
        for n in range(5):
            if 0 <= s - n < len(chunks):
                for a, t in chunks[s - n]:
                    work.stage(a, t, n)
    for a in range(count):
        work.finish(a)


def gather_all(blocks, groups, collective_id):
    rows, cols = lax.axis_size("row"), lax.axis_size("col")
    return pl.pallas_call(
        functools.partial(gather_kernel, groups),
        out_shape=[jax.ShapeDtypeStruct((rows * b.shape[0], cols * b.shape[1]), b.dtype) for b in blocks],
        in_specs=[ANY] * len(blocks),
        out_specs=[ANY] * len(blocks),
        scratch_shapes=Gather.scratch(len(blocks), cols // 2),
        compiler_params=pltpu.CompilerParams(collective_id=collective_id, has_side_effects=True),
        name="gather_weights",
    )(*blocks)


class Scatter:
    def __init__(self, place, ins, outs, bufs, sems):
        self.at, self.ins, self.outs = place, ins, outs
        self.r0, self.own, self.r1, self.r2, self.r3 = bufs
        self.s0, self.ld, self.s1, self.s2, self.s3 = sems

    @staticmethod
    def scratch(shapes, depth):
        dma, count = pltpu.SemaphoreType.DMA, len(shapes)
        bufs = []
        for lead in ((depth, 2, 2), (2, 2, 2), (depth, 2), (depth,), (depth - 1,)):
            bufs += [pltpu.VMEM(lead + s, jnp.bfloat16) for s in shapes]
        return bufs + [dma((count, 2, depth, 4)), dma((count, 2, 4)), dma((count, 2, depth, 2)), dma((count, 2, depth)), dma((count, 2, depth))]

    @staticmethod
    def split(refs, count):
        return [refs[i * count:(i + 1) * count] for i in range(5)], refs[5 * count:]

    def zc(self, t):
        return lax.rem(self.at.z + 1 + t, self.at.depth)

    def block(self, a, p, q, z, h):
        y, x = jnp.where(h == 0, p, q), jnp.where(h == 0, q, p)
        rows, lanes = self.outs[a].shape
        return block_at(self.ins[a], rows, lanes, 2 * y + h, 2 * z + x)

    def c0(self, a, t, j):
        place = self.at
        return pltpu.make_async_remote_copy(
            src_ref=self.block(a, j // 2, j % 2, self.zc(t), 1 - place.h), dst_ref=self.r0[a].at[t, j // 2, j % 2],
            send_sem=self.s0.at[a, 0, t, j], recv_sem=self.s0.at[a, 1, t, j], device_id=place.to_core, device_id_type=MESH)

    def load(self, a, t, j):
        return pltpu.make_async_copy(
            self.block(a, j // 2, j % 2, self.zc(t), self.at.h), self.own[a].at[t % 2, j // 2, j % 2], self.ld.at[a, t % 2, j])

    def c1(self, a, t, j):
        place = self.at
        return pltpu.make_async_remote_copy(
            src_ref=self.r0[a].at[t, 1 - place.p, j], dst_ref=self.r1[a].at[t, j],
            send_sem=self.s1.at[a, 0, t, j], recv_sem=self.s1.at[a, 1, t, j], device_id=place.to_p, device_id_type=MESH)

    def c2(self, a, t):
        place = self.at
        return pltpu.make_async_remote_copy(
            src_ref=self.r0[a].at[t, place.p, 1 - place.q], dst_ref=self.r2[a].at[t],
            send_sem=self.s2.at[a, 0, t], recv_sem=self.s2.at[a, 1, t], device_id=place.to_q, device_id_type=MESH)

    def c3(self, a, t):
        place = self.at
        return pltpu.make_async_remote_copy(
            src_ref=self.r0[a].at[t, place.p, place.q], dst_ref=self.r3[a].at[t],
            send_sem=self.s3.at[a, 0, t], recv_sem=self.s3.at[a, 1, t], device_id=place.to_z(self.zc(t)), device_id_type=MESH)

    def add(self, a, into, other):
        rows = self.outs[a].shape[0]
        step = 48 if rows % 48 == 0 else 16

        @pl.loop(0, rows // step)
        def _(i):
            part = pl.ds(pl.multiple_of(i * step, 16), step)
            into[part, :] = into[part, :] + other[part, :]

    def stage(self, a, t, n):
        place = self.at
        last = t == place.depth - 1
        if n == 0:
            for j in range(4):
                self.c0(a, t, j).start()
                self.load(a, t, j).start()
        elif n == 1:
            for j in range(4):
                self.c0(a, t, j).wait_recv()
                self.load(a, t, j).wait()
            for j in range(2):
                self.add(a, self.r0[a].at[t, 1 - place.p, j], self.own[a].at[t % 2, 1 - place.p, j])
                self.c1(a, t, j).start()
            for j in range(2):
                self.add(a, self.r0[a].at[t, place.p, j], self.own[a].at[t % 2, place.p, j])
        elif n == 2:
            for j in range(2):
                self.c1(a, t, j).wait_recv()
            self.add(a, self.r0[a].at[t, place.p, 1 - place.q], self.r1[a].at[t, 1 - place.q])
            self.c2(a, t).start()
            self.add(a, self.r0[a].at[t, place.p, place.q], self.r1[a].at[t, place.q])
        elif n == 3:
            self.c2(a, t).wait_recv()
            self.add(a, self.r0[a].at[t, place.p, place.q], self.r2[a].at[t])
            if not last:
                self.c3(a, t).start()
        elif last:
            self.total(a)

    def total(self, a):
        place, depth = self.at, self.at.depth
        for t in range(depth - 1):
            self.c3(a, t).wait_recv()
        rows = self.outs[a].shape[0]
        step = 48 if rows % 48 == 0 else 16
        mine, others, out = self.r0[a].at[depth - 1, place.p, place.q], self.r3[a], self.outs[a]

        @pl.loop(0, rows // step)
        def _(i):
            part = pl.ds(pl.multiple_of(i * step, 16), step)
            value = mine[part, :].astype(jnp.float32)
            for t in range(depth - 1):
                value = value + others[t, part, :].astype(jnp.float32)
            out[part, :] = value

    def finish(self, a):
        for t in range(self.at.depth):
            for j in range(4):
                self.c0(a, t, j).wait_send()
            for j in range(2):
                self.c1(a, t, j).wait_send()
            self.c2(a, t).wait_send()
            if t < self.at.depth - 1:
                self.c3(a, t).wait_send()


def chunk_list(groups, depth):
    chunks, first = [], 0
    for size in groups:
        for t in range(depth):
            chunks.append([(a, t) for a in range(first, first + size)])
        first += size
    return chunks


def scatter_kernel(groups, *refs):
    count = sum(groups)
    ins, outs = refs[:count], refs[count:2 * count]
    bufs, sems = Scatter.split(refs[2 * count:], count)
    place = Place()
    greet(place.partners())
    work = Scatter(place, ins, outs, bufs, sems)
    chunks = chunk_list(groups, place.depth)
    for s in range(len(chunks) + 4):
        for n in range(5):
            if 0 <= s - n < len(chunks):
                for a, t in chunks[s - n]:
                    work.stage(a, t, n)
    for a in range(count):
        work.finish(a)


def scatter_all(fulls, groups, collective_id):
    rows, cols = lax.axis_size("row"), lax.axis_size("col")
    shapes = [(g.shape[0] // rows, g.shape[1] // cols) for g in fulls]
    return pl.pallas_call(
        functools.partial(scatter_kernel, groups),
        out_shape=[jax.ShapeDtypeStruct(s, jnp.float32) for s in shapes],
        in_specs=[ANY] * len(fulls),
        out_specs=[pl.BlockSpec(memory_space=pltpu.VMEM)] * len(fulls),
        scratch_shapes=Scatter.scratch(shapes, cols // 2),
        compiler_params=pltpu.CompilerParams(collective_id=collective_id, has_side_effects=True, vmem_limit_bytes=58 * 2**20),
        name="scatter_grads",
    )(*fulls)


def nt(a, b):
    return lax.dot_general(a, b, (((1,), (1,)), ((), ())), preferred_element_type=f32)


def nn(a, b):
    return lax.dot_general(a, b, (((1,), (0,)), ((), ())), preferred_element_type=f32)


def tn(a, b):
    return lax.dot_general(a, b, (((0,), (0,)), ((), ())), preferred_element_type=f32)


SOFT = HEAD_DIM ** (-0.5) * math.log2(math.e)


def attend_kernel(q_ref, k_ref, v_ref, att_ref, lse_ref, k2_ref, v2_ref, sems):
    place = Place()
    greet([place.to_core])
    heads, rows, width = q_ref.shape

    def swap(i, h):
        src, dst = ((k_ref, k2_ref), (v_ref, v2_ref))[i]
        return pltpu.make_async_remote_copy(
            src_ref=src.at[h], dst_ref=dst.at[h], send_sem=sems.at[0, i, h], recv_sem=sems.at[1, i, h],
            device_id=place.to_core, device_id_type=MESH)

    for h in range(heads):
        swap(0, h).start()
        swap(1, h).start()

    @pl.loop(0, heads)
    def _(h):
        swap(0, h).wait_recv()
        swap(1, h).wait_recv()
        q = q_ref[h]
        one = nt(k_ref[h], q)
        two = nt(k2_ref[h], q)
        top = jnp.maximum(jnp.max(one, axis=0, keepdims=True), jnp.max(two, axis=0, keepdims=True)) * SOFT
        one = jnp.exp2(one * SOFT - top)
        two = jnp.exp2(two * SOFT - top)
        total = jnp.sum(one, axis=0, keepdims=True) + jnp.sum(two, axis=0, keepdims=True)
        result = tn(v_ref[h], one.astype(bf16)) + tn(v2_ref[h], two.astype(bf16))
        att_ref[h] = (result / total).T.astype(bf16)
        lse_ref[h] = top + jnp.log2(total)

    for h in range(heads):
        swap(0, h).wait_send()
        swap(1, h).wait_send()


def attend(q, k, v, collective_id):
    heads, rows, width = q.shape
    vmem = pl.BlockSpec(memory_space=pltpu.VMEM)
    return pl.pallas_call(
        attend_kernel,
        out_shape=[jax.ShapeDtypeStruct(q.shape, bf16), jax.ShapeDtypeStruct((heads, 1, rows), f32)]
        + [jax.ShapeDtypeStruct(q.shape, bf16)] * 2,
        in_specs=[vmem] * 3,
        out_specs=[vmem] * 4,
        scratch_shapes=[pltpu.SemaphoreType.DMA((2, 2, heads))],
        compiler_params=pltpu.CompilerParams(collective_id=collective_id, has_side_effects=True, vmem_limit_bytes=50 * 2**20),
        name="attend",
    )(q, k, v)


def attend_back_kernel(q_ref, k_ref, v_ref, k2_ref, v2_ref, lse_ref, o_ref, do_ref, dq_ref, dk_ref, dv_ref, send, recv, sems):
    place = Place()
    greet([place.to_core])
    heads = q_ref.shape[0]

    def swap(i, h):
        return pltpu.make_async_remote_copy(
            src_ref=send.at[i, h], dst_ref=recv.at[i, h], send_sem=sems.at[0, i, h], recv_sem=sems.at[1, i, h],
            device_id=place.to_core, device_id_type=MESH)

    @pl.loop(0, heads)
    def _(h):
        q, out_grad, lse = q_ref[h], do_ref[h], lse_ref[h]
        delta = jnp.sum(out_grad.astype(f32).T * o_ref[h].astype(f32).T, axis=0, keepdims=True)

        def half(k, v):
            probs = jnp.exp2(nt(k, q) * SOFT - lse)
            grad = (probs * (nt(v, out_grad) - delta)).astype(bf16)
            return nn(grad, q) * HEAD_DIM ** (-0.5), nn(probs.astype(bf16), out_grad), tn(k, grad)

        dk, dv, dq_two = half(k2_ref[h], v2_ref[h])
        send[0, h] = dk.astype(bf16)
        send[1, h] = dv.astype(bf16)
        swap(0, h).start()
        swap(1, h).start()
        dk, dv, dq_one = half(k_ref[h], v_ref[h])
        dk_ref[h] = dk
        dv_ref[h] = dv
        dq_ref[h] = ((dq_one + dq_two) * HEAD_DIM ** (-0.5)).T

    @pl.loop(0, heads)
    def _(h):
        swap(0, h).wait_recv()
        swap(1, h).wait_recv()
        dk_ref[h] = dk_ref[h] + recv[0, h].astype(f32)
        dv_ref[h] = dv_ref[h] + recv[1, h].astype(f32)

    for h in range(heads):
        swap(0, h).wait_send()
        swap(1, h).wait_send()


def attend_back(q, k, v, k2, v2, lse, att, att_grad, collective_id):
    heads, rows, width = q.shape
    vmem = pl.BlockSpec(memory_space=pltpu.VMEM)
    return pl.pallas_call(
        attend_back_kernel,
        out_shape=[jax.ShapeDtypeStruct(q.shape, f32)] * 3,
        in_specs=[vmem] * 8,
        out_specs=[vmem] * 3,
        scratch_shapes=[pltpu.VMEM((2,) + q.shape, bf16), pltpu.VMEM((2,) + q.shape, bf16), pltpu.SemaphoreType.DMA((2, 2, heads))],
        compiler_params=pltpu.CompilerParams(collective_id=collective_id, has_side_effects=True, vmem_limit_bytes=58 * 2**20),
        name="attend_back",
    )(q, k, v, k2, v2, lse, att, att_grad)


class Plan:
    def __init__(self, latents, condition, qkv_weight, fc1_weight):
        self.rows, self.cols = lax.axis_size("row"), lax.axis_size("col")
        self.tokens, self.width = latents.shape
        self.lats = condition.shape[0]
        self.depth_rows = qkv_weight.shape[0]
        self.head_cols = qkv_weight.shape[2]
        self.ff_cols = fc1_weight.shape[1]
        self.share = SEQ // self.tokens
        q_left, p_left, f_left = (3 * self.head_cols) % 128, self.head_cols % 128, self.ff_cols % 128
        self.near = (
            self.rows == 4 and self.share == 2 and self.cols % 2 == 0 and self.lats == self.cols // 2
            and self.depth_rows % 32 == 0 and self.tokens % 128 == 0 and q_left + p_left == 64 and f_left == 64)
        self.q_left, self.p_left, self.f_left = (q_left, p_left, f_left) if self.near else (0, 0, 0)
        self.q_main, self.p_main = 3 * self.head_cols - self.q_left, self.head_cols - self.p_left
        self.f_main = self.ff_cols - self.f_left

    def fold(self, left):
        rows, lanes = left.shape
        return left.reshape(2, rows // 2, lanes).transpose(1, 0, 2).reshape(rows // 2, 2 * lanes)

    def unfold(self, left):
        rows, lanes = left.shape
        return left.reshape(rows, 2, lanes // 2).transpose(1, 0, 2).reshape(2 * rows, lanes // 2)

    def fold_full(self, left):
        half = self.depth_rows // 2
        return left.reshape(self.rows, 2, half, self.cols, 64).transpose(0, 2, 3, 1, 4).reshape(self.rows * half, self.cols * 128)

    def unfold_full(self, left):
        half = self.depth_rows // 2
        return left.reshape(self.rows, half, self.cols, 2, 64).transpose(0, 3, 1, 2, 4).reshape(self.width, self.cols * 64)

    def swap_pairs(self):
        pairs = []
        for row in range(self.rows):
            for col in range(self.cols):
                there = (row - row % 2 + col % 2) * self.cols + col - col % 2 + row % 2
                pairs.append((row * self.cols + col, there))
        return pairs

    def swap(self, value):
        return lax.ppermute(value, ("row", "col"), self.swap_pairs()) if self.near else value


def gather_plain(blocks):
    return [lax.all_gather(lax.all_gather(b, "row", axis=0, tiled=True), "col", axis=1, tiled=True) for b in blocks]


def scatter_plain(fulls):
    parts = [lax.psum_scatter(g, "row", scatter_dimension=0, tiled=True) for g in fulls]
    return [lax.psum_scatter(g, "col", scatter_dimension=1, tiled=True).astype(f32) for g in parts]


def attend_plain(q, k, v):
    def one(item):
        scores = nt(item[0], item[1]) * HEAD_DIM ** (-0.5)
        top = jnp.max(scores, axis=-1, keepdims=True)
        probs = jnp.exp(scores - top)
        total = jnp.sum(probs, axis=-1, keepdims=True)
        return nn((probs / total).astype(bf16), item[2]).astype(bf16), top + jnp.log(total)

    return lax.map(one, (q, k, v))


def attend_back_plain(q, k, v, lse, att_grad):
    def one(item):
        q, k, v, lse, out_grad = item
        probs = jnp.exp(nt(q, k) * HEAD_DIM ** (-0.5) - lse)
        probs_grad = nt(out_grad, v)
        inner = jnp.sum(probs * probs_grad, axis=-1, keepdims=True)
        grad = (probs * (probs_grad - inner) * HEAD_DIM ** (-0.5)).astype(bf16)
        return nn(grad, k), tn(grad, q), tn(probs.astype(bf16), out_grad)

    return lax.map(one, (q, k, v, lse, att_grad))


def gelu_and_slope(u):
    c = math.sqrt(2.0 / math.pi)
    inner = jnp.tanh(c * (u + 0.044715 * u * u * u))
    value = 0.5 * u * (1.0 + inner)
    slope = 0.5 * (1.0 + inner) + 0.5 * u * (1.0 - inner * inner) * c * (1.0 + 3 * 0.044715 * u * u)
    return value, slope


def layer_norm(values):
    mean = jnp.mean(values, axis=-1, keepdims=True)
    centred = values - mean
    inverse = lax.rsqrt(jnp.mean(centred * centred, axis=-1, keepdims=True) + norm_eps)
    return centred * inverse, inverse


def norm_back(rows_grad, normal, inverse, scale):
    normal_grad = rows_grad * (1.0 + scale)
    first = jnp.mean(normal_grad, axis=-1, keepdims=True)
    second = jnp.mean(normal_grad * normal, axis=-1, keepdims=True)
    value_grad = inverse * (normal_grad - first - normal * second)
    return value_grad, jnp.sum(rows_grad, axis=0), jnp.sum(rows_grad * normal, axis=0)


def shards(latents, condition, ada_weight, ada_bias, qkv_weight, qv_bias, proj_weight, proj_bias,
           fc1_weight, fc1_bias, fc2_weight, fc2_bias, cotangent):
    plan = Plan(latents, condition, qkv_weight, fc1_weight)
    row, col = lax.axis_index("row"), lax.axis_index("col")
    rows, cols, width, tokens = plan.rows, plan.cols, plan.width, plan.tokens
    depth, hc, fc = plan.depth_rows, plan.head_cols, plan.ff_cols
    heads = cols * hc // HEAD_DIM
    groups = rows * plan.lats

    qkv_flat = qkv_weight.reshape(depth, 3 * hc)
    proj_t, fc2_t = proj_weight.T, fc2_weight.T
    blocks = [qkv_flat[:, :plan.q_main], proj_t[:, :plan.p_main], fc1_weight[:, :plan.f_main], fc2_t[:, :plan.f_main]]
    if plan.near:
        left_a = plan.fold(jnp.concatenate([qkv_flat[:, plan.q_main:], proj_t[:, plan.p_main:]], axis=1))
        blocks += [left_a, plan.fold(fc1_weight[:, plan.f_main:]), plan.fold(fc2_t[:, plan.f_main:])]
        order = (0, 1, 4, 2, 5, 3, 6)
        full = [None] * 7
        for i, w in zip(order, gather_all([blocks[i] for i in order], (3, 2, 2), 0)):
            full[i] = w
        full[4:] = [plan.unfold_full(w) for w in full[4:]]
    else:
        full = gather_plain(blocks)

    if plan.near:
        home = (row - row % 2 + col % 2) * plan.lats + col // 2
    else:
        home = row * plan.lats + col // plan.share
    values = plan.swap(latents).astype(f32)
    grad_out = plan.swap(cotangent).astype(f32)

    cond_all = lax.all_gather(condition, "row", axis=0, tiled=True).astype(f32)
    cond_act = jax.nn.silu(cond_all).astype(bf16)
    cond_mine = lax.dynamic_slice(cond_act, (0, row * depth), (groups, depth))
    ada_flat = ada_weight.reshape(depth, 6 * hc)
    partial = lax.psum(nn(cond_mine, ada_flat), "row") + ada_bias.astype(f32).reshape(1, 6 * hc)
    small = jnp.concatenate(
        [partial.reshape(-1)] + [b.astype(f32).reshape(-1) for b in (proj_bias, fc2_bias, fc1_bias, qv_bias)])
    small = lax.all_gather(small, "col", axis=0, tiled=False)
    sizes = [groups * 6 * hc, hc, hc, fc, 2 * hc]
    mod_all, proj_b, fc2_b, fc1_b, qv_b = jnp.split(small, [sum(sizes[:i + 1]) for i in range(4)], axis=1)
    mod = lax.dynamic_index_in_dim(mod_all.reshape(cols, groups, 6, hc), home, 1, keepdims=False)
    mod = mod.transpose(1, 0, 2).reshape(6, 1, width)
    shift_one, scale_one, gate_one, shift_two, scale_two, gate_two = (mod[k] for k in range(6))
    proj_b, fc2_b = proj_b.reshape(width), fc2_b.reshape(width)
    q_b, v_b = qv_b[:, :hc].reshape(heads, 1, HEAD_DIM), qv_b[:, hc:].reshape(heads, 1, HEAD_DIM)
    fc1_parts = [fc1_b[:, :plan.f_main].reshape(-1)]
    if plan.near:
        fc1_parts.append(fc1_b[:, plan.f_main:].reshape(-1))

    def to_heads(flat):
        return flat.reshape(tokens, heads, HEAD_DIM).transpose(1, 0, 2)

    def from_heads(value):
        return value.transpose(1, 0, 2).reshape(tokens, cols, hc)

    normal_one, inverse_one = layer_norm(values)
    normed_one = (normal_one * (1.0 + scale_one) + shift_one).astype(bf16)
    projected = nn(normed_one, full[0]).reshape(tokens, cols, plan.q_main)
    if plan.near:
        left_w = full[4].reshape(width, cols, 64)
        left_q, left_p = left_w[:, :, :plan.q_left].reshape(width, -1), left_w[:, :, plan.q_left:].reshape(width, -1)
        projected = jnp.concatenate([projected, nn(normed_one, left_q).reshape(tokens, cols, plan.q_left)], axis=2)
    query = (to_heads(projected[:, :, :hc]) + q_b).astype(bf16)
    key = to_heads(projected[:, :, hc:2 * hc]).astype(bf16)
    value = (to_heads(projected[:, :, 2 * hc:]) + v_b).astype(bf16)
    if plan.near:
        att, lse, key_two, value_two = attend(query, key, value, 2)
    else:
        cuts = [[s * plan.share + i for i in range(plan.share)] for s in range(cols // plan.share)]
        key_all = lax.all_gather(key, "col", axis=1, tiled=True, axis_index_groups=cuts)
        value_all = lax.all_gather(value, "col", axis=1, tiled=True, axis_index_groups=cuts)
        att, lse = attend_plain(query, key_all, value_all)
    att_flat = from_heads(att)
    att_main = att_flat[:, :, :plan.p_main].reshape(tokens, -1)
    branch_a = nt(att_main, full[1])
    if plan.near:
        att_left = att_flat[:, :, plan.p_main:]
        branch_a = branch_a + nt(att_left.reshape(tokens, -1), left_p)
    branch_a = branch_a + proj_b
    middle = values + gate_one * branch_a

    count = len(fc1_parts)
    fc1_w, fc2_w = (full[2], full[5])[:count] if plan.near else (full[2],), (full[3], full[6])[:count] if plan.near else (full[3],)
    normal_two, inverse_two = layer_norm(middle)
    normed_two = (normal_two * (1.0 + scale_two) + shift_two).astype(bf16)
    pre = [nn(normed_two, w) + b for w, b in zip(fc1_w, fc1_parts)]
    hidden, slope = zip(*[gelu_and_slope(u) for u in pre])
    hidden = [u.astype(bf16) for u in hidden]
    branch_m = sum(nt(u, w) for u, w in zip(hidden, fc2_w)) + fc2_b
    output = plan.swap((middle + gate_two * branch_m).astype(bf16))

    gate_two_grad = jnp.sum(grad_out * branch_m, axis=0)
    m_grad = grad_out * gate_two
    fc2_bias_part = jnp.sum(m_grad, axis=0)
    m_low = m_grad.astype(bf16)
    fc2_grads = [tn(m_low, u).astype(bf16) for u in hidden]
    pre_grads = [nn(m_low, w) * s for w, s in zip(fc2_w, slope)]
    fc1_bias_parts = [jnp.sum(u, axis=0) for u in pre_grads]
    pre_low = [u.astype(bf16) for u in pre_grads]
    fc1_grads = [tn(normed_two, u).astype(bf16) for u in pre_low]
    normed_two_grad = sum(nt(u, w) for u, w in zip(pre_low, fc1_w))
    middle_part, shift_two_grad, scale_two_grad = norm_back(normed_two_grad, normal_two, inverse_two, scale_two)
    middle_grad = grad_out + middle_part
    gate_one_grad = jnp.sum(middle_grad * branch_a, axis=0)
    a_grad = middle_grad * gate_one
    proj_bias_part = jnp.sum(a_grad, axis=0)
    a_low = a_grad.astype(bf16)
    proj_grad = tn(a_low, att_main).astype(bf16)
    att_grad = nn(a_low, full[1]).reshape(tokens, cols, plan.p_main)
    if plan.near:
        att_grad = jnp.concatenate([att_grad, nn(a_low, left_p).reshape(tokens, cols, plan.p_left)], axis=2)
    att_grad = to_heads(att_grad.astype(bf16))
    if plan.near:
        query_grad, key_grad, value_grad = attend_back(query, key, value, key_two, value_two, lse, att, att_grad, 3)
    else:
        query_grad, key_grad, value_grad = attend_back_plain(query, key_all, value_all, lse, att_grad)
        key_grad, value_grad = (
            lax.psum_scatter(g.astype(bf16), "col", scatter_dimension=1, tiled=True, axis_index_groups=cuts).astype(f32)
            for g in (key_grad, value_grad))
    q_bias_part, v_bias_part = jnp.sum(query_grad, axis=1), jnp.sum(value_grad, axis=1)
    qkv_low = jnp.concatenate([from_heads(g.astype(bf16)) for g in (query_grad, key_grad, value_grad)], axis=2)
    low_main = qkv_low[:, :, :plan.q_main].reshape(tokens, -1)
    qkv_grad = tn(normed_one, low_main).astype(bf16)
    normed_one_grad = nt(low_main, full[0])
    if plan.near:
        low_left = qkv_low[:, :, plan.q_main:]
        normed_one_grad = normed_one_grad + nt(low_left.reshape(tokens, -1), left_q)
        left_grad = jnp.concatenate(
            [tn(normed_one, low_left.reshape(tokens, -1)).reshape(width, cols, -1),
             tn(a_low, att_left.reshape(tokens, -1)).reshape(width, cols, -1)], axis=2).reshape(width, cols * 64).astype(bf16)
        grads = [fc2_grads[0], plan.fold_full(fc2_grads[1]), fc1_grads[0], plan.fold_full(fc1_grads[1]),
                 qkv_grad, proj_grad, plan.fold_full(left_grad)]
        sums = scatter_all(grads, (2, 2, 3), 1)
        fc2_sum = jnp.concatenate([sums[0], plan.unfold(sums[1])], axis=1)
        fc1_sum = jnp.concatenate([sums[2], plan.unfold(sums[3])], axis=1)
        left_sum = plan.unfold(sums[6])
        qkv_sum = jnp.concatenate([sums[4], left_sum[:, :plan.q_left]], axis=1)
        proj_sum = jnp.concatenate([sums[5], left_sum[:, plan.q_left:]], axis=1)
    else:
        fc2_sum, fc1_sum, qkv_sum, proj_sum = scatter_plain([fc2_grads[0], fc1_grads[0], qkv_grad, proj_grad])
    input_part, shift_one_grad, scale_one_grad = norm_back(normed_one_grad, normal_one, inverse_one, scale_one)
    latents_grad = plan.swap((middle_grad + input_part).astype(bf16)).astype(f32)

    mod_grad = jnp.stack(
        [shift_one_grad, scale_one_grad, gate_one_grad, shift_two_grad, scale_two_grad, gate_two_grad], axis=0)
    mod_grad = lax.all_gather(mod_grad, ("row", "col"), axis=0, tiled=False)
    if plan.near:
        mod_grad = mod_grad.reshape(rows // 2, 2, cols // 2, 2, 6, width).sum(axis=1).transpose(0, 2, 1, 3, 4)
    else:
        mod_grad = mod_grad.reshape(rows, cols // plan.share, plan.share, 6, width).sum(axis=2)
    mod_grad = mod_grad.reshape(groups, 6, width)
    mod_mine = lax.dynamic_slice(mod_grad, (0, 0, col * hc), (groups, 6, hc))
    ada_bsum = jnp.sum(mod_mine, axis=0)
    mod_low = mod_mine.astype(bf16).reshape(groups, 6 * hc)
    ada_wsum = tn(cond_mine, mod_low).reshape(depth, 6, hc)
    cond_part = lax.dynamic_update_slice(jnp.zeros((groups, width), f32), nt(mod_low, ada_flat), (0, row * depth))
    parts = [cond_part, proj_bias_part, fc2_bias_part, q_bias_part, v_bias_part] + fc1_bias_parts
    totals = lax.psum(jnp.concatenate([part.reshape(-1) for part in parts]), ("row", "col"))
    ends, spot = [], 0
    for part in parts:
        ends.append(totals[spot:spot + part.size])
        spot += part.size

    def mine(flat, size):
        return lax.dynamic_slice(flat, (col * size,), (size,))

    cond_summed = lax.dynamic_slice(ends[0].reshape(groups, width), (row * plan.lats, 0), (plan.lats, width))
    silu_value, silu_pull = jax.vjp(jax.nn.silu, condition.astype(f32))
    condition_grad = silu_pull(cond_summed)[0]
    proj_bsum, fc2_bsum = mine(ends[1], hc), mine(ends[2], hc)
    qv_bsum = jnp.stack([mine(ends[3], hc), mine(ends[4], hc)], axis=0)
    fc1_bsum = jnp.concatenate([mine(flat, flat.size // cols) for flat in ends[5:]])
    return (
        output, latents_grad, condition_grad, ada_wsum, ada_bsum, qkv_sum.reshape(depth, 3, hc), qv_bsum,
        proj_sum.T, proj_bsum, fc1_sum, fc1_bsum, fc2_sum.T, fc2_bsum)


def solution(mesh):
    token, grid, turned = P(("row", "col"), None), P("row", "col"), P("col", "row")
    cube, wide, flat = P("row", None, "col"), P(None, "col"), P("col")
    return jax.shard_map(
        shards,
        mesh=mesh,
        in_specs=(token, P("row", None), cube, wide, cube, wide, turned, flat, grid, flat, turned, flat, token),
        out_specs=(token, token, P("row", None), cube, wide, cube, wide, turned, flat, grid, flat, turned, flat),
        check_vma=False,
    )
```

time: 2010 us -> 899 us (0.45)
  waiting for transfers between devices: 1320 us -> 0.03 us
  Pallas kernels: 0 us -> 361 us
  matrix products: 341 us -> 128 us
  local copies, waits for them, and re-layouts: 97.3 us -> 184 us
  starting transfers between devices: 1.84 us -> 33.1 us
  other arithmetic: 63.8 us -> 35.2 us
  blocking collectives: 157 us -> 133 us
    reduce_scatter x6 -> x0, waiting for transfers between devices: 642 us -> none  [the longest x2 308 us: back_summed(): lax.psum_scatter(term.astype(jnp.bfloat16), 'col', scatter_dimension=0, t...]
    all_gather x7 -> x0, waiting for transfers between devices: 579 us -> none  [the longest x2 278 us: spread(): lax.all_gather(grad_rows.astype(jnp.bfloat16), 'col', axis=0, tiled=True)]
    pallas_call x0 -> x4, Pallas kernels: none -> 361 us  [the longest x1 151 us: gather_all(): pl.pallas_call(functools.partial(gather_kernel, groups), out_shape=[jax.S...]
    dot_general x48 -> x26, matrix products: 324 us -> 121 us  [the longest x9 48.1 us: nt(): lax.dot_general(a, b, (((1,), (1,)), ((), ())), preferred_element_type=f32)]
    unnamed x23 -> x1, waiting for transfers between devices: 103 us -> 0.02 us
    reshape x1 -> x34, local copies, waits for them, and re-layouts: 4.15 us -> 93.1 us  [the longest x8 57.1 us: fold_full(): left.reshape(self.rows, 2, half, self.cols, 64).transpose(0, 2, 3, 1, 4)]
    all_gather x3, blocking collectives: 74.3 us -> 120 us  [the longest x1 82.2 us: shards(): mod_grad = lax.all_gather(mod_grad, ('row', 'col'), axis=0, tiled=False)]
    unnamed x1 -> x0, blocking collectives: 36.3 us -> none
  transfers between devices with their start and end apart: 18 -> 5, of which waited for: 17 -> 0; matrix products, arithmetic and copies ran while one was open for 7% -> 27% of each run, Pallas kernels for 0% -> 36%
where the time goes in v1:
time: 899 us; the launch traced here: 889 us
  Pallas kernels  361 us (40%)
  local copies, waits for them, and re-layouts  184 us (20%)
  blocking collectives  133 us (15%)
  matrix products  128 us (14%)
  other arithmetic  35.2 us (4%)
  starting transfers between devices  33.1 us (4%)
  between operations  15.4 us (2%)
    pallas_call x1, Pallas kernels, gather_all(): pl.pallas_call(functools.partial(gather_kernel, groups), out_shape=[jax.S...  151 us
    pallas_call x1, Pallas kernels, scatter_all(): pl.pallas_call(functools.partial(scatter_kernel, groups), out_shape=[jax....  148 us
    all_gather x1, blocking collectives, shards(): mod_grad = lax.all_gather(mod_grad, ('row', 'col'), axis=0, tiled=False)  82.2 us
    reshape x8, local copies, waits for them, and re-layouts, fold_full(): left.reshape(self.rows, 2, half, self.cols, 64).transpose(0, 2, 3, 1, 4)  57.1 us
    dot_general x9, matrix products, nt(): lax.dot_general(a, b, (((1,), (1,)), ((), ())), preferred_element_type=f32)  48.1 us
    dot_general x9, matrix products, tn(): lax.dot_general(a, b, (((0,), (0,)), ((), ())), preferred_element_type=f32)  40.6 us
    pallas_call x1, Pallas kernels, attend_back(): pl.pallas_call(attend_back_kernel, out_shape=[jax.ShapeDtypeStruct(q.shap...  36.5 us
    ppermute x4, starting transfers between devices, swap(): lax.ppermute(value, ('row', 'col'), self.swap_pairs())  33.1 us
  transfers between devices with their start and end apart: 5, of which 0 were waited for; matrix products, arithmetic and copies ran while one was open for 27% of the time, Pallas kernels for 36%

profile of v1, /device:TPU:0, one launch (start us, length us, event | category | flops | bytes accessed | tf_op | source)
XLA Modules:
  0.0 888.9 jit_solution(6383525604293131935)
XLA Ops:
  7.3 10.5 %collective-permute-start.2 = (bf16[512,1152]{1,0:T(8,128)(2,1)}, bf16[512,1152]{1,0:T(8,128)(2,1)}, u32[]{:S(2)}, u32[]{:S(2)}) collective-permute-start(bf16[512,1152]{1,0:T(8,128)(2,1)} %param.25), channel_id=1, source_target_pairs={{0,0},{1,8},{2,2},{3,10},{4,4},{5,12},{6,6},{7,14},{8,1},{9,9},{10... | collective-permute-start | bytes 3538952 | tf_op jit(solution)/shard_map/ppermute | solution.py:511
  27.4 6.2 all-gather.2
  34.6 12.6 %psum.14 = f32[16,864]{1,0:T(8,128)S(1)} all-reduce(f32[16,864]{1,0:T(8,128)S(1)} %fusion.73), channel_id=1, replica_groups=mesh['row'=4,'col'=8] {'row'}, use_global_device_ids=true, to_apply=%region_0.1 | all-reduce | flops 13824 | bytes 110592 | tf_op jit(solution)/shard_map/psum | solution.py:603
  47.6 31.6 %all-gather.3 = f32[8,1,14976]{2,1,0:T(1,128)S(1)} all-gather(f32[1,1,14976]{2,1,0:T(1,128)S(1)} %reshape.346), channel_id=2, replica_groups=mesh['row'=4,'col'=8] {'col'}, dimensions={0}, use_global_device_ids=true | all-gather | bytes 539136 | tf_op jit(solution)/shard_map/all_gather | solution.py:606
  85.6 150.7 %gather_weights.1 = (bf16[1152,3072]{1,0:T(8,128)(2,1)}, bf16[1152,1024]{1,0:T(8,128)(2,1)}, bf16[576,1024]{1,0:T(8,128)(2,1)}, bf16[1152,4096]{1,0:T(8,128)(2,1...) custom-call(bf16[288,384]{1,0:T(8,128)(2,1)} %copy.167.refs_0_, ...), custom_call_target="tpu_custom_call" | custom-call | tf_op jit(solution)/shard_map/gather_weights/pallas_call | solution.py:177
  238.3 2.4 reshape.303
  240.7 6.1 copy.131
  246.8 6.3 reshape_reshape.3
  256.1 2.4 reshape.308
  258.5 6.1 copy.136
  264.6 6.3 reshape.309
  271.0 2.2 copy.137
  273.2 2.4 reshape.310
  275.6 6.1 copy.138
  281.7 6.3 reshape.311
  288.8 7.0 fusion.78
  298.3 2.1 pad_maximum_fusion.2
  300.5 4.6 copy.127
  305.1 3.6 copy.129
  308.7 3.4 copy.133
  312.1 4.2 fusion.26.q_ref
  318.2 25.3 %attend.1 = (bf16[16,512,72]{2,1,0:T(8,128)(2,1)S(1)}, f32[16,1,512]{2,1,0:T(1,128)S(1)}, bf16[16,512,72]{2,1,0:T(8,128)(2,1)}, bf16[16,512,72]{2,1,0:T(8,128)(2,1)}) custom-call(bf16[16,512,72]{2,1,0:T(8,128)(2,1)} %fusion.26.q_ref, bf16[16,512,72]{2,1,0:T(8,128)(2,1)} %bitcast.181, bf16[16,512,72]{2,1,0:T(8,128)(2,1)} %fusion.27.v_ref), custom_call_target="tpu_custom_call" | custom-call | tf_op jit(solution)/shard_map/attend/pallas_call | solution.py:401
  344.1 2.5 copy.134
  352.9 7.9 fusion.87
  360.8 12.6 %fusion.74 = f32[512,1152]{1,0:T(8,128)S(1)} fusion(bf16[1152,4096]{1,0:T(8,128)(2,1)} %get-tuple-element.39, f32[512,4096]{1,0:T(8,128)} %fusion.87, f32[4096]{0:T(1024)S(1)} %bitcast.237), kind=kOutput, calls=%fused_computation.161 | convolution fusion | flops 4852809728 | bytes 20201472 | tf_op jit(solution)/shard_map/dot_general | solution.py:349
  373.5 15.6 %fusion.85 = (f32[4096]{0:T(1024)S(1)}, bf16[512,4096]{1,0:T(8,128)(2,1)}) fusion(f32[512,4096]{1,0:T(8,128)} %fusion.87, f32[4096]{0:T(1024)S(1)} %bitcast.238, bf16[1152,4096]{1,0:T(8,128)(2,1)} %get-tuple-element.39, bf16[512,1152]{1,0:T(8,128)(2,1)} %collective-permute-done.2, f32[1152]{0:T(1024)S(1)} %mul.280), kind=kOutput, calls=%fused_computation.168 | convolution fusion | flops 4877643776 | bytes 23237120 | tf_op jit(solution)/shard_map/dot_general | solution.py:353
  389.1 10.3 %fusion.29 = f32[512,1152]{1,0:T(8,128)S(1)} fusion(bf16[1152,4096]{1,0:T(8,128)(2,1)} %get-tuple-element.38, bf16[512,4096]{1,0:T(8,128)(2,1)} %get-tuple-element.150), kind=kOutput, calls=%fused_computation.71 | convolution fusion | flops 4831838208 | bytes 15990784 | tf_op jit(solution)/shard_map/dot_general | solution.py:349
  400.6 3.6 fusion.86
  405.8 5.5 fusion.14
  415.4 2.6 copy.140
  418.0 36.5 %attend_back.1 = (f32[16,512,72]{2,1,0:T(8,128)}, f32[16,512,72]{2,1,0:T(8,128)}, f32[16,512,72]{2,1,0:T(8,128)}) custom-call(bf16[16,512,72]{2,1,0:T(8,128)(2,1)} %fusion.26.q_ref, bf16[16,512,72]{2,1,0:T(8,128)(2,1)} %bitcast.182, bf16[16,512,72]{2,1,0:T(8,128)(2,1)} %fusion.27.v_ref, bf16[16,512,72]{2,1,0:T(8,128)(2,1)} %get-tuple-element.42.k2_ref, ...), custom_call_target="tpu_custom_call" | custom-call | tf_op jit(solution)/shard_map/attend_back/pallas_call | solution.py:458
  454.5 9.0 %fusion.81 = (f32[16,72]{1,0:T(8,128)S(1)}, bf16[512,16,72]{2,0,1:T(8,128)(2,1)S(1)}, bf16[512,16,72]{2,0,1:T(8,128)(2,1)}, f32[16,72]{1,0:T(8,128)S(1)}) fusion(f32[16,512,72]{2,1,0:T(8,128)} %get-tuple-element.47, f32[16,512,72]{2,1,0:T(8,128)} %get-tuple-element.45), kind=kLoop, calls=%fused_computation.164 | loop fusion | flops 2356992 | bytes 7087104 | tf_op jit(solution)/shard_map/reduce_sum | solution.py:688
  463.5 2.3 copy.143
  465.9 3.7 convolution_bitcast_fusion.1
  469.9 2.4 copy.142
  472.3 3.8 copy.141
  476.1 2.1 pad_maximum_fusion
  478.8 10.6 %fusion.23 = (f32[1152]{0:T(1024)S(1)}, f32[512]{0:T(512)}, f32[512]{0:T(512)}, f32[1152]{0:T(1024)S(1)}, f32[512,1152]{1,0:T(8,128)}) fusion(bf16[512,1152]{1,0:T(8,128)(2,1)S(1)} %copy-done.5, f32[512]{0:T(512)S(1)} %add_rsqrt_fusion.1, f32[512]{0:T(512)S(1)} %broadcast_multiply_fusion.5, f32[1152]{0:T(1024)S(1)} %add.248, ...), kind=kOutput, calls=%fused_computation.50 | convolution fusion | flops 3630363648 | bytes 16143872 | tf_op jit(solution)/shard_map/dot_general | solution.py:349
  489.6 82.2 %all-gather.4 = f32[32,6,1152]{2,1,0:T(8,128)} all-gather(f32[1,6,1152]{2,1,0:T(8,128)S(1)} %bitcast.234), channel_id=3, replica_groups=mesh['row'=4,'col'=8] {'row','col'}, dimensions={0}, use_global_device_ids=true | all-gather | bytes 912384 | tf_op jit(solution)/shard_map/all_gather | solution.py:714
  571.8 2.2 reduce_sum.212
  577.5 9.8 %convolution_convert_fusion.refs_2_ = bf16[1152,4096]{1,0:T(8,128)(2,1)} fusion(bf16[512,1152]{1,0:T(8,128)(2,1)} %copy-done.24, bf16[512,4096]{1,0:T(8,128)(2,1)} %get-tuple-element.150), kind=kOutput, calls=%fused_computation | convolution fusion | flops 4836556800 | bytes 14811136 | tf_op jit(solution)/shard_map/dot_general | solution.py:357
  589.2 2.9 convolution_convert_fusion.3.refs_5_
  592.1 2.1 convolution_convert_fusion.7
  594.2 10.3 %collective-permute-start.1 = (bf16[512,1152]{1,0:T(8,128)(2,1)}, bf16[512,1152]{1,0:T(8,128)(2,1)}, u32[]{:S(2)}, u32[]{:S(2)}) collective-permute-start(bf16[512,1152]{1,0:T(8,128)(2,1)} %get-tuple-element.134), channel_id=1, source_target_pairs={{0,0},{1,8},{2,2},{3,10},{4,4},{5,12},{6,6},{7,14},{8,1},{9,9},{10... | collective-permute-start | bytes 3538952 | tf_op jit(solution)/shard_map/ppermute | solution.py:511
  606.5 10.3 %collective-permute-start.3 = (bf16[512,1152]{1,0:T(8,128)(2,1)}, bf16[512,1152]{1,0:T(8,128)(2,1)}, u32[]{:S(2)}, u32[]{:S(2)}) collective-permute-start(bf16[512,1152]{1,0:T(8,128)(2,1)} %fusion.22), channel_id=1, source_target_pairs={{0,0},{1,8},{2,2},{3,10},{4,4},{5,12},{6,6},{7,14},{8,1},{9,9},{10... | collective-permute-start | bytes 3538952 | tf_op jit(solution)/shard_map/ppermute | solution.py:511
  618.6 2.2 fusion.63
  620.9 3.6 convolution_convert_fusion.5
  624.4 2.4 copy.147
  626.8 8.7 reshape.324
  635.5 10.8 %copy.161 = bf16[4,144,8,2,64]{4,3,2,1,0:T(2,128)(2,1)} copy(bf16[4,144,8,2,64]{1,3,0,4,2:T(2,128)(2,1)} %bitcast.191) | data formatting | bytes 2359296 | tf_op jit(solution)/shard_map/reshape | solution.py:496
  646.3 6.4 reshape.359.refs_1_
  652.7 2.4 copy.149
  655.1 8.7 reshape.326
  663.7 10.8 %copy.162 = bf16[4,144,8,2,64]{4,3,2,1,0:T(2,128)(2,1)} copy(bf16[4,144,8,2,64]{1,3,0,4,2:T(2,128)(2,1)} %bitcast.192) | data formatting | bytes 2359296 | tf_op jit(solution)/shard_map/reshape | solution.py:496
  674.5 6.4 reshape.360.refs_3_
  682.1 4.1 convert_element_type.150
  686.2 3.9 copy.175
  690.0 3.9 reshape.330
  695.4 10.5 %convolution_convert_fusion.1.refs_0_ = bf16[1152,4096]{1,0:T(8,128)(2,1)} fusion(bf16[512,1152]{1,0:T(8,128)(2,1)} %collective-permute-done.2, f32[1152]{0:T(1024)S(1)} %mul.280, f32[512,4096]{1,0:T(8,128)} %fusion.87, f32[4096]{0:T(1024)S(1)} %bitcast.239), kind=kOutput, calls=%fused_computation.1 | convolution fusion | flops 4859297792 | bytes 19026432 | tf_op jit(solution)/shard_map/dot_general | solution.py:357
  705.9 6.7 convolution_convert_fusion.2.refs_4_
  712.6 148.4 %scatter_grads.1 = (f32[288,512]{1,0:T(8,128)}, f32[144,128]{1,0:T(8,128)}, f32[288,512]{1,0:T(8,128)}, f32[144,128]{1,0:T(8,128)}, f32[288,384]{1,0:T(8,128)}, /*index=5*/f32[288,128]{1,0:T(8,128)}, f32[144,128]{1,0:T(8,128)}) custom-call(bf16[1152,4096]{1,0:T(8,128)(2,1)} %convolution_convert_fusion.1.refs_0_, bf16[576,1024]{1,0:T(8,128)(2,1)} %reshape.359.refs_1_, ...), custom_call_target="tpu_custom_call" | custom-call | tf_op jit(solution)/shard_map/scatter_grads/pallas_call | solution.py:337
  863.2 2.0 pad_maximum_fusion.5
  876.6 2.8 convert_element_type.141
  879.5 2.4 copy.188
  (245 shorter events, 67.3 us)
Async XLA Ops:
  7.2 26.4 %copy-start = (bf16[288,6,144]{0,2,1:T(8,128)(2,1)S(1)}, bf16[288,6,144]{0,2,1:T(8,128)(2,1)}, u32[]{:S(2)}) copy-start(bf16[288,6,144]{0,2,1:T(8,128)(2,1)} %param.15) | copy-start | bytes 1492996
  7.2 20.2 %copy-start.35 = (bf16[4,1152]{1,0:T(4,128)(2,1)S(1)}, bf16[4,1152]{1,0:T(4,128)(2,1)}, u32[]{:S(2)}) copy-start(bf16[4,1152]{1,0:T(4,128)(2,1)} %param.14) | copy-start | bytes 27652
  7.2 39.9 %copy-start.38 = (bf16[6,144]{1,0:T(8,128)(2,1)S(1)}, bf16[6,144]{1,0:T(8,128)(2,1)}, u32[]{:S(2)}) copy-start(bf16[6,144]{1,0:T(8,128)(2,1)} %param.16) | copy-start | bytes 5188
  7.2 40.1 %copy-start.43 = (bf16[2,144]{1,0:T(2,128)(2,1)S(1)}, bf16[2,144]{1,0:T(2,128)(2,1)}, u32[]{:S(2)}) copy-start(bf16[2,144]{1,0:T(2,128)(2,1)} %param.18) | copy-start | bytes 1732
  7.2 40.2 %copy-start.44 = (bf16[144]{0:T(256)(128)(2,1)S(1)}, bf16[144]{0:T(256)(128)(2,1)}, u32[]{:S(2)}) copy-start(bf16[144]{0:T(256)(128)(2,1)} %param.20) | copy-start | bytes 868
  7.2 40.2 %copy-start.45 = (bf16[144]{0:T(256)(128)(2,1)S(1)}, bf16[144]{0:T(256)(128)(2,1)}, u32[]{:S(2)}) copy-start(bf16[144]{0:T(256)(128)(2,1)} %param.24) | copy-start | bytes 868
  7.2 40.2 %copy-start.39 = (bf16[576]{0:T(1024)(128)(2,1)S(1)}, bf16[576]{0:T(1024)(128)(2,1)}, u32[]{:S(2)}) copy-start(bf16[576]{0:T(1024)(128)(2,1)} %param.22) | copy-start | bytes 3460
  7.3 862.8 %all-reduce.2.cloned.1.call-start = ((), (), s32[]{:S(2)}) async-start(), calls=%async_computation | async-start | bytes 221184 | tf_op jit(solution)/shard_map/psum | solution.py:726
  7.3 366.2 %collective-permute-start.2 = (bf16[512,1152]{1,0:T(8,128)(2,1)}, bf16[512,1152]{1,0:T(8,128)(2,1)}, u32[]{:S(2)}, u32[]{:S(2)}) collective-permute-start(bf16[512,1152]{1,0:T(8,128)(2,1)} %param.25), channel_id=1, source_target_pairs={{0,0},{1,8},{2,2},{3,10},{4,4},{5,12},{6,6},{7,14},{8,1},{9,9},{10... | collective-permute-start | bytes 3538952 | tf_op jit(solution)/shard_map/ppermute | solution.py:511
  17.8 270.3 %collective-permute-start = (bf16[512,1152]{1,0:T(8,128)(2,1)}, bf16[512,1152]{1,0:T(8,128)(2,1)S(1)}, u32[]{:S(2)}, u32[]{:S(2)}) collective-permute-start(bf16[512,1152]{1,0:T(8,128)(2,1)} %param.13), channel_id=1, source_target_pairs={{0,0},{1,8},{2,2},{3,10},{4,4},{5,12},{6,6},{7,14},{8,1},{9,9},{10... | collective-permute-start | bytes 3538952 | tf_op jit(solution)/shard_map/ppermute | solution.py:511
  33.6 0.6 copy-start.32
  79.1 5.0 slice-start
  79.2 157.2 %copy-start.19 = (f32[8,1,14976]{2,0,1:T(8,128)}, f32[8,1,14976]{2,0,1:T(8,128)S(1)}, u32[]{:S(2)}) copy-start(f32[8,1,14976]{2,0,1:T(8,128)S(1)} %copy.176) | copy-start | bytes 1437700
  288.1 8.9 %copy-start.3 = (bf16[512,1152]{1,0:T(8,128)(2,1)}, bf16[512,1152]{1,0:T(8,128)(2,1)S(1)}, u32[]{:S(2)}) copy-start(bf16[512,1152]{1,0:T(8,128)(2,1)S(1)} %collective-permute-done) | copy-start | bytes 3538948
  295.8 1.7 copy-start.20
  312.1 4.2 copy-start.6
  343.5 0.6 copy-start.2
  344.1 4.1 copy-start.1
  346.6 1.7 copy-start.11
  346.6 2.2 copy-start.18
  348.3 1.8 copy-start.4
  348.3 4.6 slice-start.1
  348.4 3.6 copy-start.12
  350.0 2.8 slice-start.2
  350.0 2.8 slice-start.3
  352.9 46.5 %copy-start.24 = (bf16[512,1152]{1,0:T(8,128)(2,1)}, bf16[512,1152]{1,0:T(8,128)(2,1)S(1)}, u32[]{:S(2)}) copy-start(bf16[512,1152]{1,0:T(8,128)(2,1)S(1)} %add_convert_fusion.3) | copy-start | bytes 3538948
  389.1 10.3 %copy-start.9 = (bf16[1152,512]{0,1:T(8,128)(2,1)S(1)}, bf16[1152,512]{0,1:T(8,128)(2,1)}, u32[]{:S(2)}) copy-start(bf16[1152,512]{0,1:T(8,128)(2,1)} %reshape.309) | copy-start | bytes 3538948
  399.4 1.3 copy-start.21
  400.6 5.1 copy-start.46
  404.3 1.5 copy-start.27
  411.3 1.9 copy-start.7
  411.5 1.7 copy-start.22
  465.8 3.7 copy-start.14
  472.3 3.8 copy-start.10
  476.1 2.1 copy-start.5
  476.1 2.7 copy-start.47
  478.2 11.3 %copy-start.15 = (bf16[512,8,384]{0,2,1:T(8,128)(2,1)}, bf16[512,8,384]{0,2,1:T(8,128)(2,1)S(1)}, u32[]{:S(2)}) copy-start(bf16[512,8,384]{0,2,1:T(8,128)(2,1)S(1)} %pad_maximum_fusion) | copy-start | bytes 9437188
  577.5 9.9 %copy-start.25 = (bf16[512,1152]{1,0:T(8,128)(2,1)S(1)}, bf16[512,1152]{1,0:T(8,128)(2,1)}, u32[]{:S(2)}) copy-start(bf16[512,1152]{1,0:T(8,128)(2,1)} %copy-done.24) | copy-start | bytes 3538948
  577.5 9.9 %copy-start.28 = (bf16[512,512]{1,0:T(8,128)(2,1)S(1)}, bf16[512,512]{1,0:T(8,128)(2,1)}, u32[]{:S(2)}) copy-start(bf16[512,512]{1,0:T(8,128)(2,1)} %copy-done.27) | copy-start | bytes 1572868
  587.3 1.9 copy-start.13
  587.4 1.9 copy-start.23
  592.1 12.5 %copy-start.42 = (f32[512]{0:T(512)S(1)}, f32[512]{0:T(512)}, u32[]{:S(2)}) copy-start(f32[512]{0:T(512)} %get-tuple-element.110) | copy-start | bytes 6148
  592.1 12.5 %copy-start.41 = (f32[512]{0:T(512)S(1)}, f32[512]{0:T(512)}, u32[]{:S(2)}) copy-start(f32[512]{0:T(512)} %get-tuple-element.111) | copy-start | bytes 6148
  592.1 12.5 %copy-start.8 = (f32[512,1152]{1,0:T(8,128)S(1)}, f32[512,1152]{1,0:T(8,128)}, u32[]{:S(2)}) copy-start(f32[512,1152]{1,0:T(8,128)} %copy-done.7) | copy-start | bytes 7077892
  592.1 12.5 %copy-start.17 = (f32[512,1152]{1,0:T(8,128)S(1)}, f32[512,1152]{1,0:T(8,128)}, u32[]{:S(2)}) copy-start(f32[512,1152]{1,0:T(8,128)} %get-tuple-element.148) | copy-start | bytes 7077892
  594.2 282.4 %collective-permute-start.1 = (bf16[512,1152]{1,0:T(8,128)(2,1)}, bf16[512,1152]{1,0:T(8,128)(2,1)}, u32[]{:S(2)}, u32[]{:S(2)}) collective-permute-start(bf16[512,1152]{1,0:T(8,128)(2,1)} %get-tuple-element.134), channel_id=1, source_target_pairs={{0,0},{1,8},{2,2},{3,10},{4,4},{5,12},{6,6},{7,14},{8,1},{9,9},{10... | collective-permute-start | bytes 3538952 | tf_op jit(solution)/shard_map/ppermute | solution.py:511
  604.6 13.1 %copy-start.37 = (f32[1152]{0:T(1024)S(1)}, f32[1152]{0:T(1024)}, u32[]{:S(2)}) copy-start(f32[1152]{0:T(1024)} %get-tuple-element.136) | copy-start | bytes 13828
  604.6 13.1 %copy-start.40 = (f32[512]{0:T(512)S(1)}, f32[512]{0:T(512)}, u32[]{:S(2)}) copy-start(f32[512]{0:T(512)} %get-tuple-element.151) | copy-start | bytes 6148
  606.5 270.2 %collective-permute-start.3 = (bf16[512,1152]{1,0:T(8,128)(2,1)}, bf16[512,1152]{1,0:T(8,128)(2,1)}, u32[]{:S(2)}, u32[]{:S(2)}) collective-permute-start(bf16[512,1152]{1,0:T(8,128)(2,1)} %fusion.22), channel_id=1, source_target_pairs={{0,0},{1,8},{2,2},{3,10},{4,4},{5,12},{6,6},{7,14},{8,1},{9,9},{10... | collective-permute-start | bytes 3538952 | tf_op jit(solution)/shard_map/ppermute | solution.py:511
  617.7 0.6 copy-start.30
  680.9 1.0 copy-start.31
  695.4 10.5 %copy-start.16 = (bf16[512,8,384]{0,2,1:T(8,128)(2,1)S(1)}, bf16[512,8,384]{0,2,1:T(8,128)(2,1)}, u32[]{:S(2)}) copy-start(bf16[512,8,384]{0,2,1:T(8,128)(2,1)} %copy-done.15) | copy-start | bytes 9437188
  861.0 4.2 copy-start.29
  861.0 4.4 copy-start.34
  861.0 4.6 copy-start.26
  863.2 3.3 copy-start.33
  865.6 10.4 %copy-start.36 = (bf16[4,1152]{1,0:T(4,128)(2,1)S(1)}, bf16[4,1152]{1,0:T(4,128)(2,1)}, u32[]{:S(2)}) copy-start(bf16[4,1152]{1,0:T(4,128)(2,1)} %param.14) | copy-start | bytes 27652
Sparse Core Ops, SparseCore 0:
  618.5 118.1 all-reduce.1

commit v2 on v1

--- a/solution.py
+++ b/solution.py
@@ -32,6 +32,9 @@
 
     def to_z(self, z):
         return (self.row, 2 * z + self.x)
+
+    def diagonal(self):
+        return (self.row + 1 - 2 * self.h, self.col + 1 - 2 * self.x)
 
     def yx(self, p, q):
         return jnp.where(self.h == 0, p, q), jnp.where(self.h == 0, q, p)
@@ -135,13 +138,14 @@
             self.c_p(a, t, 1).wait_recv()
             self.c_k(a, t, 3).start()
         else:
+            if t == 0:
+                self.c_local(a).wait()
             for j in range(4):
                 self.c_k(a, t, j).wait_recv()
 
     def finish(self, a):
         for k in range(1, self.at.depth):
             self.c_z(a, k).wait_send()
-        self.c_local(a).wait()
         for t in range(self.at.depth):
             self.c_q(a, t).wait_send()
             for j in range(2):
@@ -466,6 +470,477 @@
     )(q, k, v, k2, v2, lse, att, att_grad)
 
 
+VECS = 24
+
+
+def softmax_head(q, k, k2):
+    one, two = nt(k, q), nt(k2, q)
+    top = jnp.maximum(jnp.max(one, axis=0, keepdims=True), jnp.max(two, axis=0, keepdims=True)) * SOFT
+    one, two = jnp.exp2(one * SOFT - top), jnp.exp2(two * SOFT - top)
+    total = jnp.sum(one, axis=0, keepdims=True) + jnp.sum(two, axis=0, keepdims=True)
+    return one.astype(bf16), two.astype(bf16), total, top + jnp.log2(total)
+
+
+def norm_rows(values):
+    mean = jnp.mean(values, axis=-1, keepdims=True)
+    centred = values - mean
+    inverse = lax.rsqrt(jnp.mean(centred * centred, axis=-1, keepdims=True) + norm_eps)
+    return centred * inverse, inverse
+
+
+def gelu_both(u):
+    c = math.sqrt(2.0 / math.pi)
+    square = u * u
+    inner = jnp.tanh(u * (c + (c * 0.044715) * square))
+    half = 0.5 * (1.0 + inner)
+    slope = half + (0.5 * u) * (1.0 - inner * inner) * (c + (3 * c * 0.044715) * square)
+    return u * half, slope
+
+
+class Swap:
+    def __init__(self, place, src, dst, sems, i):
+        self.stay = place.h == place.x
+        self.local = pltpu.make_async_copy(src, dst, sems.at[i, 0])
+        self.remote = pltpu.make_async_remote_copy(
+            src_ref=src, dst_ref=dst, send_sem=sems.at[i, 0], recv_sem=sems.at[i, 1],
+            device_id=place.diagonal(), device_id_type=MESH)
+
+    def start(self):
+        pl.when(self.stay)(self.local.start)
+        pl.when(jnp.logical_not(self.stay))(self.remote.start)
+
+    def wait(self):
+        pl.when(self.stay)(self.local.wait)
+        pl.when(jnp.logical_not(self.stay))(self.remote.wait)
+
+
+def unfold_into(left, target):
+    rows = target.shape[0] // 4
+    half = rows // 2
+    for r in range(4):
+        tile = left[r * half:(r + 1) * half, :].astype(f32)
+        target[r * rows:r * rows + half, :] = jnp.concatenate([tile[:, :64], tile[:, 128:192]], axis=1).astype(bf16)
+        target[r * rows + half:(r + 1) * rows, :] = jnp.concatenate([tile[:, 64:128], tile[:, 192:]], axis=1).astype(bf16)
+
+
+GROUPS = (3, 2, 2)
+
+
+def forward_kernel(*refs):
+    lat, cot, cond, ada, bias = refs[:5]
+    blocks, refs = refs[5:12], refs[12:]
+    fulls, refs = refs[:7], refs[7:]
+    (o_w, o_cot, o_x, o_n1, o_q, o_k, o_v, o_k2, o_v2, o_lse, o_att, o_ba, o_mid, o_n2, o_hid, o_slo, o_out, o_vec), refs = refs[:18], refs[18:]
+    (x_v, n1, q_v, k_v, v_v, k2_v, v2_v, lse_v, ot, att, ba, mid, n2, hid, slo, acc, wbuf, lbuf, out_v, cot_v, vec,
+     c_send, c_recv, s_send, s_recv, m_own, m_oth), refs = refs[:27], refs[27:]
+    ag_sems, (swap_sems, c_sems, s_sems, m_sems, o_sems, kv_sems, w_sems, save_sems, wsave_sems) = refs[:5], refs[5:]
+
+    place = Place()
+    depth, rows_n = place.depth, 4
+    row, col = place.row, place.col
+    cols_n = 2 * depth
+    tokens, width = x_v.shape
+    hc = width // cols_n
+    drows = ada.shape[0]
+    q_main, p_main = blocks[0].shape[1], blocks[1].shape[1]
+    half = tokens // 2
+
+    row_peers = [((row + k) % rows_n, col) for k in range(1, rows_n)]
+    col_peers = [(row, (col + k) % cols_n) for k in range(1, cols_n)]
+    greet(place.partners() + row_peers + col_peers + [place.diagonal()])
+
+    def send(src, dst, s_sem, r_sem, to):
+        return pltpu.make_async_remote_copy(
+            src_ref=src, dst_ref=dst, send_sem=s_sem, recv_sem=r_sem, device_id=to, device_id_type=MESH)
+
+    cond_value = cond[...]
+    act = (cond_value / (1.0 + jnp.exp(-cond_value))).astype(bf16).astype(f32)
+    for r in range(rows_n):
+        c_send[r] = act[:, r * drows:(r + 1) * drows]
+
+    def cond_copy(k):
+        to = (row + k) % rows_n
+        return send(c_send.at[to], c_recv.at[row], c_sems.at[0, k], c_sems.at[1, row], (to, col))
+
+    def cond_got(k):
+        src = (row + k) % rows_n
+        return send(c_send.at[src], c_recv.at[src], c_sems.at[0, k], c_sems.at[1, src], (src, col))
+
+    for k in range(1, rows_n):
+        cond_copy(k).start()
+    swap_x = Swap(place, lat, x_v, swap_sems, 0)
+    swap_x.start()
+
+    work = Gather(place, blocks, fulls, ag_sems)
+    for a in range(3):
+        work.start(a)
+
+    members, first = [], 0
+    for size in GROUPS:
+        members.append(list(range(first, first + size)))
+        first += size
+    chunks = [(g, t) for g in range(len(GROUPS)) for t in range(depth)]
+    events = [(s - n, n) for s in range(len(chunks) + 4) for n in range(5) if 0 <= s - n < len(chunks)]
+    at = [0]
+
+    def pump(count):
+        for s, n in events[at[0]:at[0] + count]:
+            if n == 0 and s in (2, depth + 2):
+                for a in members[1 if s == 2 else 2]:
+                    work.start(a)
+            g, t = chunks[s]
+            for a in members[g]:
+                work.stage(a, t, n)
+        at[0] += count
+
+    def pump_to(s, n):
+        pump(max(0, events.index((s, n)) + 1 - at[0]))
+
+    pump_to(0, 0)
+    c_recv[row] = c_send[row]
+    for k in range(1, rows_n):
+        cond_got(k).wait_recv()
+    act_all = c_recv[...].reshape(rows_n * 8, drows).astype(bf16)
+    s_send[...] = nn(act_all, ada[...]).reshape(rows_n, 8, 6 * hc)
+
+    def sum_copy(k):
+        to = (row + k) % rows_n
+        return send(s_send.at[to], s_recv.at[row], s_sems.at[0, k], s_sems.at[1, row], (to, col))
+
+    def sum_got(k):
+        src = (row + k) % rows_n
+        return send(s_send.at[src], s_recv.at[src], s_sems.at[0, k], s_sems.at[1, src], (src, col))
+
+    for k in range(1, rows_n):
+        sum_copy(k).start()
+    pump_to(0, 1)
+    s_recv[row] = s_send[row]
+    for k in range(1, rows_n):
+        sum_got(k).wait_recv()
+    m_own[col] = s_recv[0] + s_recv[1] + s_recv[2] + s_recv[3] + bias[...]
+
+    def mod_copy(k):
+        return send(m_own.at[col], m_own.at[col], m_sems.at[0, k], m_sems.at[1, col], (row, (col + k) % cols_n))
+
+    def mod_got(k):
+        src = (col + k) % cols_n
+        return send(m_own.at[src], m_own.at[src], m_sems.at[0, k], m_sems.at[1, src], (row, src))
+
+    for k in range(1, cols_n):
+        mod_copy(k).start()
+    pump_to(0, 2)
+    for k in range(1, cols_n):
+        mod_got(k).wait_recv()
+    other = send(m_own, m_oth, o_sems.at[0], o_sems.at[1], place.to_core)
+    other.start()
+    pump_to(0, 3)
+    other.wait_recv()
+    stay = place.h == place.x
+    for c in range(cols_n):
+        line = jnp.where(stay, m_own[c, pl.ds(place.z, 1), :], m_oth[c, pl.ds(place.z, 1), :])
+        for k in range(6):
+            vec[k:k + 1, c * hc:(c + 1) * hc] = line[:, k * hc:(k + 1) * hc]
+        line = m_own[c, 4:5, :]
+        vec[6:7, c * hc:(c + 1) * hc] = line[:, 576:576 + hc]
+        vec[7:8, c * hc:(c + 1) * hc] = line[:, 576 + hc:]
+        z, i = c // 2, c % 2
+        vec[16 + z:17 + z, i * 512:(i + 1) * 512] = line[:, :512]
+        vec[16 + z:17 + z, 1024 + i * 64:1024 + (i + 1) * 64] = line[:, 512:576]
+
+    swap_x.wait()
+    swap_dy = Swap(place, cot, o_cot, swap_sems, 1)
+    swap_dy.start()
+    part = 128
+
+    def row_parts(body):
+        @pl.loop(0, tokens // part)
+        def _(i):
+            body(pl.ds(pl.multiple_of(i * part, part), part))
+
+    def first_norm(at_rows):
+        normal, _ = norm_rows(x_v[at_rows, :].astype(f32))
+        n1[at_rows, :] = (normal * (1.0 + vec[1:2, :]) + vec[0:1, :]).astype(bf16)
+
+    row_parts(first_norm)
+
+    saves = []
+
+    def save(src, dst):
+        copy = pltpu.make_async_copy(src, dst, save_sems.at[len(saves)])
+        copy.start()
+        saves.append(copy)
+
+    save(x_v, o_x)
+    save(n1, o_n1)
+
+    def fetch(s):
+        g, t = chunks[s]
+        zc, slot = work.zc(t), s % depth
+        lanes = [q_main, p_main] if g == 0 else [blocks[members[g][0]].shape[1]]
+        spot, copies = 0, []
+        for i, n in enumerate(lanes):
+            src = fulls[members[g][i]].at[:, pl.ds(pl.multiple_of(zc * 2 * n, 128), 2 * n)]
+            copies.append(pltpu.make_async_copy(src, wbuf.at[slot, :, spot:spot + 2 * n], w_sems.at[s % 2, i]))
+            spot += 2 * n
+        src = fulls[members[g][-1]].at[:, pl.ds(pl.multiple_of(zc * 256, 128), 256)]
+        copies.append(pltpu.make_async_copy(src, lbuf.at[s % 2], w_sems.at[s % 2, 2]))
+        return copies
+
+    def fetch_start(s):
+        pump_to(s, 4)
+        if s >= depth:
+            weight_save(s - depth).wait()
+        for copy in fetch(s):
+            copy.start()
+
+    def fetch_wait(s):
+        for copy in fetch(s):
+            copy.wait()
+        unfold_into(lbuf.at[s % 2], wbuf.at[s % depth, :, 1024:1152])
+        weight_save(s).start()
+
+    def weight_save(s):
+        g, t = chunks[s]
+        return pltpu.make_async_copy(wbuf.at[s % depth], o_w.at[g, work.zc(t)], wsave_sems.at[s])
+
+    def swap_kv(i, h):
+        src, dst = ((k_v, k2_v), (v_v, v2_v))[i]
+        return send(src.at[h], dst.at[h], kv_sems.at[0, i, h], kv_sems.at[1, i, h], place.to_core)
+
+    def project(s):
+        t, slot = chunks[s][1], s % depth
+        zc = work.zc(t)
+
+        @pl.loop(0, 2)
+        def _(i):
+            at_rows = pl.ds(pl.multiple_of(i * half, half), half)
+            main = nn(n1[at_rows, :], wbuf[slot, :, :2 * q_main])
+            left = nn(n1[at_rows, :], wbuf[slot, :, 1024:1152])
+            for j in range(2):
+                biases = m_own[2 * zc + j]
+                own = main[:, j * q_main:(j + 1) * q_main]
+                tail = left[:, j * 64:j * 64 + 3 * hc - q_main]
+                for e in range(2):
+                    h = 4 * zc + 2 * j + e
+                    a = e * HEAD_DIM
+                    q_v[h, at_rows, :] = (own[:, a:a + HEAD_DIM] + biases[5:6, a:a + HEAD_DIM]).astype(bf16)
+                    k_v[h, at_rows, :] = own[:, hc + a:hc + a + HEAD_DIM].astype(bf16)
+                    if e == 0:
+                        value = own[:, 2 * hc:2 * hc + HEAD_DIM]
+                    else:
+                        value = jnp.concatenate([own[:, 2 * hc + HEAD_DIM:], tail], axis=1)
+                    v_v[h, at_rows, :] = (value + biases[5:6, hc + a:hc + a + HEAD_DIM]).astype(bf16)
+
+        for i in range(4):
+            swap_kv(0, 4 * zc + i).start()
+            swap_kv(1, 4 * zc + i).start()
+
+    def attention(s):
+        zc = work.zc(chunks[s][1])
+        start = at[0]
+
+        @pl.loop(0, 4)
+        def _(i):
+            h = 4 * zc + i
+            swap_kv(0, h).wait_recv()
+            swap_kv(1, h).wait_recv()
+            one, two, total, lse = softmax_head(q_v[h], k_v[h], k2_v[h])
+            ot[i] = (tn(v_v[h], one) + tn(v2_v[h], two)) / total
+            lse_v[h] = lse
+            for k in range(4):
+                at[0] = start + k
+
+                @pl.when(i == k)
+                def _():
+                    pump(1)
+
+        at[0] = start + 4
+        att[zc, :, 2 * p_main:] = jnp.zeros((tokens, 128), bf16)
+        for j in range(2):
+            pair = jnp.concatenate([ot[2 * j], ot[2 * j + 1]], axis=0).T.astype(bf16)
+            att[zc, :, j * p_main:(j + 1) * p_main] = pair[:, :p_main]
+            att[zc, :, 2 * p_main + 64 * j + 48:2 * p_main + 64 * j + 64] = pair[:, p_main:]
+
+        @pl.loop(0, 2)
+        def _(i):
+            at_rows = pl.ds(pl.multiple_of(i * half, half), half)
+            term = nt(att[zc, at_rows, :], wbuf[s % depth, :, 2 * q_main:])
+            if s == 0:
+                acc[at_rows, :] = term
+            else:
+                acc[at_rows, :] += term
+
+    for s in range(depth):
+        fetch_start(s)
+        fetch_wait(s)
+        project(s)
+        if s > 0:
+            attention(s - 1)
+    attention(depth - 1)
+    for src, dst in ((q_v, o_q), (k_v, o_k), (v_v, o_v), (k2_v, o_k2), (v2_v, o_v2), (lse_v, o_lse), (att, o_att)):
+        save(src, dst)
+
+    def second_norm(at_rows):
+        branch = acc[at_rows, :] + vec[6:7, :]
+        ba[at_rows, :] = branch.astype(bf16)
+        middle = x_v[at_rows, :].astype(f32) + vec[2:3, :] * branch
+        mid[at_rows, :] = middle
+        normal, _ = norm_rows(middle)
+        n2[at_rows, :] = (normal * (1.0 + vec[4:5, :]) + vec[3:4, :]).astype(bf16)
+
+    row_parts(second_norm)
+    for src, dst in ((ba, o_ba), (mid, o_mid), (n2, o_n2)):
+        save(src, dst)
+
+    for s in range(depth, 2 * depth):
+        fetch_start(s)
+        fetch_wait(s)
+        zc = work.zc(chunks[s][1])
+
+        def up(at_rows):
+            u = nn(n2[at_rows, :], wbuf[s % depth]) + vec[pl.ds(16 + zc, 1), :]
+            value, slope = gelu_both(u)
+            hid[zc, at_rows, :] = value.astype(bf16)
+            slo[zc, at_rows, :] = slope.astype(bf16)
+
+        row_parts(up)
+    save(hid, o_hid)
+    save(slo, o_slo)
+    for s in range(2 * depth, 3 * depth):
+        fetch_start(s)
+        fetch_wait(s)
+        zc = work.zc(chunks[s][1])
+
+        def down(at_rows):
+            term = nt(hid[zc, at_rows, :], wbuf[s % depth])
+            if s == 2 * depth:
+                acc[at_rows, :] = term
+            else:
+                acc[at_rows, :] += term
+
+        row_parts(down)
+
+    swap_dy.wait()
+    load_dy = pltpu.make_async_copy(o_cot, cot_v, w_sems.at[0, 0])
+    load_dy.start()
+    load_dy.wait()
+    vec[8:9, :] = jnp.zeros((1, width), f32)
+
+    def finish(at_rows):
+        branch = acc[at_rows, :] + vec[7:8, :]
+        out_v[at_rows, :] = (mid[at_rows, :] + vec[5:6, :] * branch).astype(bf16)
+        vec[8:9, :] += jnp.sum(cot_v[at_rows, :].astype(f32) * branch, axis=0, keepdims=True)
+
+    row_parts(finish)
+    save(out_v, o_out)
+    save(vec, o_vec)
+
+    for a in range(7):
+        work.finish(a)
+    for k in range(1, rows_n):
+        cond_copy(k).wait_send()
+        sum_copy(k).wait_send()
+    for k in range(1, cols_n):
+        mod_copy(k).wait_send()
+    other.wait_send()
+
+    @pl.loop(0, 4 * depth)
+    def _(h):
+        swap_kv(0, h).wait_send()
+        swap_kv(1, h).wait_send()
+
+    for s in range(2 * depth, 3 * depth):
+        weight_save(s).wait()
+    for copy in saves:
+        copy.wait()
+
+
+def forward(lat, cot, cond, ada, bias, blocks, collective_id):
+    rows, cols = lax.axis_size("row"), lax.axis_size("col")
+    depth = cols // 2
+    tokens, width = lat.shape
+    heads = width // HEAD_DIM
+    lanes = 1152
+    hc6 = ada.shape[1]
+    shape = jax.ShapeDtypeStruct
+    head = shape((heads, tokens, HEAD_DIM), bf16)
+    token = shape((tokens, width), bf16)
+    outs = [shape((rows * b.shape[0], cols * b.shape[1]), bf16) for b in blocks] + [
+        shape((3, depth, width, lanes), bf16), token, token, token, head, head, head, head, head,
+        shape((heads, 1, tokens), f32), shape((depth, tokens, 384), bf16), token, shape((tokens, width), f32), token,
+        shape((depth, tokens, lanes), bf16), shape((depth, tokens, lanes), bf16), token, shape((VECS, width), f32)]
+    dma, vm = pltpu.SemaphoreType.DMA, pltpu.VMEM
+    t16, h16 = vm((tokens, width), bf16), vm((heads, tokens, HEAD_DIM), bf16)
+    drows = ada.shape[0]
+    scratch = [
+        t16, t16, h16, h16, h16, h16, h16, vm((heads, 1, tokens), f32), vm((4, HEAD_DIM, tokens), f32),
+        vm((depth, tokens, 384), bf16), t16, vm((tokens, width), f32), t16, vm((depth, tokens, lanes), bf16),
+        vm((depth, tokens, lanes), bf16), vm((tokens, width), f32), vm((depth, width, lanes), bf16), vm((2, width // 2, 256), bf16),
+        t16, t16, vm((VECS, width), f32), vm((rows, 8, drows), f32), vm((rows, 8, drows), f32), vm((rows, 8, hc6), f32),
+        vm((rows, 8, hc6), f32), vm((cols, 8, hc6), f32), vm((cols, 8, hc6), f32)]
+    scratch += Gather.scratch(len(blocks), depth)
+    scratch += [dma((2, 2)), dma((2, rows)), dma((2, rows)), dma((2, cols)), dma((2,)), dma((2, 2, heads)), dma((2, 3)), dma((32,)),
+                dma((3 * depth,))]
+    vmem = pl.BlockSpec(memory_space=pltpu.VMEM)
+    got = pl.pallas_call(
+        forward_kernel,
+        out_shape=outs,
+        in_specs=[ANY, ANY, vmem, vmem, vmem] + [ANY] * len(blocks),
+        out_specs=[ANY] * len(outs),
+        scratch_shapes=scratch,
+        compiler_params=pltpu.CompilerParams(collective_id=collective_id, has_side_effects=True, vmem_limit_bytes=62 * 2**20),
+        name="forward",
+    )(lat, cot, cond, ada, bias, *blocks)
+    return got[len(blocks):]
+
+
+class ZScatter(Scatter):
+    def __init__(self, place, sources, outs, bufs, sems, parts):
+        super().__init__(place, sources, outs, bufs, sems)
+        self.parts = parts
+
+    def block(self, a, p, q, z, h):
+        y, x = jnp.where(h == 0, p, q), jnp.where(h == 0, q, p)
+        rows, lanes = self.outs[a].shape
+        g, first, depth_rows = self.parts[a]
+        r = 2 * y + h
+        if first is None:
+            spot, lane = r * depth_rows + x * rows, 1024
+        else:
+            spot, lane = r * depth_rows, first + x * lanes
+        return self.ins[g].at[z, pl.ds(pl.multiple_of(spot, 16), rows), pl.ds(pl.multiple_of(lane, 128) if first is not None else lane, lanes)]
+
+
+def zscatter_kernel(groups, parts, *refs):
+    count = sum(groups)
+    ins, outs = refs[:3], refs[3:3 + count]
+    bufs, sems = Scatter.split(refs[3 + count:], count)
+    place = Place()
+    greet(place.partners())
+    work = ZScatter(place, ins, outs, bufs, sems, parts)
+    chunks = chunk_list(groups, place.depth)
+    for s in range(len(chunks) + 4):
+        for n in range(5):
+            if 0 <= s - n < len(chunks):
+                for a, t in chunks[s - n]:
+                    work.stage(a, t, n)
+    for a in range(count):
+        work.finish(a)
+
+
+def zscatter_all(fulls, shapes, groups, parts, collective_id):
+    cols = lax.axis_size("col")
+    return pl.pallas_call(
+        functools.partial(zscatter_kernel, groups, parts),
+        out_shape=[jax.ShapeDtypeStruct(s, jnp.float32) for s in shapes],
+        in_specs=[ANY] * len(fulls),
+        out_specs=[pl.BlockSpec(memory_space=pltpu.VMEM)] * len(shapes),
+        scratch_shapes=Scatter.scratch(shapes, cols // 2),
+        compiler_params=pltpu.CompilerParams(collective_id=collective_id, has_side_effects=True, vmem_limit_bytes=58 * 2**20),
+        name="scatter_grads",
+    )(*fulls)
+
+
 class Plan:
     def __init__(self, latents, condition, qkv_weight, fc1_weight):
         self.rows, self.cols = lax.axis_size("row"), lax.axis_size("col")
@@ -566,9 +1041,157 @@
     return value_grad, jnp.sum(rows_grad, axis=0), jnp.sum(rows_grad * normal, axis=0)
 
 
+def shards_near(plan, latents, condition, ada_weight, ada_bias, qkv_weight, qv_bias, proj_weight, proj_bias,
+                fc1_weight, fc1_bias, fc2_weight, fc2_bias, cotangent):
+    row, col = lax.axis_index("row"), lax.axis_index("col")
+    rows, cols, width, tokens = plan.rows, plan.cols, plan.width, plan.tokens
+    depth, hc, fc = plan.depth_rows, plan.head_cols, plan.ff_cols
+    zs = cols // 2
+    heads = cols * hc // HEAD_DIM
+    groups = rows * plan.lats
+    qkv_flat = qkv_weight.reshape(depth, 3 * hc)
+    proj_t, fc2_t = proj_weight.T, fc2_weight.T
+    left_a = plan.fold(jnp.concatenate([qkv_flat[:, plan.q_main:], proj_t[:, plan.p_main:]], axis=1))
+    blocks = [qkv_flat[:, :plan.q_main], proj_t[:, :plan.p_main], left_a,
+              fc1_weight[:, :plan.f_main], plan.fold(fc1_weight[:, plan.f_main:]),
+              fc2_t[:, :plan.f_main], plan.fold(fc2_t[:, plan.f_main:])]
+    cond8 = jnp.pad(condition.astype(f32), ((0, 8 - plan.lats), (0, 0)))
+    ada_flat = ada_weight.reshape(depth, 6 * hc)
+    line = jnp.concatenate([fc1_bias, proj_bias, fc2_bias]).astype(f32).reshape(1, 6 * hc)
+    tail = jnp.pad(qv_bias.astype(f32).reshape(1, 2 * hc), ((0, 0), (0, 4 * hc)))
+    bias = jnp.concatenate([jnp.broadcast_to(ada_bias.astype(f32).reshape(1, 6 * hc), (plan.lats, 6 * hc)), line, tail,
+                            jnp.zeros((8 - plan.lats - 2, 6 * hc), f32)], axis=0)
+    (w, grad_out, values, normed_one, query, key, value, key_two, value_two, lse, att, branch_a, middle, normed_two,
+     hidden, slope, out, vec) = forward(latents, cotangent, cond8, ada_flat, bias, blocks, 0)
+    output = plan.swap(out)
+    values, grad_out, branch_a = values.astype(f32), grad_out.astype(f32), branch_a.astype(f32)
+    shift_one, scale_one, gate_one, shift_two, scale_two, gate_two = (vec[k:k + 1] for k in range(6))
+    gate_two_grad = vec[8]
+    normal_one, inverse_one = layer_norm(values)
+    normal_two, inverse_two = layer_norm(middle)
+    cond_all = lax.all_gather(condition, "row", axis=0, tiled=True).astype(f32)
+    cond_act = jax.nn.silu(cond_all).astype(bf16)
+    cond_mine = lax.dynamic_slice(cond_act, (0, row * depth), (groups, depth))
+
+    def to_heads(flat):
+        return flat.reshape(tokens, heads, HEAD_DIM).transpose(1, 0, 2)
+
+    def from_heads(value):
+        return value.transpose(1, 0, 2).reshape(tokens, cols, hc)
+
+    m_grad = grad_out * gate_two
+    fc2_bias_part = jnp.sum(m_grad, axis=0)
+    m_low = m_grad.astype(bf16)
+    fc2_grad = jnp.stack([tn(m_low, hidden[z]).astype(bf16) for z in range(zs)])
+    pre_grad = [nn(m_low, w[2, z]) * slope[z] for z in range(zs)]
+    fc1_bias_part = jnp.stack([jnp.sum(u, axis=0) for u in pre_grad])
+    pre_low = [u.astype(bf16) for u in pre_grad]
+    fc1_grad = jnp.stack([tn(normed_two, u).astype(bf16) for u in pre_low])
+    normed_two_grad = sum(nt(u, w[1, z]) for z, u in enumerate(pre_low))
+    middle_part, shift_two_grad, scale_two_grad = norm_back(normed_two_grad, normal_two, inverse_two, scale_two)
+    middle_grad = grad_out + middle_part
+    gate_one_grad = jnp.sum(middle_grad * branch_a, axis=0)
+    a_grad = middle_grad * gate_one
+    proj_bias_part = jnp.sum(a_grad, axis=0)
+    a_low = a_grad.astype(bf16)
+    qm, pm, ql = 2 * plan.q_main, 2 * plan.p_main, plan.q_left
+
+    att_grads, proj_grads = [], []
+    for z in range(zs):
+        got = nn(a_low, w[0, z, :, qm:])
+        for j in range(2):
+            att_grads.append(jnp.concatenate(
+                [got[:, j * plan.p_main:(j + 1) * plan.p_main], got[:, pm + 64 * j + ql:pm + 64 * (j + 1)]], axis=1))
+        proj_grads.append(tn(a_low, att[z]))
+    att_grad = to_heads(jnp.concatenate(att_grads, axis=1).astype(bf16))
+    att_pairs = []
+    for z in range(zs):
+        for j in range(2):
+            att_pairs.append(jnp.concatenate(
+                [att[z][:, j * plan.p_main:(j + 1) * plan.p_main], att[z][:, pm + 64 * j + ql:pm + 64 * (j + 1)]], axis=1))
+    att_heads = to_heads(jnp.concatenate(att_pairs, axis=1))
+    query_grad, key_grad, value_grad = attend_back(query, key, value, key_two, value_two, lse, att_heads, att_grad, 3)
+    q_bias_part, v_bias_part = jnp.sum(query_grad, axis=1), jnp.sum(value_grad, axis=1)
+    qkv_low = jnp.concatenate([from_heads(g.astype(bf16)) for g in (query_grad, key_grad, value_grad)], axis=2)
+    att_wgrads, normed_one_grad = [], 0.0
+    for z in range(zs):
+        pair = qkv_low[:, 2 * z:2 * z + 2]
+        main = pair[:, :, :plan.q_main].reshape(tokens, qm)
+        left = jnp.pad(pair[:, :, plan.q_main:], ((0, 0), (0, 0), (0, 64 - ql))).reshape(tokens, 128)
+        both = jnp.concatenate([main, left], axis=1)
+        normed_one_grad = normed_one_grad + nt(main, w[0, z, :, :qm]) + nt(left, w[0, z, :, qm + pm:])
+        got = tn(normed_one, both)
+        att_wgrads.append(jnp.concatenate(
+            [got[:, :qm], proj_grads[z][:, :pm], got[:, qm:] + proj_grads[z][:, pm:]], axis=1).astype(bf16))
+    att_wgrad = jnp.stack(att_wgrads)
+    half = depth // 2
+    shapes = [(depth, plan.f_main), (half, 128), (depth, plan.f_main), (half, 128), (depth, plan.q_main), (depth, plan.p_main), (half, 128)]
+    parts = [(0, 0, depth), (0, None, depth), (1, 0, depth), (1, None, depth), (2, 0, depth), (2, qm, depth), (2, None, depth)]
+    sums = zscatter_all([fc2_grad, fc1_grad, att_wgrad], shapes, (2, 2, 3), parts, 1)
+    lefts = jnp.stack([sums[1], sums[3], sums[6]])
+    x = col % 2
+    give = jnp.where(x == 0, lefts[:, :, 64:], lefts[:, :, :64])
+    keep = jnp.where(x == 0, lefts[:, :, :64], lefts[:, :, 64:])
+    got = lax.ppermute(give, "col", [(i, i + 1 - 2 * (i % 2)) for i in range(cols)])
+    lefts = jnp.where(x == 0, jnp.concatenate([keep, got], axis=1), jnp.concatenate([got, keep], axis=1))
+    fc2_sum = jnp.concatenate([sums[0], lefts[0]], axis=1)
+    fc1_sum = jnp.concatenate([sums[2], lefts[1]], axis=1)
+    qkv_sum = jnp.concatenate([sums[4], lefts[2][:, :ql]], axis=1)
+    proj_sum = jnp.concatenate([sums[5], lefts[2][:, ql:]], axis=1)
+    input_part, shift_one_grad, scale_one_grad = norm_back(normed_one_grad, normal_one, inverse_one, scale_one)
+    latents_grad = plan.swap((middle_grad + input_part).astype(bf16)).astype(f32)
+    mod_grad = jnp.stack(
+        [shift_one_grad, scale_one_grad, gate_one_grad, shift_two_grad, scale_two_grad, gate_two_grad], axis=0)
+    fc1_flat = jnp.concatenate([fc1_bias_part[:, :1024].reshape(-1), fc1_bias_part[:, 1024:].reshape(-1)])
+    fc1_parts = [fc1_flat[:cols * plan.f_main], fc1_flat[cols * plan.f_main:]]
+    return finish(plan, condition, cond_mine, ada_flat, mod_grad,
+                  [proj_bias_part, fc2_bias_part, q_bias_part, v_bias_part] + fc1_parts,
+                  (output, latents_grad, qkv_sum, proj_sum, fc1_sum, fc2_sum))
+
+
+def finish(plan, condition, cond_mine, ada_flat, mod_grad, bias_parts, done):
+    output, latents_grad, qkv_sum, proj_sum, fc1_sum, fc2_sum = done
+    row, col = lax.axis_index("row"), lax.axis_index("col")
+    rows, cols, width, depth, hc = plan.rows, plan.cols, plan.width, plan.depth_rows, plan.head_cols
+    groups = rows * plan.lats
+    mod_grad = lax.all_gather(mod_grad, ("row", "col"), axis=0, tiled=False)
+    if plan.near:
+        mod_grad = mod_grad.reshape(rows // 2, 2, cols // 2, 2, 6, width).sum(axis=1).transpose(0, 2, 1, 3, 4)
+    else:
+        mod_grad = mod_grad.reshape(rows, cols // plan.share, plan.share, 6, width).sum(axis=2)
+    mod_grad = mod_grad.reshape(groups, 6, width)
+    mod_mine = lax.dynamic_slice(mod_grad, (0, 0, col * hc), (groups, 6, hc))
+    ada_bsum = jnp.sum(mod_mine, axis=0)
+    mod_low = mod_mine.astype(bf16).reshape(groups, 6 * hc)
+    ada_wsum = tn(cond_mine, mod_low).reshape(depth, 6, hc)
+    cond_part = lax.dynamic_update_slice(jnp.zeros((groups, width), f32), nt(mod_low, ada_flat), (0, row * depth))
+    parts = [cond_part] + bias_parts
+    totals = lax.psum(jnp.concatenate([part.reshape(-1) for part in parts]), ("row", "col"))
+    ends, spot = [], 0
+    for part in parts:
+        ends.append(totals[spot:spot + part.size])
+        spot += part.size
+
+    def mine(flat, size):
+        return lax.dynamic_slice(flat, (col * size,), (size,))
+
+    cond_summed = lax.dynamic_slice(ends[0].reshape(groups, width), (row * plan.lats, 0), (plan.lats, width))
+    silu_value, silu_pull = jax.vjp(jax.nn.silu, condition.astype(f32))
+    condition_grad = silu_pull(cond_summed)[0]
+    proj_bsum, fc2_bsum = mine(ends[1], hc), mine(ends[2], hc)
+    qv_bsum = jnp.stack([mine(ends[3], hc), mine(ends[4], hc)], axis=0)
+    fc1_bsum = jnp.concatenate([mine(flat, flat.size // cols) for flat in ends[5:]])
+    return (
+        output, latents_grad, condition_grad, ada_wsum, ada_bsum, qkv_sum.reshape(depth, 3, hc), qv_bsum,
+        proj_sum.T, proj_bsum, fc1_sum, fc1_bsum, fc2_sum.T, fc2_bsum)
+
+
 def shards(latents, condition, ada_weight, ada_bias, qkv_weight, qv_bias, proj_weight, proj_bias,
            fc1_weight, fc1_bias, fc2_weight, fc2_bias, cotangent):
     plan = Plan(latents, condition, qkv_weight, fc1_weight)
+    if plan.near:
+        return shards_near(plan, latents, condition, ada_weight, ada_bias, qkv_weight, qv_bias, proj_weight, proj_bias,
+                           fc1_weight, fc1_bias, fc2_weight, fc2_bias, cotangent)
     row, col = lax.axis_index("row"), lax.axis_index("col")
     rows, cols, width, tokens = plan.rows, plan.cols, plan.width, plan.tokens
     depth, hc, fc = plan.depth_rows, plan.head_cols, plan.ff_cols
@@ -711,36 +1334,9 @@
 
     mod_grad = jnp.stack(
         [shift_one_grad, scale_one_grad, gate_one_grad, shift_two_grad, scale_two_grad, gate_two_grad], axis=0)
-    mod_grad = lax.all_gather(mod_grad, ("row", "col"), axis=0, tiled=False)
-    if plan.near:
-        mod_grad = mod_grad.reshape(rows // 2, 2, cols // 2, 2, 6, width).sum(axis=1).transpose(0, 2, 1, 3, 4)
-    else:
-        mod_grad = mod_grad.reshape(rows, cols // plan.share, plan.share, 6, width).sum(axis=2)
-    mod_grad = mod_grad.reshape(groups, 6, width)
-    mod_mine = lax.dynamic_slice(mod_grad, (0, 0, col * hc), (groups, 6, hc))
-    ada_bsum = jnp.sum(mod_mine, axis=0)
-    mod_low = mod_mine.astype(bf16).reshape(groups, 6 * hc)
-    ada_wsum = tn(cond_mine, mod_low).reshape(depth, 6, hc)
-    cond_part = lax.dynamic_update_slice(jnp.zeros((groups, width), f32), nt(mod_low, ada_flat), (0, row * depth))
-    parts = [cond_part, proj_bias_part, fc2_bias_part, q_bias_part, v_bias_part] + fc1_bias_parts
-    totals = lax.psum(jnp.concatenate([part.reshape(-1) for part in parts]), ("row", "col"))
-    ends, spot = [], 0
-    for part in parts:
-        ends.append(totals[spot:spot + part.size])
-        spot += part.size
-
-    def mine(flat, size):
-        return lax.dynamic_slice(flat, (col * size,), (size,))
-
-    cond_summed = lax.dynamic_slice(ends[0].reshape(groups, width), (row * plan.lats, 0), (plan.lats, width))
-    silu_value, silu_pull = jax.vjp(jax.nn.silu, condition.astype(f32))
-    condition_grad = silu_pull(cond_summed)[0]
-    proj_bsum, fc2_bsum = mine(ends[1], hc), mine(ends[2], hc)
-    qv_bsum = jnp.stack([mine(ends[3], hc), mine(ends[4], hc)], axis=0)
-    fc1_bsum = jnp.concatenate([mine(flat, flat.size // cols) for flat in ends[5:]])
-    return (
-        output, latents_grad, condition_grad, ada_wsum, ada_bsum, qkv_sum.reshape(depth, 3, hc), qv_bsum,
-        proj_sum.T, proj_bsum, fc1_sum, fc1_bsum, fc2_sum.T, fc2_bsum)
+    return finish(plan, condition, cond_mine, ada_flat, mod_grad,
+                  [proj_bias_part, fc2_bias_part, q_bias_part, v_bias_part] + fc1_bias_parts,
+                  (output, latents_grad, qkv_sum, proj_sum, fc1_sum, fc2_sum))
 
 
 def solution(mesh):

time: 899 us -> 883 us (0.982)
  waiting for transfers between devices: 0.03 us -> 100 us
  local copies, waits for them, and re-layouts: 184 us -> 101 us
  blocking collectives: 133 us -> 83.6 us
  other arithmetic: 35.2 us -> 72.8 us
  starting transfers between devices: 33.1 us -> 5.27 us
  Pallas kernels: 361 us -> 384 us
  matrix products: 128 us -> 114 us
    psum x1, waiting for transfers between devices: 0.01 us -> 100 us  [finish(): lax.psum(jnp.concatenate([part.reshape(-1) for part in parts]), ('row', '...]
    reshape x25 -> x7, local copies, waits for them, and re-layouts: 82.6 us -> 7.45 us  [the longest x3 4.28 us: finish(): part.reshape(-1)]
    all_gather x3 -> x2, blocking collectives: 120 us -> 83.6 us  [the longest x1 78.4 us: finish(): mod_grad = lax.all_gather(mod_grad, ('row', 'col'), axis=0, tiled=False)]
    ppermute x4 -> x2, starting transfers between devices: 33.1 us -> 3.97 us  [swap(): lax.ppermute(value, ('row', 'col'), self.swap_pairs())]
    pallas_call x3 -> x2, Pallas kernels: 324 us -> 348 us  [the longest x1 197 us: forward(): pl.pallas_call(forward_kernel, out_shape=outs, in_specs=[ANY, ANY, vmem,...]
    another operation x1 -> x6, other arithmetic: 0.58 us -> 23.2 us  [the longest x1 12 us: shards_near(): fc1_grad = jnp.stack([tn(normed_two, u).astype(bf16) for u in pre_low])]
    transpose x8 -> x1, local copies, waits for them, and re-layouts: 20.5 us -> 2 us  [finish(): mod_grad.reshape(rows // 2, 2, cols // 2, 2, 6, width).sum(axis=1)]
    unnamed x116 -> x188, local copies, waits for them, and re-layouts: 11.1 us -> 27.4 us
  transfers between devices with their start and end apart: 5 -> 4, of which waited for: 0 -> 1; matrix products, arithmetic and copies ran while one was open for 27% -> 9% of each run, Pallas kernels for 36% -> 0%
where the time goes in v2:
time: 883 us; the launch traced here: 877 us
  Pallas kernels  384 us (43%)
  matrix products  114 us (13%)
  local copies, waits for them, and re-layouts  101 us (11%)
  waiting for transfers between devices  100 us (11%)
  blocking collectives  83.6 us (9%)
  other arithmetic  72.8 us (8%)
  between operations  15.4 us (2%)
    pallas_call x1, Pallas kernels, forward(): pl.pallas_call(forward_kernel, out_shape=outs, in_specs=[ANY, ANY, vmem,...  197 us
    pallas_call x1, Pallas kernels, zscatter_all(): pl.pallas_call(functools.partial(zscatter_kernel, groups, parts), out_sha...  150 us
    psum x1, waiting for transfers between devices, finish(): lax.psum(jnp.concatenate([part.reshape(-1) for part in parts]), ('row', '...  100 us
    all_gather x1, blocking collectives, finish(): mod_grad = lax.all_gather(mod_grad, ('row', 'col'), axis=0, tiled=False)  78.4 us
    dot_general x13, matrix products, nt(): lax.dot_general(a, b, (((1,), (1,)), ((), ())), preferred_element_type=f32)  46.4 us
    dot_general x17, matrix products, tn(): lax.dot_general(a, b, (((0,), (0,)), ((), ())), preferred_element_type=f32)  39.2 us
    pallas_call x1, Pallas kernels, attend_back(): pl.pallas_call(attend_back_kernel, out_shape=[jax.ShapeDtypeStruct(q.shap...  36.4 us
    dot_general x8, matrix products, nn(): lax.dot_general(a, b, (((1,), (0,)), ((), ())), preferred_element_type=f32)  28.8 us
  transfers between devices with their start and end apart: 4, of which 1 were waited for; matrix products, arithmetic and copies ran while one was open for 9% of the time, Pallas kernels for 0%

profile of v2, /device:TPU:0, one launch (start us, length us, event | category | flops | bytes accessed | tf_op | source)
XLA Modules:
  0.0 876.9 jit_solution(18173367208313974637)
XLA Ops:
  10.9 1.7 slice.542.refs_10_
  13.4 1.7 slice.424.refs_8_
  21.4 197.1 %forward.1 = (bf16[1152,3072]{1,0:T(8,128)(2,1)}, bf16[1152,1024]{1,0:T(8,128)(2,1)}, bf16[576,1024]{1,0:T(8,128)(2,1)}, bf16[1152,4096]{1,0:T(8,128)(2,1)}, bf1...) custom-call(bf16[512,1152]{1,0:T(8,128)(2,1)} %refs_0_.1, ...), custom_call_target="tpu_custom_call" | custom-call | tf_op jit(solution)/shard_map/forward/pallas_call | solution.py:885
  218.5 2.1 add_reduce_fusion
  220.7 5.0 fusion.156
  225.7 5.6 fusion.155
  231.3 5.2 fusion.154
  236.6 5.3 fusion.153
  241.8 5.2 fusion.24
  249.5 4.1 convolution_add_fusion.6
  253.6 4.0 convolution_add_fusion.5
  257.6 4.9 multiply_reduce_fusion
  262.5 2.7 multiply_reduce_fusion.4
  265.4 1.9 convolution_convert_fusion.8
  267.3 1.9 convolution_convert_fusion.9
  269.2 2.0 convolution_convert_fusion.10
  271.2 1.9 convolution_convert_fusion.11
  279.5 2.1 fusion.137
  281.6 2.0 fusion.138
  293.8 3.6 copy.92
  297.4 3.9 concatenate.142
  301.3 2.4 copy.90
  303.7 3.5 copy.91
  307.3 36.4 %attend_back.1 = (f32[16,512,72]{2,1,0:T(8,128)}, f32[16,512,72]{2,1,0:T(8,128)}, f32[16,512,72]{2,1,0:T(8,128)}) custom-call(bf16[16,512,72]{2,1,0:T(8,128)(2,1)} %get-tuple-element.48.q_ref, bf16[16,512,72]{2,1,0:T(8,128)(2,1)} %get-tuple-element.49.k_ref, bf16[16,512,72]{2,1,0:T(8,128)(2,1)} %get-tuple-element.50.v_ref, ...), custom_call_target="tpu_custom_call" | custom-call | tf_op jit(solution)/shard_map/attend_back/pallas_call | solution.py:462
  343.7 10.5 %fusion.141 = (f32[16,72]{1,0:T(8,128)}, bf16[512,16,72]{2,0,1:T(8,128)(2,1)}, bf16[512,16,72]{2,0,1:T(8,128)(2,1)}, f32[16,72]{1,0:T(8,128)}) fusion(f32[16,512,72]{2,1,0:T(8,128)} %get-tuple-element.57, f32[16,512,72]{2,1,0:T(8,128)} %get-tuple-element.55), kind=kLoop, calls=%fused_computation.258 | loop fusion | flops 2356992 | bytes 7087104 | tf_op jit(solution)/shard_map/reduce_sum | solution.py:1114
  354.2 3.7 copy.93
  357.9 3.7 copy.95
  361.5 3.9 convert_bitcast_fusion.1
  365.4 3.7 copy.94
  370.2 3.7 pad_maximum_fusion.6
  393.7 3.2 fusion.7
  396.9 3.3 fusion.6
  400.2 3.5 fusion.5
  403.7 3.2 fusion.4
  406.9 3.4 fusion
  410.3 3.3 fusion.1
  413.5 3.3 fusion.2
  416.8 3.2 fusion.3
  420.0 12.0 %pad_maximum_fusion.1.refs_1_ = bf16[4,1152,1152]{2,1,0:T(8,128)(2,1)} fusion(bf16[1,1152,1152]{2,1,0:T(8,128)(2,1)} %fusion.7, bf16[1,1152,1152]{2,1,0:T(8,128)(2,1)} %fusion.6, bf16[1,1152,1152]{2,1,0:T(8,128)(2,1)} %fusion.5, bf16[1,1152,1152]{2,1,0:T(8,128)(2,1)} %fusion.4), kind=kLoop, calls=%fused_computation.1 | loop fusion | flops 15925248 | bytes 21233664 | tf_op jit(solution)/shard_map/stack | solution.py:1089
  432.1 5.6 pad_maximum_fusion.refs_0_
  439.3 4.1 maximum_maximum_fusion.refs_2_
  443.4 150.4 %scatter_grads.1 = (f32[288,512]{1,0:T(8,128)}, f32[144,128]{1,0:T(8,128)}, f32[288,512]{1,0:T(8,128)}, f32[144,128]{1,0:T(8,128)}, f32[288,384]{1,0:T(8,128)}, /*index=5*/f32[288,128]{1,0:T(8,128)}, f32[144,128]{1,0:T(8,128)}) custom-call(bf16[4,1152,1152]{2,1,0:T(8,128)(2,1)} %pad_maximum_fusion.refs_0_, bf16[4,1152,1152]{2,1,0:T(8,128)(2,1)} %pad_maximum_fusion.1.refs_1_, ...), custom_call_target="tpu_custom_call" | custom-call | tf_op jit(solution)/shard_map/scatter_grads/pallas_call | solution.py:933
  597.0 4.1 fusion.52
  601.0 4.2 fusion.50
  605.2 4.2 fusion.48
  609.4 4.2 fusion.46
  616.6 2.5 fusion.8
  619.1 1.6 fusion.9
  622.4 4.1 fusion.40
  631.0 78.4 %all-gather.1 = f32[32,6,1152]{2,1,0:T(8,128)} all-gather(f32[1,6,1152]{2,1,0:T(8,128)} %bitcast.296), channel_id=2, replica_groups=mesh['row'=4,'col'=8] {'row','col'}, dimensions={0}, use_global_device_ids=true | all-gather | bytes 912384 | tf_op jit(solution)/shard_map/all_gather | solution.py:1157
  709.3 2.2 reduce_sum.220
  711.6 2.0 copy.96
  713.6 1.9 reshape.426
  717.1 1.9 convolution_bitcast_fusion
  721.1 1.5 reshape.427
  736.2 3.5 fusion.39
  739.7 2.1 collective-permute-start.1
  741.8 1.9 collective-permute-start
  744.0 5.2 all-gather.2
  750.7 1.6 dynamic-slice_reduce_fusion
  752.3 100.1 %all-reduce.8.cloned.1.call-done = f32[27648]{0:T(1024)} async-done(((f32[27648]{0:T(1024)}), f32[27648]{0:T(1024)}) %all-reduce.8.cloned.1.call-update) | async-done | bytes 110608 | tf_op jit(solution)/shard_map/psum | solution.py:1169
  863.2 2.0 maximum_bitcast_fusion
  865.2 2.0 pad_maximum_fusion.7
  867.2 1.6 convert_element_type.184
  (313 shorter events, 95.1 us)
Async XLA Ops:
  7.2 10.6 %copy-start.20 = (bf16[288,6,144]{0,2,1:T(8,128)(2,1)S(1)}, bf16[288,6,144]{0,2,1:T(8,128)(2,1)}, u32[]{:S(2)}) copy-start(bf16[288,6,144]{0,2,1:T(8,128)(2,1)} %param.15) | copy-start | bytes 1492996
  7.2 845.2 %all-reduce.8.cloned.1.call-start = ((), (), s32[]{:S(2)}) async-start(), calls=%async_computation | async-start | bytes 221184 | tf_op jit(solution)/shard_map/psum | solution.py:1169
  9.1 9.8 %slice-start = ((bf16[288,576]{1,0:T(8,128)(2,1)}), bf16[288,64]{1,0:T(8,128)(2,1)S(1)}, s32[]{:S(2)}) async-start(bf16[288,576]{1,0:T(8,128)(2,1)} %param.21), calls=%async_computation.1 | async-start | bytes 147456 | tf_op jit(solution)/shard_map/slice | solution.py:1056
  9.1 10.6 %copy-start.64 = (bf16[6,144]{1,0:T(8,128)(2,1)S(1)}, bf16[6,144]{1,0:T(8,128)(2,1)}, u32[]{:S(2)}) copy-start(bf16[6,144]{1,0:T(8,128)(2,1)} %param.16) | copy-start | bytes 5188
  9.1 10.7 %copy-start.65 = (bf16[576]{0:T(1024)(128)(2,1)S(1)}, bf16[576]{0:T(1024)(128)(2,1)}, u32[]{:S(2)}) copy-start(bf16[576]{0:T(1024)(128)(2,1)} %param.22) | copy-start | bytes 3460
  9.1 10.7 %copy-start.69 = (bf16[144]{0:T(256)(128)(2,1)S(1)}, bf16[144]{0:T(256)(128)(2,1)}, u32[]{:S(2)}) copy-start(bf16[144]{0:T(256)(128)(2,1)} %param.20) | copy-start | bytes 868
  9.1 10.7 %copy-start.70 = (bf16[144]{0:T(256)(128)(2,1)S(1)}, bf16[144]{0:T(256)(128)(2,1)}, u32[]{:S(2)}) copy-start(bf16[144]{0:T(256)(128)(2,1)} %param.24) | copy-start | bytes 868
  9.1 10.7 %copy-start.66 = (bf16[2,144]{1,0:T(2,128)(2,1)S(1)}, bf16[2,144]{1,0:T(2,128)(2,1)}, u32[]{:S(2)}) copy-start(bf16[2,144]{1,0:T(2,128)(2,1)} %param.18) | copy-start | bytes 1732
  9.1 10.8 %copy-start.49 = (bf16[4,1152]{1,0:T(4,128)(2,1)S(1)}, bf16[4,1152]{1,0:T(4,128)(2,1)}, u32[]{:S(2)}) copy-start(bf16[4,1152]{1,0:T(4,128)(2,1)} %param.14) | copy-start | bytes 27652
  220.7 5.0 copy-start.36
  220.7 5.0 copy-start.67
  225.7 16.1 %copy-start.74 = (bf16[512,1152]{1,0:T(8,128)(2,1)}, bf16[512,1152]{1,0:T(8,128)(2,1)S(1)}, u32[]{:S(2)}) copy-start(bf16[512,1152]{1,0:T(8,128)(2,1)S(1)} %get-tuple-element.175) | copy-start | bytes 3538948
  241.8 5.2 copy-start.1
  249.5 4.1 copy-start.77
  253.6 4.0 copy-start.57
  253.6 4.0 copy-start.72
  257.6 4.9 copy-start.2
  257.6 4.9 copy-start.38
  269.2 3.9 copy-start.8
  370.1 4.6 copy-start
  373.8 6.4 copy-start.16
  373.9 12.3 %copy-start.14 = (bf16[512,2,384]{0,2,1:T(8,128)(2,1)}, bf16[512,2,384]{0,2,1:T(8,128)(2,1)S(1)}, u32[]{:S(2)}) copy-start(bf16[512,2,384]{0,2,1:T(8,128)(2,1)S(1)} %get-tuple-element.128) | copy-start | bytes 2359300
  373.9 16.1 %copy-start.12 = (bf16[512,2,384]{0,2,1:T(8,128)(2,1)}, bf16[512,2,384]{0,2,1:T(8,128)(2,1)S(1)}, u32[]{:S(2)}) copy-start(bf16[512,2,384]{0,2,1:T(8,128)(2,1)S(1)} %get-tuple-element.130) | copy-start | bytes 2359300
  393.7 3.2 copy-start.78
  396.9 3.3 copy-start.76
  400.2 3.5 copy-start.75
  400.2 6.7 slice-start.1
  403.7 3.2 copy-start.37
  403.7 3.2 slice-start.2
  420.0 12.0 %copy-start.21 = (bf16[1,1152,1152]{2,1,0:T(8,128)(2,1)S(1)}, bf16[1,1152,1152]{2,1,0:T(8,128)(2,1)}, u32[]{:S(2)}) copy-start(bf16[1,1152,1152]{2,1,0:T(8,128)(2,1)} %fusion) | copy-start | bytes 7962628
  420.0 12.0 %copy-start.22 = (bf16[1,1152,1152]{2,1,0:T(8,128)(2,1)S(1)}, bf16[1,1152,1152]{2,1,0:T(8,128)(2,1)}, u32[]{:S(2)}) copy-start(bf16[1,1152,1152]{2,1,0:T(8,128)(2,1)} %fusion.1) | copy-start | bytes 7962628
  420.0 12.0 %copy-start.23 = (bf16[1,1152,1152]{2,1,0:T(8,128)(2,1)S(1)}, bf16[1,1152,1152]{2,1,0:T(8,128)(2,1)}, u32[]{:S(2)}) copy-start(bf16[1,1152,1152]{2,1,0:T(8,128)(2,1)} %fusion.2) | copy-start | bytes 7962628
  420.0 12.0 %copy-start.24 = (bf16[1,1152,1152]{2,1,0:T(8,128)(2,1)S(1)}, bf16[1,1152,1152]{2,1,0:T(8,128)(2,1)}, u32[]{:S(2)}) copy-start(bf16[1,1152,1152]{2,1,0:T(8,128)(2,1)} %fusion.3) | copy-start | bytes 7962628
  432.0 5.7 copy-start.4
  432.0 5.7 copy-start.5
  432.0 5.7 copy-start.6
  432.1 6.7 copy-start.7
  432.1 6.8 copy-start.28
  432.1 6.9 copy-start.29
  432.1 7.0 copy-start.39
  432.1 7.0 copy-start.40
  432.1 7.1 copy-start.41
  432.1 7.2 copy-start.42
  443.4 153.6 %copy-start.19 = (bf16[512,2,384]{0,2,1:T(8,128)(2,1)S(1)}, bf16[512,2,384]{0,2,1:T(8,128)(2,1)}, u32[]{:S(2)}) copy-start(bf16[512,2,384]{0,2,1:T(8,128)(2,1)} %copy-done.18) | copy-start | bytes 2359300
  595.7 5.3 copy-start.17
  595.7 263.2 %collective-permute-start.2 = (f32[3,144,64]{2,1,0:T(8,128)}, f32[3,144,64]{2,1,0:T(8,128)}, u32[]{:S(2)}, u32[]{:S(2)}) collective-permute-start(f32[3,144,64]{2,1,0:T(8,128)} %get-tuple-element.160), channel_id=1, source_target_pairs={{0,1},{1,0},{2,3},{3,2},{4,5},{5,4},{6,7},{7,6},{8,9},{9,8},{10,11... | collective-permute-start | bytes 331784 | tf_op jit(solution)/shard_map/ppermute | solution.py:1135
  601.0 4.2 copy-start.15
  605.2 4.2 copy-start.13
  609.4 5.8 copy-start.63
  609.4 5.8 copy-start.62
  609.4 6.4 copy-start.3
  613.6 2.9 copy-start.26
  613.6 2.9 copy-start.31
  616.1 6.3 copy-start.58
  616.5 5.8 copy-start.59
  622.4 5.4 copy-start.56
  622.4 5.9 copy-start.61
  622.4 6.5 copy-start.60
  736.2 7.5 copy-start.47
  736.2 7.8 copy-start.50
  739.7 119.2 %copy-start.43 = (f32[3,144,64]{2,1,0:T(8,128)S(1)}, f32[3,144,64]{2,1,0:T(8,128)}, u32[]{:S(2)}) copy-start(f32[3,144,64]{2,1,0:T(8,128)} %get-tuple-element.159) | copy-start | bytes 331780
  739.7 120.5 %copy-start.48 = (f32[288,128]{1,0:T(8,128)S(1)}, f32[288,128]{1,0:T(8,128)}, u32[]{:S(2)}) copy-start(f32[288,128]{1,0:T(8,128)} %get-tuple-element.66) | copy-start | bytes 442372
  739.7 127.5 %collective-permute-start.1 = (bf16[512,1152]{1,0:T(8,128)(2,1)}, bf16[512,1152]{1,0:T(8,128)(2,1)S(1)}, u32[]{:S(2)}, u32[]{:S(2)}) collective-permute-start(bf16[512,1152]{1,0:T(8,128)(2,1)} %fusion.39), channel_id=1, source_target_pairs={{0,0},{1,8},{2,2},{3,10},{4,4},{5,12},{6,6},{7,14},{8,1},{9,9},{10... | collective-permute-start | bytes 3538952 | tf_op jit(solution)/shard_map/ppermute | solution.py:986
  741.8 127.0 %collective-permute-start = (bf16[512,1152]{1,0:T(8,128)(2,1)}, bf16[512,1152]{1,0:T(8,128)(2,1)S(1)}, u32[]{:S(2)}, u32[]{:S(2)}) collective-permute-start(bf16[512,1152]{1,0:T(8,128)(2,1)} %get-tuple-element.41), channel_id=1, source_target_pairs={{0,0},{1,8},{2,2},{3,10},{4,4},{5,12},{6,6},{7,14},{8,1},{9,9},{10... | collective-permute-start | bytes 3538952 | tf_op jit(solution)/shard_map/ppermute | solution.py:986
  (22 other events, 33.5 us)
Sparse Core Ops, SparseCore 0:
  734.9 117.4 all-reduce.7

commit v3 on v2

v3 whole, which is shorter than its diff:
```python
import functools
import math
import jax
import jax.numpy as jnp
from jax import lax
from jax.experimental import pallas as pl
from jax.experimental.pallas import tpu as pltpu
from jax.sharding import PartitionSpec as P

HEAD_DIM = 72
SEQ = 1024
norm_eps = 1e-06
bf16, f32 = jnp.bfloat16, jnp.float32

MESH = pl.DeviceIdType.MESH
ANY = pl.BlockSpec(memory_space=pl.ANY)


class Place:
    def __init__(self):
        row, col = lax.axis_index("row"), lax.axis_index("col")
        self.row, self.col = row, col
        self.depth = lax.axis_size("col") // 2
        self.y, self.h = row // 2, row % 2
        self.z, self.x = col // 2, col % 2
        self.p = jnp.where(self.h == 0, self.y, self.x)
        self.q = jnp.where(self.h == 0, self.x, self.y)
        flip_x, flip_y = (row, col + 1 - 2 * self.x), (row + 2 - 4 * self.y, col)
        self.to_q = tuple(jnp.where(self.h == 0, a, b) for a, b in zip(flip_x, flip_y))
        self.to_p = tuple(jnp.where(self.h == 0, b, a) for a, b in zip(flip_x, flip_y))
        self.to_core = (row + 1 - 2 * self.h, col)

    def to_z(self, z):
        return (self.row, 2 * z + self.x)

    def diagonal(self):
        return (self.row + 1 - 2 * self.h, self.col + 1 - 2 * self.x)

    def yx(self, p, q):
        return jnp.where(self.h == 0, p, q), jnp.where(self.h == 0, q, p)

    def partners(self):
        near = [self.to_q, self.to_p, self.to_core]
        return near + [self.to_z((self.z + k) % self.depth) for k in range(1, self.depth)]


def greet(partners):
    barrier = pltpu.get_barrier_semaphore()
    for partner in partners:
        pl.semaphore_signal(barrier, inc=1, device_id=partner, device_id_type=MESH)
    pl.semaphore_wait(barrier, len(partners))


def block_at(ref, rows, lanes, r, c):
    return ref.at[pl.ds(pl.multiple_of(r * rows, 16), rows), pl.ds(pl.multiple_of(c * lanes, 128), lanes)]


class Gather:
    sems = (1, 2, 2, 4, 8)

    def __init__(self, place, ins, outs, sems):
        self.at, self.ins, self.outs = place, ins, outs
        self.local, self.zs, self.qs, self.ps, self.ks = sems

    @staticmethod
    def scratch(count, depth):
        dma = pltpu.SemaphoreType.DMA
        return [dma((count,)), dma((count, 2, depth)), dma((count, 2, depth)), dma((count, 2, depth, 2)), dma((count, 2, depth, 4))]

    def block(self, a, p, q, z, h=None):
        y, x = self.at.yx(p, q)
        rows, lanes = self.ins[a].shape
        h = self.at.h if h is None else h
        return block_at(self.outs[a], rows, lanes, 2 * y + h, 2 * z + x)

    def zc(self, t):
        return (self.at.z + self.at.depth - t) % self.at.depth

    def copy(self, src, dst, sems, index, to):
        return pltpu.make_async_remote_copy(
            src_ref=src, dst_ref=dst, send_sem=sems.at[(index[0], 0) + index[1:]], recv_sem=sems.at[(index[0], 1) + index[1:]],
            device_id=to, device_id_type=MESH)

    def own(self, a):
        return self.block(a, self.at.p, self.at.q, self.at.z)

    def c_local(self, a):
        return pltpu.make_async_copy(self.ins[a], self.own(a), self.local.at[a])

    def c_z(self, a, k):
        place = self.at
        return pltpu.make_async_remote_copy(
            src_ref=self.ins[a], dst_ref=self.own(a), send_sem=self.zs.at[a, 0, k], recv_sem=self.zs.at[a, 1, place.z],
            device_id=place.to_z((place.z + k) % place.depth), device_id_type=MESH)

    def r_z(self, a, t):
        place = self.at
        here = self.block(a, place.p, place.q, self.zc(t))
        return pltpu.make_async_remote_copy(
            src_ref=self.ins[a], dst_ref=here, send_sem=self.zs.at[a, 0, 0], recv_sem=self.zs.at[a, 1, self.zc(t)],
            device_id=place.to_z(place.z), device_id_type=MESH)

    def c_q(self, a, t):
        place = self.at
        spot = self.block(a, place.p, place.q, self.zc(t))
        return self.copy(self.ins[a] if t == 0 else spot, spot, self.qs, (a, self.zc(t)), place.to_q)

    def c_p(self, a, t, j):
        place = self.at
        spot = self.block(a, place.p, place.q if j == 0 else 1 - place.q, self.zc(t))
        return self.copy(self.ins[a] if t == 0 and j == 0 else spot, spot, self.ps, (a, self.zc(t), j), place.to_p)

    def c_k(self, a, t, j):
        place = self.at
        spot = self.block(a, place.p if j < 2 else 1 - place.p, place.q if j % 2 == 0 else 1 - place.q, self.zc(t))
        return self.copy(self.ins[a] if t == 0 and j == 0 else spot, spot, self.ks, (a, self.zc(t), j), place.to_core)

    def start(self, a):
        for k in range(1, self.at.depth):
            self.c_z(a, k).start()
        self.c_local(a).start()

    def stage(self, a, t, n):
        if n == 0:
            if t > 0:
                self.r_z(a, t).wait_recv()
            self.c_q(a, t).start()
            self.c_p(a, t, 0).start()
            self.c_k(a, t, 0).start()
        elif n == 1:
            self.c_q(a, t).wait_recv()
            self.c_p(a, t, 1).start()
            self.c_k(a, t, 1).start()
        elif n == 2:
            self.c_p(a, t, 0).wait_recv()
            self.c_k(a, t, 2).start()
        elif n == 3:
            self.c_p(a, t, 1).wait_recv()
            self.c_k(a, t, 3).start()
        else:
            if t == 0:
                self.c_local(a).wait()
            for j in range(4):
                self.c_k(a, t, j).wait_recv()

    def finish(self, a):
        for k in range(1, self.at.depth):
            self.c_z(a, k).wait_send()
        for t in range(self.at.depth):
            self.c_q(a, t).wait_send()
            for j in range(2):
                self.c_p(a, t, j).wait_send()
            for j in range(4):
                self.c_k(a, t, j).wait_send()


def nt(a, b):
    return lax.dot_general(a, b, (((1,), (1,)), ((), ())), preferred_element_type=f32)


def nn(a, b):
    return lax.dot_general(a, b, (((1,), (0,)), ((), ())), preferred_element_type=f32)


def tn(a, b):
    return lax.dot_general(a, b, (((0,), (0,)), ((), ())), preferred_element_type=f32)


SOFT = HEAD_DIM ** (-0.5) * math.log2(math.e)


VECS = 24


def softmax_head(q, k, k2):
    one, two = nt(k, q), nt(k2, q)
    top = jnp.maximum(jnp.max(one, axis=0, keepdims=True), jnp.max(two, axis=0, keepdims=True)) * SOFT
    one, two = jnp.exp2(one * SOFT - top), jnp.exp2(two * SOFT - top)
    total = jnp.sum(one, axis=0, keepdims=True) + jnp.sum(two, axis=0, keepdims=True)
    return one.astype(bf16), two.astype(bf16), total, top + jnp.log2(total)


def norm_rows(values):
    mean = jnp.mean(values, axis=-1, keepdims=True)
    centred = values - mean
    inverse = lax.rsqrt(jnp.mean(centred * centred, axis=-1, keepdims=True) + norm_eps)
    return centred * inverse, inverse


def gelu_both(u):
    c = math.sqrt(2.0 / math.pi)
    square = u * u
    inner = jnp.tanh(u * (c + (c * 0.044715) * square))
    half = 0.5 * (1.0 + inner)
    slope = half + (0.5 * u) * (1.0 - inner * inner) * (c + (3 * c * 0.044715) * square)
    return u * half, slope


class Swap:
    def __init__(self, place, src, dst, sems, i):
        self.stay = place.h == place.x
        self.local = pltpu.make_async_copy(src, dst, sems.at[i, 0])
        self.remote = pltpu.make_async_remote_copy(
            src_ref=src, dst_ref=dst, send_sem=sems.at[i, 0], recv_sem=sems.at[i, 1],
            device_id=place.diagonal(), device_id_type=MESH)

    def start(self):
        pl.when(self.stay)(self.local.start)
        pl.when(jnp.logical_not(self.stay))(self.remote.start)

    def wait(self):
        pl.when(self.stay)(self.local.wait)
        pl.when(jnp.logical_not(self.stay))(self.remote.wait)


def unfold_into(left, target):
    rows = target.shape[0] // 4
    half = rows // 2
    for r in range(4):
        tile = left[r * half:(r + 1) * half, :].astype(f32)
        target[r * rows:r * rows + half, :] = jnp.concatenate([tile[:, :64], tile[:, 128:192]], axis=1).astype(bf16)
        target[r * rows + half:(r + 1) * rows, :] = jnp.concatenate([tile[:, 64:128], tile[:, 192:]], axis=1).astype(bf16)


GROUPS = (3, 2, 2)


def forward_kernel(*refs):
    lat, cot, cond, ada, bias = refs[:5]
    blocks, refs = refs[5:12], refs[12:]
    fulls, refs = refs[:7], refs[7:]
    (o_w, o_cot, o_x, o_n1, o_q, o_k, o_v, o_k2, o_v2, o_lse, o_att, o_ba, o_mid, o_n2, o_hid, o_slo, o_out, o_vec, o_act), refs = refs[:19], refs[19:]
    (x_v, n1, q_v, k_v, v_v, k2_v, v2_v, lse_v, ot, att, ba, mid, n2, hid, slo, acc, wbuf, lbuf, out_v, cot_v, vec,
     c_send, c_recv, s_send, s_recv, m_own, m_oth), refs = refs[:27], refs[27:]
    ag_sems, (swap_sems, c_sems, s_sems, m_sems, o_sems, kv_sems, w_sems, save_sems, wsave_sems) = refs[:5], refs[5:]

    place = Place()
    depth, rows_n = place.depth, 4
    row, col = place.row, place.col
    cols_n = 2 * depth
    tokens, width = x_v.shape
    hc = width // cols_n
    drows = ada.shape[0]
    q_main, p_main = blocks[0].shape[1], blocks[1].shape[1]
    half = tokens // 2

    row_peers = [((row + k) % rows_n, col) for k in range(1, rows_n)]
    col_peers = [(row, (col + k) % cols_n) for k in range(1, cols_n)]
    greet(place.partners() + row_peers + col_peers + [place.diagonal()])

    def send(src, dst, s_sem, r_sem, to):
        return pltpu.make_async_remote_copy(
            src_ref=src, dst_ref=dst, send_sem=s_sem, recv_sem=r_sem, device_id=to, device_id_type=MESH)

    cond_value = cond[...]
    act = (cond_value / (1.0 + jnp.exp(-cond_value))).astype(bf16).astype(f32)
    for r in range(rows_n):
        c_send[r] = act[:, r * drows:(r + 1) * drows]

    def cond_copy(k):
        to = (row + k) % rows_n
        return send(c_send.at[to], c_recv.at[row], c_sems.at[0, k], c_sems.at[1, row], (to, col))

    def cond_got(k):
        src = (row + k) % rows_n
        return send(c_send.at[src], c_recv.at[src], c_sems.at[0, k], c_sems.at[1, src], (src, col))

    for k in range(1, rows_n):
        cond_copy(k).start()
    swap_x = Swap(place, lat, x_v, swap_sems, 0)
    swap_x.start()

    work = Gather(place, blocks, fulls, ag_sems)
    for a in range(3):
        work.start(a)

    members, first = [], 0
    for size in GROUPS:
        members.append(list(range(first, first + size)))
        first += size
    chunks = [(g, t) for g in range(len(GROUPS)) for t in range(depth)]
    events = [(s - n, n) for s in range(len(chunks) + 4) for n in range(5) if 0 <= s - n < len(chunks)]
    at = [0]

    def pump(count):
        for s, n in events[at[0]:at[0] + count]:
            if n == 0 and s in (2, depth + 2):
                for a in members[1 if s == 2 else 2]:
                    work.start(a)
            g, t = chunks[s]
            for a in members[g]:
                work.stage(a, t, n)
        at[0] += count

    def pump_to(s, n):
        pump(max(0, events.index((s, n)) + 1 - at[0]))

    pump_to(0, 0)
    c_recv[row] = c_send[row]
    for k in range(1, rows_n):
        cond_got(k).wait_recv()
    act_all = c_recv[...].reshape(rows_n * 8, drows).astype(bf16)
    s_send[...] = nn(act_all, ada[...]).reshape(rows_n, 8, 6 * hc)

    def sum_copy(k):
        to = (row + k) % rows_n
        return send(s_send.at[to], s_recv.at[row], s_sems.at[0, k], s_sems.at[1, row], (to, col))

    def sum_got(k):
        src = (row + k) % rows_n
        return send(s_send.at[src], s_recv.at[src], s_sems.at[0, k], s_sems.at[1, src], (src, col))

    for k in range(1, rows_n):
        sum_copy(k).start()
    pump_to(0, 1)
    s_recv[row] = s_send[row]
    for k in range(1, rows_n):
        sum_got(k).wait_recv()
    m_own[col] = s_recv[0] + s_recv[1] + s_recv[2] + s_recv[3] + bias[...]

    def mod_copy(k):
        return send(m_own.at[col], m_own.at[col], m_sems.at[0, k], m_sems.at[1, col], (row, (col + k) % cols_n))

    def mod_got(k):
        src = (col + k) % cols_n
        return send(m_own.at[src], m_own.at[src], m_sems.at[0, k], m_sems.at[1, src], (row, src))

    for k in range(1, cols_n):
        mod_copy(k).start()
    pump_to(0, 2)
    for k in range(1, cols_n):
        mod_got(k).wait_recv()
    other = send(m_own, m_oth, o_sems.at[0], o_sems.at[1], place.to_core)
    other.start()
    pump_to(0, 3)
    other.wait_recv()
    stay = place.h == place.x
    for c in range(cols_n):
        line = jnp.where(stay, m_own[c, pl.ds(place.z, 1), :], m_oth[c, pl.ds(place.z, 1), :])
        for k in range(6):
            vec[k:k + 1, c * hc:(c + 1) * hc] = line[:, k * hc:(k + 1) * hc]
        line = m_own[c, 4:5, :]
        vec[6:7, c * hc:(c + 1) * hc] = line[:, 576:576 + hc]
        vec[7:8, c * hc:(c + 1) * hc] = line[:, 576 + hc:]
        z, i = c // 2, c % 2
        vec[16 + z:17 + z, i * 512:(i + 1) * 512] = line[:, :512]
        vec[16 + z:17 + z, 1024 + i * 64:1024 + (i + 1) * 64] = line[:, 512:576]

    swap_x.wait()
    swap_dy = Swap(place, cot, o_cot, swap_sems, 1)
    swap_dy.start()
    part = 128

    def row_parts(body):
        @pl.loop(0, tokens // part)
        def _(i):
            body(pl.ds(pl.multiple_of(i * part, part), part))

    def first_norm(at_rows):
        normal, _ = norm_rows(x_v[at_rows, :].astype(f32))
        n1[at_rows, :] = (normal * (1.0 + vec[1:2, :]) + vec[0:1, :]).astype(bf16)

    row_parts(first_norm)

    saves = []

    def save(src, dst):
        copy = pltpu.make_async_copy(src, dst, save_sems.at[len(saves)])
        copy.start()
        saves.append(copy)

    save(x_v, o_x)
    save(n1, o_n1)
    save(c_recv, o_act)

    def fetch(s):
        g, t = chunks[s]
        zc, slot = work.zc(t), s % depth
        lanes = [q_main, p_main] if g == 0 else [blocks[members[g][0]].shape[1]]
        spot, copies = 0, []
        for i, n in enumerate(lanes):
            src = fulls[members[g][i]].at[:, pl.ds(pl.multiple_of(zc * 2 * n, 128), 2 * n)]
            copies.append(pltpu.make_async_copy(src, wbuf.at[slot, :, spot:spot + 2 * n], w_sems.at[s % 2, i]))
            spot += 2 * n
        src = fulls[members[g][-1]].at[:, pl.ds(pl.multiple_of(zc * 256, 128), 256)]
        copies.append(pltpu.make_async_copy(src, lbuf.at[s % 2], w_sems.at[s % 2, 2]))
        return copies

    def fetch_start(s):
        pump_to(s, 4)
        if s >= depth:
            weight_save(s - depth).wait()
        for copy in fetch(s):
            copy.start()

    def fetch_wait(s):
        for copy in fetch(s):
            copy.wait()
        unfold_into(lbuf.at[s % 2], wbuf.at[s % depth, :, 1024:1152])
        weight_save(s).start()

    def weight_save(s):
        g, t = chunks[s]
        return pltpu.make_async_copy(wbuf.at[s % depth], o_w.at[g, work.zc(t)], wsave_sems.at[s])

    def swap_kv(i, h):
        src, dst = ((k_v, k2_v), (v_v, v2_v))[i]
        return send(src.at[h], dst.at[h], kv_sems.at[0, i, h], kv_sems.at[1, i, h], place.to_core)

    def project(s):
        t, slot = chunks[s][1], s % depth
        zc = work.zc(t)

        @pl.loop(0, 2)
        def _(i):
            at_rows = pl.ds(pl.multiple_of(i * half, half), half)
            main = nn(n1[at_rows, :], wbuf[slot, :, :2 * q_main])
            left = nn(n1[at_rows, :], wbuf[slot, :, 1024:1152])
            for j in range(2):
                biases = m_own[2 * zc + j]
                own = main[:, j * q_main:(j + 1) * q_main]
                tail = left[:, j * 64:j * 64 + 3 * hc - q_main]
                for e in range(2):
                    h = 4 * zc + 2 * j + e
                    a = e * HEAD_DIM
                    q_v[h, at_rows, :] = (own[:, a:a + HEAD_DIM] + biases[5:6, a:a + HEAD_DIM]).astype(bf16)
                    k_v[h, at_rows, :] = own[:, hc + a:hc + a + HEAD_DIM].astype(bf16)
                    if e == 0:
                        value = own[:, 2 * hc:2 * hc + HEAD_DIM]
                    else:
                        value = jnp.concatenate([own[:, 2 * hc + HEAD_DIM:], tail], axis=1)
                    v_v[h, at_rows, :] = (value + biases[5:6, hc + a:hc + a + HEAD_DIM]).astype(bf16)

        for i in range(4):
            swap_kv(0, 4 * zc + i).start()
            swap_kv(1, 4 * zc + i).start()

    def attention(s):
        zc = work.zc(chunks[s][1])
        start = at[0]

        @pl.loop(0, 4)
        def _(i):
            h = 4 * zc + i
            swap_kv(0, h).wait_recv()
            swap_kv(1, h).wait_recv()
            one, two, total, lse = softmax_head(q_v[h], k_v[h], k2_v[h])
            ot[i] = (tn(v_v[h], one) + tn(v2_v[h], two)) / total
            lse_v[h] = lse
            for k in range(4):
                at[0] = start + k

                @pl.when(i == k)
                def _():
                    pump(1)

        at[0] = start + 4
        att[zc, :, 2 * p_main:] = jnp.zeros((tokens, 128), bf16)
        for j in range(2):
            pair = jnp.concatenate([ot[2 * j], ot[2 * j + 1]], axis=0).T.astype(bf16)
            att[zc, :, j * p_main:(j + 1) * p_main] = pair[:, :p_main]
            att[zc, :, 2 * p_main + 64 * j + 48:2 * p_main + 64 * j + 64] = pair[:, p_main:]

        @pl.loop(0, 2)
        def _(i):
            at_rows = pl.ds(pl.multiple_of(i * half, half), half)
            term = nt(att[zc, at_rows, :], wbuf[s % depth, :, 2 * q_main:])
            if s == 0:
                acc[at_rows, :] = term
            else:
                acc[at_rows, :] += term

    for s in range(depth):
        fetch_start(s)
        fetch_wait(s)
        project(s)
        if s > 0:
            attention(s - 1)
    attention(depth - 1)
    for src, dst in ((q_v, o_q), (k_v, o_k), (v_v, o_v), (k2_v, o_k2), (v2_v, o_v2), (lse_v, o_lse), (att, o_att)):
        save(src, dst)

    def second_norm(at_rows):
        branch = acc[at_rows, :] + vec[6:7, :]
        ba[at_rows, :] = branch.astype(bf16)
        middle = x_v[at_rows, :].astype(f32) + vec[2:3, :] * branch
        mid[at_rows, :] = middle
        normal, _ = norm_rows(middle)
        n2[at_rows, :] = (normal * (1.0 + vec[4:5, :]) + vec[3:4, :]).astype(bf16)

    row_parts(second_norm)
    for src, dst in ((ba, o_ba), (mid, o_mid), (n2, o_n2)):
        save(src, dst)

    for s in range(depth, 2 * depth):
        fetch_start(s)
        fetch_wait(s)
        zc = work.zc(chunks[s][1])

        def up(at_rows):
            u = nn(n2[at_rows, :], wbuf[s % depth]) + vec[pl.ds(16 + zc, 1), :]
            value, slope = gelu_both(u)
            hid[zc, at_rows, :] = value.astype(bf16)
            slo[zc, at_rows, :] = slope.astype(bf16)

        row_parts(up)
    save(hid, o_hid)
    save(slo, o_slo)
    for s in range(2 * depth, 3 * depth):
        fetch_start(s)
        fetch_wait(s)
        zc = work.zc(chunks[s][1])

        def down(at_rows):
            term = nt(hid[zc, at_rows, :], wbuf[s % depth])
            if s == 2 * depth:
                acc[at_rows, :] = term
            else:
                acc[at_rows, :] += term

        row_parts(down)

    swap_dy.wait()
    load_dy = pltpu.make_async_copy(o_cot, cot_v, w_sems.at[0, 0])
    load_dy.start()
    load_dy.wait()
    vec[8:9, :] = jnp.zeros((1, width), f32)

    def finish(at_rows):
        branch = acc[at_rows, :] + vec[7:8, :]
        out_v[at_rows, :] = (mid[at_rows, :] + vec[5:6, :] * branch).astype(bf16)
        vec[8:9, :] += jnp.sum(cot_v[at_rows, :].astype(f32) * branch, axis=0, keepdims=True)

    row_parts(finish)
    save(out_v, o_out)
    save(vec, o_vec)

    for a in range(7):
        work.finish(a)
    for k in range(1, rows_n):
        cond_copy(k).wait_send()
        sum_copy(k).wait_send()
    for k in range(1, cols_n):
        mod_copy(k).wait_send()
    other.wait_send()

    @pl.loop(0, 4 * depth)
    def _(h):
        swap_kv(0, h).wait_send()
        swap_kv(1, h).wait_send()

    for s in range(2 * depth, 3 * depth):
        weight_save(s).wait()
    for copy in saves:
        copy.wait()


def forward(lat, cot, cond, ada, bias, blocks, collective_id):
    rows, cols = lax.axis_size("row"), lax.axis_size("col")
    depth = cols // 2
    tokens, width = lat.shape
    heads = width // HEAD_DIM
    lanes = 1152
    hc6 = ada.shape[1]
    shape = jax.ShapeDtypeStruct
    head = shape((heads, tokens, HEAD_DIM), bf16)
    token = shape((tokens, width), bf16)
    outs = [shape((rows * b.shape[0], cols * b.shape[1]), bf16) for b in blocks] + [
        shape((3, depth, width, lanes), bf16), token, token, token, head, head, head, head, head,
        shape((heads, 1, tokens), f32), shape((depth, tokens, 384), bf16), token, shape((tokens, width), f32), token,
        shape((depth, tokens, lanes), bf16), shape((depth, tokens, lanes), bf16), token, shape((VECS, width), f32), shape((rows, 8, ada.shape[0]), f32)]
    dma, vm = pltpu.SemaphoreType.DMA, pltpu.VMEM
    t16, h16 = vm((tokens, width), bf16), vm((heads, tokens, HEAD_DIM), bf16)
    drows = ada.shape[0]
    scratch = [
        t16, t16, h16, h16, h16, h16, h16, vm((heads, 1, tokens), f32), vm((4, HEAD_DIM, tokens), f32),
        vm((depth, tokens, 384), bf16), t16, vm((tokens, width), f32), t16, vm((depth, tokens, lanes), bf16),
        vm((depth, tokens, lanes), bf16), vm((tokens, width), f32), vm((depth, width, lanes), bf16), vm((2, width // 2, 256), bf16),
        t16, t16, vm((VECS, width), f32), vm((rows, 8, drows), f32), vm((rows, 8, drows), f32), vm((rows, 8, hc6), f32),
        vm((rows, 8, hc6), f32), vm((cols, 8, hc6), f32), vm((cols, 8, hc6), f32)]
    scratch += Gather.scratch(len(blocks), depth)
    scratch += [dma((2, 2)), dma((2, rows)), dma((2, rows)), dma((2, cols)), dma((2,)), dma((2, 2, heads)), dma((2, 3)), dma((32,)),
                dma((3 * depth,))]
    vmem = pl.BlockSpec(memory_space=pltpu.VMEM)
    got = pl.pallas_call(
        forward_kernel,
        out_shape=outs,
        in_specs=[ANY, ANY, vmem, vmem, vmem] + [ANY] * len(blocks),
        out_specs=[ANY] * len(outs),
        scratch_shapes=scratch,
        compiler_params=pltpu.CompilerParams(collective_id=collective_id, has_side_effects=True, vmem_limit_bytes=62 * 2**20),
        name="forward",
    )(lat, cot, cond, ada, bias, *blocks)
    return got[len(blocks):]


def backward_kernel(*refs):
    (w, dy_h, x_h, n1_h, q_h, k_h, v_h, k2_h, v2_h, att_h, ba_h, mid_h, n2_h, hid_h, slo_h, out_h), refs = refs[:16], refs[16:]
    (lse, vec, act, ada, cond), refs = refs[:5], refs[5:]
    (o_out, o_lat, o_pq, o_fc2, o_fc1, o_qkv, o_proj, o_ada, o_rows, o_cond), refs = refs[:10], refs[10:]
    (acc, give, r0, r1, r1l, r2, r2l, r3, r3l, lf, lx), refs = refs[:11], refs[11:]
    (wbuf, hs, pre, pq, turn, tmp, ml, gm, gx, slo, att, heads, grad_o, delta, kv_give, kv_got, own, gv), refs = refs[:18], refs[18:]
    (tt, tc, um, vm_, modl, cp, cr, cf), refs = refs[:8], refs[8:]
    (swap_sems, s0, s1, s2, s3, lx_sems, w_sems, hs_sems, slo_sems, tmp_sems, head_sems, kv_sems, pq_sems, t_sems, u_sems, v_sems, cr_sems, cf_sems) = refs

    place = Place()
    depth, rows_n = place.depth, 4
    row, col, h = place.row, place.col, place.h
    cols_n = 2 * depth
    tokens, width = ml.shape
    hc = width // cols_n
    drows = ada.shape[0]
    lrows = drows // 2
    half, part = tokens // 2, 128
    q_main, p_main = 384, 128
    scale = HEAD_DIM ** (-0.5)
    row_peers = [((row + k) % rows_n, col) for k in range(1, rows_n)]
    col_peers = [(row, (col + k) % cols_n) for k in range(1, cols_n)]
    flip_x, flip_y = (row, col + 1 - 2 * place.x), (row + 2 - 4 * place.y, col)
    greet(place.partners() + row_peers + col_peers + [place.diagonal()])

    def send(src, dst, s_sem, r_sem, to):
        return pltpu.make_async_remote_copy(
            src_ref=src, dst_ref=dst, send_sem=s_sem, recv_sem=r_sem, device_id=to, device_id_type=MESH)

    def row_parts(body):
        @pl.loop(0, tokens // part)
        def _(i):
            body(pl.ds(pl.multiple_of(i * part, part), part))

    def row_halves(body):
        @pl.loop(0, 2)
        def _(i):
            body(pl.ds(pl.multiple_of(i * half, half), half))

    def zc(t):
        return lax.rem(place.z + 1 + t, depth)

    def load(src, i):
        copy = pltpu.make_async_copy(src, tmp.at[i], tmp_sems.at[i])
        copy.start()
        return copy

    def weight_load(u):
        return pltpu.make_async_copy(w.at[2 - u // depth, zc(u % depth)], wbuf.at[u % 2], w_sems.at[u % 2])

    def slope_load(u):
        return pltpu.make_async_copy(slo_h.at[zc(u)], slo.at[u % 2], slo_sems.at[u % 2])

    def weight_use(u):
        weight_load(u).wait()
        if u + 1 < 3 * depth:
            weight_load(u + 1).start()


    def tick_loads(s):
        g, t = s // depth, s % depth
        if g == 0:
            return [pltpu.make_async_copy(hid_h.at[zc(t)], hs.at[s % 2], hs_sems.at[s % 2, 0])]
        if g == 1:
            return []
        return [pltpu.make_async_copy(o_pq.at[zc(t)], hs.at[s % 2, :, :896], hs_sems.at[s % 2, 0]),
                pltpu.make_async_copy(att_h.at[zc(t)], att.at[s % 2], hs_sems.at[s % 2, 1])]

    def tick_prefetch(s):
        if s < 3 * depth:
            for copy in tick_loads(s):
                copy.start()

    def pq_save(t):
        return pltpu.make_async_copy(pq, o_pq.at[zc(t)], pq_sems.at[t])

    def c0(s, y):
        return send(give.at[s % 2, y], r0.at[s % 2, y], s0.at[0, s % 2, y], s0.at[1, s % 2, y], place.to_core)

    def spots(s, y, x):
        return (acc.at[s % 4, y, :, pl.ds(pl.multiple_of(x * 512, 512), 512)],
                acc.at[s % 4, y, pl.ds(pl.multiple_of(x * lrows, 16), lrows), 1024:1152])

    def c1(s, j):
        main, left = spots(s, *place.yx(1 - place.p, j))
        k = s % 4
        return [send(main, r1.at[k, j], s1.at[0, k, j, 0], s1.at[1, k, j, 0], place.to_p),
                send(left, r1l.at[k, j], s1.at[0, k, j, 1], s1.at[1, k, j, 1], place.to_p)]

    def c2(s):
        main, left = spots(s, *place.yx(place.p, 1 - place.q))
        k = s % 4
        return [send(main, r2.at[k], s2.at[0, k, 0], s2.at[1, k, 0], place.to_q),
                send(left, r2l.at[k], s2.at[0, k, 1], s2.at[1, k, 1], place.to_q)]

    def c3(s):
        g, t = s // depth, s % depth
        main, left = spots(s, *place.yx(place.p, place.q))
        to = place.to_z(zc(t))
        return [send(main, r3.at[g, t], s3.at[0, g, t, 0], s3.at[1, g, t, 0], to),
                send(left, r3l.at[g, t], s3.at[0, g, t, 1], s3.at[1, g, t, 1], to)]

    def add_into(into, other):
        n = into.shape[0]

        @pl.loop(0, n // 48)
        def _(i):
            at_rows = pl.ds(pl.multiple_of(i * 48, 16), 48)
            into[at_rows, :] = into[at_rows, :] + other[at_rows, :]

    def tick_a(s):
        g, t = s // depth, s % depth
        k = s % 4
        if s >= 4:
            for j in range(2):
                for copy in c1(s - 4, j):
                    copy.wait_send()
            for copy in c2(s - 4):
                copy.wait_send()
            if (s - 4) % depth < depth - 1:
                for copy in c3(s - 4):
                    copy.wait_send()
        if s >= 2:
            for y in range(2):
                c0(s - 2, y).wait_send()
        for copy in tick_loads(s):
            copy.wait()

        def rows_of(r):
            at_rows = pl.ds(pl.multiple_of(r * drows, 16), drows)
            if g == 0:
                return nn(turn[0, at_rows, :], hs[s % 2]).astype(bf16)
            if g == 1:
                return nn(turn[0, at_rows, :], pre[zc(t)]).astype(bf16)
            one = nn(turn[1, at_rows, :], hs[s % 2, :, :896])
            two = nn(turn[0, at_rows, :], att[s % 2])
            return jnp.concatenate(
                [one[:, :q_main], two[:, :p_main], one[:, q_main:2 * q_main], two[:, p_main:2 * p_main],
                 one[:, 2 * q_main:] + two[:, 2 * p_main:]], axis=1).astype(bf16)

        @pl.loop(0, 2)
        def _(y):
            give[s % 2, y] = rows_of(2 * y + 1 - h)
            acc[k, y] = rows_of(2 * y + h)

        for y in range(2):
            c0(s, y).start()
        tick_prefetch(s + 1)

    def tick_b(s):
        if 0 <= s - 1 < 3 * depth:
            n = s - 1
            for j in range(2):
                for copy in c1(n, j):
                    copy.wait_recv()
            for into, other in zip(spots(n, *place.yx(place.p, 1 - place.q)), (r1.at[n % 4, 1 - place.q], r1l.at[n % 4, 1 - place.q])):
                add_into(into, other)
            for copy in c2(n):
                copy.start()
            for into, other in zip(spots(n, *place.yx(place.p, place.q)), (r1.at[n % 4, place.q], r1l.at[n % 4, place.q])):
                add_into(into, other)
        if s < 3 * depth:
            for y in range(2):
                c0(s, y).wait_recv()
            for y in range(2):
                add_into(acc.at[s % 4, y], r0.at[s % 2, y])
            for j in range(2):
                for copy in c1(s, j):
                    copy.start()
        if 0 <= s - 2 < 3 * depth:
            n = s - 2
            for copy in c2(n):
                copy.wait_recv()
            for into, other in zip(spots(n, *place.yx(place.p, place.q)), (r2.at[n % 4], r2l.at[n % 4])):
                add_into(into, other)
            if n % depth < depth - 1:
                for copy in c3(n):
                    copy.start()
        if 0 <= s - 3 < 3 * depth and (s - 3) % depth == depth - 1:
            total((s - 3) // depth)

    def left_copy(g):
        return send(lf.at[g], lx.at[g], lx_sems.at[0, g], lx_sems.at[1, g], flip_x)

    def total(g):
        last = (g + 1) * depth - 1
        for t in range(depth - 1):
            for copy in c3(g * depth + t):
                copy.wait_recv()
        main, left = spots(last, *place.yx(place.p, place.q))

        @pl.loop(0, drows // 48)
        def _(i):
            at_rows = pl.ds(pl.multiple_of(i * 48, 16), 48)
            value = main[at_rows, :].astype(f32)
            for t in range(depth - 1):
                value = value + r3[g, t, at_rows, :].astype(f32)
            if g == 0:
                o_fc2[at_rows, :512] = value
            elif g == 1:
                o_fc1[at_rows, :512] = value
            else:
                o_qkv[at_rows, :q_main] = value[:, :q_main]
                o_proj[at_rows, :p_main] = value[:, q_main:]

        value = left[...].astype(f32)
        for t in range(depth - 1):
            value = value + r3l[g, t].astype(f32)
        lf[g] = value
        left_copy(g).start()

    def left_finish(g):
        left_copy(g).wait_recv()
        first = place.x == 0
        top = jnp.where(first, lf[g][:, :64], lx[g][:, 64:])
        bottom = jnp.where(first, lx[g][:, :64], lf[g][:, 64:])
        tail = 3 * hc - q_main
        for spot, value in ((0, top), (lrows, bottom)):
            if g == 0:
                o_fc2[spot:spot + lrows, 512:] = value
            elif g == 1:
                o_fc1[spot:spot + lrows, 512:] = value
            else:
                o_qkv[spot:spot + lrows, q_main:] = value[:, :tail]
                o_proj[spot:spot + lrows, p_main:] = value[:, tail:]

    def turn_into(i, src):
        @pl.loop(0, width // 128)
        def _(n):
            spot = pl.ds(pl.multiple_of(n * 128, 128), 128)
            turn[i, spot, :] = src[:, spot].T

    swap_out = Swap(place, out_h, o_out, swap_sems, 0)
    load_dy = load(dy_h, 0)
    weight_load(0).start()
    slope_load(0).start()
    tick_prefetch(0)
    swap_out.start()
    gv[...] = jnp.zeros_like(gv)
    tt[...] = jnp.zeros_like(tt)
    gv[5:6, :] = vec[8:9, :]
    load_dy.wait()

    def first(at_rows):
        grad = tmp[0, at_rows, :].astype(f32) * vec[5:6, :]
        gv[7:8, :] += jnp.sum(grad, axis=0, keepdims=True)
        ml[at_rows, :] = grad.astype(bf16)

    row_parts(first)
    turn_into(0, ml)

    def hidden_back(u):
        z = zc(u)
        weight_use(u)
        slope_load(u).wait()
        if u + 1 < depth:
            slope_load(u + 1).start()
        sums = gv.at[8:9, :]
        sums[...] = jnp.zeros((1, width), f32)

        def body(at_rows):
            grad = nn(ml[at_rows, :], wbuf[u % 2]) * slo[u % 2, at_rows, :].astype(f32)
            sums[...] += jnp.sum(grad, axis=0, keepdims=True)
            pre[z, at_rows, :] = grad.astype(bf16)

        row_parts(body)
        for j in range(2):
            tt[2 * z + j, 1:2, :512] = sums[:, 512 * j:512 * (j + 1)]
            tt[2 * z + j, 1:2, 512:576] = sums[:, 1024 + 64 * j:1024 + 64 * (j + 1)]

    def normed_back(u):
        z = zc(u % depth)
        weight_use(u)

        def body(at_rows):
            term = nt(pre[z, at_rows, :], wbuf[u % 2])
            if u == depth:
                gx[at_rows, :] = term
            else:
                gx[at_rows, :] += term

        row_parts(body)

    tick_a(0)
    hidden_back(0)
    tick_b(0)
    hidden_back(1)
    tick_a(1)
    hidden_back(2)
    tick_b(1)
    hidden_back(3)
    for u in range(depth, 2 * depth):
        if u == depth + 1:
            tick_a(2)
        if u == depth + 3:
            tick_b(2)
        normed_back(u)

    load_mid = pltpu.make_async_copy(mid_h, gm, tmp_sems.at[2])
    load_mid.start()
    load_ba, load_dy = load(ba_h, 1), load(dy_h, 0)
    load_mid.wait()
    load_ba.wait()
    load_dy.wait()

    def norm_grad(values, grads, shift_row, scale_row, scale_vec):
        normal, inverse = norm_rows(values)
        gv[shift_row:shift_row + 1, :] += jnp.sum(grads, axis=0, keepdims=True)
        gv[scale_row:scale_row + 1, :] += jnp.sum(grads * normal, axis=0, keepdims=True)
        inner = grads * (1.0 + scale_vec)
        one = jnp.mean(inner, axis=-1, keepdims=True)
        two = jnp.mean(inner * normal, axis=-1, keepdims=True)
        return inverse * (inner - one - normal * two)

    def second(at_rows):
        grad = norm_grad(gm[at_rows, :], gx[at_rows, :], 3, 4, vec[4:5, :]) + tmp[0, at_rows, :].astype(f32)
        gm[at_rows, :] = grad
        gv[2:3, :] += jnp.sum(grad * tmp[1, at_rows, :].astype(f32), axis=0, keepdims=True)
        grad = grad * vec[2:3, :]
        gv[6:7, :] += jnp.sum(grad, axis=0, keepdims=True)
        ml[at_rows, :] = grad.astype(bf16)

    row_parts(second)

    def heads_load(t):
        spot = pl.ds(4 * zc(t), 4)
        return [pltpu.make_async_copy(src.at[spot], heads.at[i], head_sems.at[i])
                for i, src in enumerate((q_h, k_h, v_h, k2_h, v2_h))]

    def att_load(t):
        return pltpu.make_async_copy(att_h.at[zc(t)], att.at[t % 2], hs_sems.at[t % 2, 1])

    def kv_swap(t, kind, i):
        return send(kv_give.at[kind, i], kv_got.at[t % 2, kind, i], kv_sems.at[0, 0, kind, i], kv_sems.at[1, t % 2, kind, i], place.to_core)

    def pair_of(value, j):
        spot = 2 * p_main + 64 * j + 48
        return jnp.concatenate([value[:, j * p_main:(j + 1) * p_main], value[:, spot:spot + 16]], axis=1)

    def attention_open(t):
        u = 2 * depth + t
        weight_use(u)
        att_load(t).wait()

        def body(at_rows):
            grads = nn(ml[at_rows, :], wbuf[u % 2, :, 2 * q_main:])
            results = att[t % 2, at_rows, :].astype(f32)
            for j in range(2):
                grad = pair_of(grads, j).astype(bf16)
                product = (grad.astype(f32) * pair_of(results, j)).T
                for e in range(2):
                    grad_o[2 * j + e, at_rows, :] = grad[:, e * HEAD_DIM:(e + 1) * HEAD_DIM]
                    delta[2 * j + e, :, at_rows] = jnp.sum(product[e * HEAD_DIM:(e + 1) * HEAD_DIM, :], axis=0, keepdims=True)

        row_halves(body)
        for copy in heads_load(t):
            copy.wait()

    def attention_heads(t, between):
        @pl.loop(0, 4)
        def _(i):
            q, out_grad, shift, less = heads[0, i], grad_o[i], lse[4 * zc(t) + i], delta[i]

            def side(k, v):
                probs = jnp.exp2(nt(k, q) * SOFT - shift)
                grad = (probs * (nt(v, out_grad) - less)).astype(bf16)
                return nn(grad, q) * scale, nn(probs.astype(bf16), out_grad), tn(k, grad)

            dk, dv, dq_two = side(heads[3, i], heads[4, i])
            kv_give[0, i] = dk.astype(bf16)
            kv_give[1, i] = dv.astype(bf16)
            kv_swap(t, 0, i).start()
            kv_swap(t, 1, i).start()
            dk, dv, dq_one = side(heads[1, i], heads[2, i])
            own[1, i] = dk
            own[2, i] = dv
            own[0, i] = ((dq_one + dq_two) * scale).T
            for n, action in between:
                pl.when(i == n)(action)

    def attention_close(t):
        u = 2 * depth + t
        z = zc(t)
        if t + 1 < depth:
            for copy in heads_load(t + 1):
                copy.start()
            att_load(t + 1).start()
        for kind in range(2):
            for i in range(4):
                kv_swap(t, kind, i).wait()
        if t > 0:
            pq_save(t - 1).wait()

        def body(at_rows):
            for j in range(2):
                pieces, tails = [[], [], []], None
                for e in range(2):
                    i = 2 * j + e
                    dq = own[0, i, at_rows, :]
                    dk = own[1, i, at_rows, :] + kv_got[t % 2, 0, i, at_rows, :].astype(f32)
                    dv = own[2, i, at_rows, :] + kv_got[t % 2, 1, i, at_rows, :].astype(f32)
                    tt[2 * z + j, 2:3, e * HEAD_DIM:(e + 1) * HEAD_DIM] += jnp.sum(dq, axis=0, keepdims=True)
                    tt[2 * z + j, 2:3, hc + e * HEAD_DIM:hc + (e + 1) * HEAD_DIM] += jnp.sum(dv, axis=0, keepdims=True)
                    for n, value in enumerate((dq, dk, dv)):
                        pieces[n].append(value)
                last = pieces[2][1]
                cut = q_main - 2 * hc - HEAD_DIM
                line = pieces[0] + pieces[1] + [pieces[2][0], last[:, :cut]]
                pq[at_rows, j * q_main:(j + 1) * q_main] = jnp.concatenate(line, axis=1).astype(bf16)
                rest = jnp.concatenate([last[:, cut:], jnp.zeros((last.shape[0], 64 - HEAD_DIM + cut), f32)], axis=1)
                pq[at_rows, 2 * q_main + 64 * j:2 * q_main + 64 * (j + 1)] = rest.astype(bf16)
            term = nt(pq[at_rows, :2 * q_main], wbuf[u % 2, :, :2 * q_main]) + nt(pq[at_rows, 2 * q_main:], wbuf[u % 2, :, 1024:])
            if t == 0:
                gx[at_rows, :] = term
            else:
                gx[at_rows, :] += term

        row_halves(body)
        pq_save(t).start()

    for copy in heads_load(0):
        copy.start()
    att_load(0).start()
    load_n2 = load(n2_h, 0)
    tick_a(3)
    load_n2.wait()
    turn_into(0, tmp.at[0])
    attention_open(0)
    tick_b(3)
    attention_heads(0, [(1, lambda: tick_a(4)), (3, lambda: tick_b(4))])
    attention_close(0)
    attention_open(1)
    tick_a(5)
    attention_heads(1, [(0, lambda: tick_b(5)), (2, lambda: tick_a(6))])
    attention_close(1)
    tick_b(6)
    attention_open(2)
    attention_heads(2, [(1, lambda: tick_a(7))])
    load_x, load_n1 = load(x_h, 0), load(n1_h, 1)
    tick_b(7)
    load_n1.wait()
    turn_into(1, tmp.at[1])
    turn_into(0, ml)
    attention_close(2)
    attention_open(3)
    tick_a(8)
    attention_heads(3, [(1, lambda: tick_b(8))])
    attention_close(3)
    pq_save(3).wait()
    tick_a(9)
    load_x.wait()

    def third(at_rows):
        grad = norm_grad(tmp[0, at_rows, :].astype(f32), gx[at_rows, :], 0, 1, vec[1:2, :]) + gm[at_rows, :]
        tmp[1, at_rows, :] = grad.astype(bf16)

    row_parts(third)
    swap_lat = Swap(place, tmp.at[1], o_lat, swap_sems, 1)
    swap_lat.start()

    for c in range(cols_n):
        spot = slice(c * hc, (c + 1) * hc)
        for k in range(6):
            tt[c, 0:1, k * hc:(k + 1) * hc] = gv[k:k + 1, spot]
        tt[c, 1:2, 576:576 + hc] = gv[6:7, spot]
        tt[c, 1:2, 576 + hc:] = gv[7:8, spot]
    copy_t = send(tt, tc, t_sems.at[0], t_sems.at[1], place.to_core)
    copy_t.start()
    tick_b(9)
    copy_t.wait()
    tt[...] = tt[...] + tc[...]

    def u_copy(k):
        to = (col + k) % cols_n
        return send(tt.at[to], um.at[col], u_sems.at[0, k], u_sems.at[1, col], (row, to))

    def u_got(k):
        src = (col + k) % cols_n
        return send(tt.at[src], um.at[src], u_sems.at[0, k], u_sems.at[1, src], (row, src))

    for k in range(1, cols_n):
        u_copy(k).start()
    um[col] = tt[col]
    tick_a(10)
    for k in range(1, cols_n):
        u_got(k).wait_recv()
    copy_v = send(um, vm_, v_sems.at[0], v_sems.at[1], flip_y)
    copy_v.start()
    tick_b(10)
    copy_v.wait_recv()
    modl[...] = jnp.zeros_like(modl)
    sums = um[0] + vm_[0]
    for c in range(1, cols_n):
        sums = sums + um[c] + vm_[c]
    o_rows[...] = sums
    for c in range(cols_n):
        modl[2 * place.y + c % 2, c // 2:c // 2 + 1, :] = um[c, 0:1, :]
        modl[2 - 2 * place.y + c % 2, c // 2:c // 2 + 1, :] = vm_[c, 0:1, :]
    low = modl[...].reshape(rows_n * 8, 6 * hc).astype(bf16)
    o_ada[...] = tn(act[...].reshape(rows_n * 8, drows).astype(bf16), low)
    cp[...] = nt(low, ada[...]).reshape(rows_n, 8, drows)

    def cr_copy(k):
        return send(cp, cr.at[col], cr_sems.at[0, k], cr_sems.at[1, col], (row, (col + k) % cols_n))

    def cr_got(k):
        src = (col + k) % cols_n
        return send(cp, cr.at[src], cr_sems.at[0, k], cr_sems.at[1, src], (row, src))

    for k in range(1, cols_n):
        cr_copy(k).start()
    tick_a(11)
    tick_b(11)
    for k in range(1, cols_n):
        cr_got(k).wait_recv()
        cr_copy(k).wait_send()
    cr[col] = cp[...]
    cp[...] = sum(cr[c] for c in range(cols_n))

    def cf_copy(k):
        to = (row + k) % rows_n
        return send(cp.at[to], cf.at[row], cf_sems.at[0, k], cf_sems.at[1, row], (to, col))

    def cf_got(k):
        src = (row + k) % rows_n
        return send(cp.at[src], cf.at[src], cf_sems.at[0, k], cf_sems.at[1, src], (src, col))

    for k in range(1, rows_n):
        cf_copy(k).start()
    cf[row] = cp[row]
    tick_b(12)
    for k in range(1, rows_n):
        cf_got(k).wait_recv()
    cond_value = cond[...]
    gate = 1.0 / (1.0 + jnp.exp(-cond_value))
    slope = gate * (1.0 + cond_value * (1.0 - gate))
    for r in range(rows_n):
        spot = slice(r * drows, (r + 1) * drows)
        o_cond[:, spot] = cf[r] * slope[:, spot]
    tick_b(13)
    left_finish(0)
    left_finish(1)
    tick_b(14)
    left_finish(2)

    for s in range(3 * depth - 4, 3 * depth):
        for j in range(2):
            for copy in c1(s, j):
                copy.wait_send()
        for copy in c2(s):
            copy.wait_send()
        if s % depth < depth - 1:
            for copy in c3(s):
                copy.wait_send()
    for s in range(3 * depth - 2, 3 * depth):
        for y in range(2):
            c0(s, y).wait_send()
    for g in range(3):
        left_copy(g).wait_send()
    for k in range(1, cols_n):
        u_copy(k).wait_send()
    copy_v.wait_send()
    for k in range(1, rows_n):
        cf_copy(k).wait_send()
    swap_lat.wait()
    swap_out.wait()


def backward(saved, out, lse, vec, act, ada, cond, collective_id):
    rows, cols = lax.axis_size("row"), lax.axis_size("col")
    depth = cols // 2
    tokens, width = out.shape
    heads, drows, hc6 = width // HEAD_DIM, ada.shape[0], ada.shape[1]
    hc, lanes, lrows = width // cols, 1152, drows // 2
    shape, dma, vm = jax.ShapeDtypeStruct, pltpu.SemaphoreType.DMA, pltpu.VMEM
    token = shape((tokens, width), bf16)
    outs = [token, token, shape((depth, tokens, 896), bf16), shape((drows, 576), f32), shape((drows, 576), f32),
            shape((drows, 3 * hc), f32), shape((drows, hc), f32), shape((drows, hc6), f32), shape((8, hc6), f32),
            shape((8, width), f32)]
    head = (tokens, HEAD_DIM)
    scratch = [
        vm((4, 2, drows, lanes), bf16), vm((2, 2, drows, lanes), bf16), vm((2, 2, drows, lanes), bf16),
        vm((4, 2, drows, 512), bf16), vm((4, 2, lrows, 128), bf16), vm((4, drows, 512), bf16), vm((4, lrows, 128), bf16),
        vm((3, depth - 1, drows, 512), bf16), vm((3, depth - 1, lrows, 128), bf16), vm((3, lrows, 128), f32), vm((3, lrows, 128), f32),
        vm((2, width, lanes), bf16), vm((2, tokens, lanes), bf16), vm((depth, tokens, lanes), bf16), vm((tokens, 896), bf16),
        vm((2, width, tokens), bf16), vm((2, tokens, width), bf16), vm((tokens, width), bf16), vm((tokens, width), f32),
        vm((tokens, width), f32), vm((2, tokens, lanes), bf16), vm((2, tokens, 384), bf16), vm((5, 4) + head, bf16),
        vm((4,) + head, bf16), vm((4, 1, tokens), f32), vm((2, 4) + head, bf16), vm((2, 2, 4) + head, bf16), vm((3, 4) + head, f32),
        vm((16, width), f32),
        vm((cols, 8, hc6), f32), vm((cols, 8, hc6), f32), vm((cols, 8, hc6), f32), vm((cols, 8, hc6), f32), vm((rows, 8, hc6), f32),
        vm((rows, 8, drows), f32), vm((cols, rows, 8, drows), f32), vm((rows, 8, drows), f32)]
    scratch += [
        dma((2, 2)), dma((2, 2, 2)), dma((2, 4, 2, 2)), dma((2, 4, 2)), dma((2, 3, depth, 2)), dma((2, 3)), dma((2,)), dma((2, 2)),
        dma((2,)), dma((3,)), dma((5,)), dma((2, 2, 2, 4)), dma((depth,)), dma((2,)), dma((2, cols)), dma((2,)), dma((2, cols)),
        dma((2, rows))]
    vmem = pl.BlockSpec(memory_space=pltpu.VMEM)
    return pl.pallas_call(
        backward_kernel,
        out_shape=outs,
        in_specs=[ANY] * 16 + [vmem] * 5,
        out_specs=[ANY] * 3 + [vmem] * 7,
        scratch_shapes=scratch,
        compiler_params=pltpu.CompilerParams(collective_id=collective_id, has_side_effects=True, vmem_limit_bytes=63 * 2**20),
        name="backward",
    )(*saved, out, lse, vec, act, ada, cond)


class Plan:
    def __init__(self, latents, condition, qkv_weight, fc1_weight):
        self.rows, self.cols = lax.axis_size("row"), lax.axis_size("col")
        self.tokens, self.width = latents.shape
        self.lats = condition.shape[0]
        self.depth_rows = qkv_weight.shape[0]
        self.head_cols = qkv_weight.shape[2]
        self.ff_cols = fc1_weight.shape[1]
        self.share = SEQ // self.tokens
        self.near = (
            self.rows == 4 and self.share == 2 and self.cols == 8 and self.lats == self.cols // 2
            and (self.depth_rows, self.head_cols, self.ff_cols) == (288, 2 * HEAD_DIM, 576) and self.width == 1152)


def fold(left):
    rows, lanes = left.shape
    return left.reshape(2, rows // 2, lanes).transpose(1, 0, 2).reshape(rows // 2, 2 * lanes)


def gather_plain(blocks):
    return [lax.all_gather(lax.all_gather(b, "row", axis=0, tiled=True), "col", axis=1, tiled=True) for b in blocks]


def scatter_plain(fulls):
    parts = [lax.psum_scatter(g, "row", scatter_dimension=0, tiled=True) for g in fulls]
    return [lax.psum_scatter(g, "col", scatter_dimension=1, tiled=True).astype(f32) for g in parts]


def attend_plain(q, k, v):
    def one(item):
        scores = nt(item[0], item[1]) * HEAD_DIM ** (-0.5)
        top = jnp.max(scores, axis=-1, keepdims=True)
        probs = jnp.exp(scores - top)
        total = jnp.sum(probs, axis=-1, keepdims=True)
        return nn((probs / total).astype(bf16), item[2]).astype(bf16), top + jnp.log(total)

    return lax.map(one, (q, k, v))


def attend_back_plain(q, k, v, lse, att_grad):
    def one(item):
        q, k, v, lse, out_grad = item
        probs = jnp.exp(nt(q, k) * HEAD_DIM ** (-0.5) - lse)
        probs_grad = nt(out_grad, v)
        inner = jnp.sum(probs * probs_grad, axis=-1, keepdims=True)
        grad = (probs * (probs_grad - inner) * HEAD_DIM ** (-0.5)).astype(bf16)
        return nn(grad, k), tn(grad, q), tn(probs.astype(bf16), out_grad)

    return lax.map(one, (q, k, v, lse, att_grad))


def gelu_and_slope(u):
    c = math.sqrt(2.0 / math.pi)
    inner = jnp.tanh(c * (u + 0.044715 * u * u * u))
    value = 0.5 * u * (1.0 + inner)
    slope = 0.5 * (1.0 + inner) + 0.5 * u * (1.0 - inner * inner) * c * (1.0 + 3 * 0.044715 * u * u)
    return value, slope


def layer_norm(values):
    mean = jnp.mean(values, axis=-1, keepdims=True)
    centred = values - mean
    inverse = lax.rsqrt(jnp.mean(centred * centred, axis=-1, keepdims=True) + norm_eps)
    return centred * inverse, inverse


def norm_back(rows_grad, normal, inverse, scale):
    normal_grad = rows_grad * (1.0 + scale)
    first = jnp.mean(normal_grad, axis=-1, keepdims=True)
    second = jnp.mean(normal_grad * normal, axis=-1, keepdims=True)
    value_grad = inverse * (normal_grad - first - normal * second)
    return value_grad, jnp.sum(rows_grad, axis=0), jnp.sum(rows_grad * normal, axis=0)


def shards_near(plan, latents, condition, ada_weight, ada_bias, qkv_weight, qv_bias, proj_weight, proj_bias,
                fc1_weight, fc1_bias, fc2_weight, fc2_bias, cotangent):
    depth, hc, fc = plan.depth_rows, plan.head_cols, plan.ff_cols
    q_main, p_main, f_main = 384, 128, 512
    qkv_flat = qkv_weight.reshape(depth, 3 * hc)
    proj_t, fc2_t = proj_weight.T, fc2_weight.T
    left_a = fold(jnp.concatenate([qkv_flat[:, q_main:], proj_t[:, p_main:]], axis=1))
    blocks = [qkv_flat[:, :q_main], proj_t[:, :p_main], left_a,
              fc1_weight[:, :f_main], fold(fc1_weight[:, f_main:]), fc2_t[:, :f_main], fold(fc2_t[:, f_main:])]
    cond = jnp.pad(condition.astype(f32), ((0, 8 - plan.lats), (0, 0)))
    ada = ada_weight.reshape(depth, 6 * hc)
    line = jnp.concatenate([fc1_bias, proj_bias, fc2_bias]).astype(f32).reshape(1, 6 * hc)
    tail = jnp.pad(qv_bias.astype(f32).reshape(1, 2 * hc), ((0, 0), (0, 4 * hc)))
    bias = jnp.concatenate([jnp.broadcast_to(ada_bias.astype(f32).reshape(1, 6 * hc), (plan.lats, 6 * hc)), line, tail,
                            jnp.zeros((8 - plan.lats - 2, 6 * hc), f32)], axis=0)
    (w, dy, x, n1, q, k, v, k2, v2, lse, att, ba, mid, n2, hid, slo, out, vec, act) = forward(
        latents, cotangent, cond, ada, bias, blocks, 0)
    output, lat_grad, _, fc2_sum, fc1_sum, qkv_sum, proj_sum, ada_sum, rows, cond_grad = backward(
        (w, dy, x, n1, q, k, v, k2, v2, att, ba, mid, n2, hid, slo), out, lse, vec, act, ada, cond, 1)
    return (
        output, lat_grad.astype(f32), cond_grad[:plan.lats], ada_sum.reshape(depth, 6, hc), rows[0].reshape(6, hc),
        qkv_sum.reshape(depth, 3, hc), rows[2, :2 * hc].reshape(2, hc), proj_sum.T, rows[1, fc:fc + hc],
        fc1_sum, rows[1, :fc], fc2_sum.T, rows[1, fc + hc:])


def shards(latents, condition, ada_weight, ada_bias, qkv_weight, qv_bias, proj_weight, proj_bias,
           fc1_weight, fc1_bias, fc2_weight, fc2_bias, cotangent):
    plan = Plan(latents, condition, qkv_weight, fc1_weight)
    if plan.near:
        return shards_near(plan, latents, condition, ada_weight, ada_bias, qkv_weight, qv_bias, proj_weight, proj_bias,
                           fc1_weight, fc1_bias, fc2_weight, fc2_bias, cotangent)
    row, col = lax.axis_index("row"), lax.axis_index("col")
    rows, cols, width, tokens = plan.rows, plan.cols, plan.width, plan.tokens
    depth, hc, fc = plan.depth_rows, plan.head_cols, plan.ff_cols
    heads = cols * hc // HEAD_DIM
    groups = rows * plan.lats

    blocks = [qkv_weight.reshape(depth, 3 * hc), proj_weight.T, fc1_weight, fc2_weight.T]
    qkv_w, proj_w, fc1_w, fc2_w = gather_plain(blocks)
    home = row * plan.lats + col // plan.share
    values, grad_out = latents.astype(f32), cotangent.astype(f32)

    cond_all = lax.all_gather(condition, "row", axis=0, tiled=True).astype(f32)
    cond_act = jax.nn.silu(cond_all).astype(bf16)
    cond_mine = lax.dynamic_slice(cond_act, (0, row * depth), (groups, depth))
    ada_flat = ada_weight.reshape(depth, 6 * hc)
    partial = lax.psum(nn(cond_mine, ada_flat), "row") + ada_bias.astype(f32).reshape(1, 6 * hc)
    small = jnp.concatenate(
        [partial.reshape(-1)] + [b.astype(f32).reshape(-1) for b in (proj_bias, fc2_bias, fc1_bias, qv_bias)])
    small = lax.all_gather(small, "col", axis=0, tiled=False)
    sizes = [groups * 6 * hc, hc, hc, fc, 2 * hc]
    mod_all, proj_b, fc2_b, fc1_b, qv_b = jnp.split(small, [sum(sizes[:i + 1]) for i in range(4)], axis=1)
    mod = lax.dynamic_index_in_dim(mod_all.reshape(cols, groups, 6, hc), home, 1, keepdims=False)
    mod = mod.transpose(1, 0, 2).reshape(6, 1, width)
    shift_one, scale_one, gate_one, shift_two, scale_two, gate_two = (mod[k] for k in range(6))
    proj_b, fc2_b, fc1_b = proj_b.reshape(width), fc2_b.reshape(width), fc1_b.reshape(-1)
    q_b, v_b = qv_b[:, :hc].reshape(heads, 1, HEAD_DIM), qv_b[:, hc:].reshape(heads, 1, HEAD_DIM)

    def to_heads(flat):
        return flat.reshape(tokens, heads, HEAD_DIM).transpose(1, 0, 2)

    def from_heads(value):
        return value.transpose(1, 0, 2).reshape(tokens, cols, hc)

    normal_one, inverse_one = layer_norm(values)
    normed_one = (normal_one * (1.0 + scale_one) + shift_one).astype(bf16)
    projected = nn(normed_one, qkv_w).reshape(tokens, cols, 3 * hc)
    query = (to_heads(projected[:, :, :hc]) + q_b).astype(bf16)
    key = to_heads(projected[:, :, hc:2 * hc]).astype(bf16)
    value = (to_heads(projected[:, :, 2 * hc:]) + v_b).astype(bf16)
    cuts = [[s * plan.share + i for i in range(plan.share)] for s in range(cols // plan.share)]
    key_all = lax.all_gather(key, "col", axis=1, tiled=True, axis_index_groups=cuts)
    value_all = lax.all_gather(value, "col", axis=1, tiled=True, axis_index_groups=cuts)
    att, lse = attend_plain(query, key_all, value_all)
    att_flat = from_heads(att).reshape(tokens, width)
    branch_a = nt(att_flat, proj_w) + proj_b
    middle = values + gate_one * branch_a

    normal_two, inverse_two = layer_norm(middle)
    normed_two = (normal_two * (1.0 + scale_two) + shift_two).astype(bf16)
    hidden, slope = gelu_and_slope(nn(normed_two, fc1_w) + fc1_b)
    hidden = hidden.astype(bf16)
    branch_m = nt(hidden, fc2_w) + fc2_b
    output = (middle + gate_two * branch_m).astype(bf16)

    gate_two_grad = jnp.sum(grad_out * branch_m, axis=0)
    m_grad = grad_out * gate_two
    fc2_bias_part = jnp.sum(m_grad, axis=0)
    m_low = m_grad.astype(bf16)
    fc2_grad = tn(m_low, hidden).astype(bf16)
    pre_grad = nn(m_low, fc2_w) * slope
    fc1_bias_part = jnp.sum(pre_grad, axis=0)
    pre_low = pre_grad.astype(bf16)
    fc1_grad = tn(normed_two, pre_low).astype(bf16)
    normed_two_grad = nt(pre_low, fc1_w)
    middle_part, shift_two_grad, scale_two_grad = norm_back(normed_two_grad, normal_two, inverse_two, scale_two)
    middle_grad = grad_out + middle_part
    gate_one_grad = jnp.sum(middle_grad * branch_a, axis=0)
    a_grad = middle_grad * gate_one
    proj_bias_part = jnp.sum(a_grad, axis=0)
    a_low = a_grad.astype(bf16)
    proj_grad = tn(a_low, att_flat).astype(bf16)
    att_grad = to_heads(nn(a_low, proj_w).astype(bf16))
    query_grad, key_grad, value_grad = attend_back_plain(query, key_all, value_all, lse, att_grad)
    key_grad, value_grad = (
        lax.psum_scatter(g.astype(bf16), "col", scatter_dimension=1, tiled=True, axis_index_groups=cuts).astype(f32)
        for g in (key_grad, value_grad))
    q_bias_part, v_bias_part = jnp.sum(query_grad, axis=1), jnp.sum(value_grad, axis=1)
    qkv_low = jnp.concatenate([from_heads(g.astype(bf16)) for g in (query_grad, key_grad, value_grad)], axis=2)
    qkv_low = qkv_low.reshape(tokens, 3 * width)
    qkv_grad = tn(normed_one, qkv_low).astype(bf16)
    normed_one_grad = nt(qkv_low, qkv_w)
    fc2_sum, fc1_sum, qkv_sum, proj_sum = scatter_plain([fc2_grad, fc1_grad, qkv_grad, proj_grad])
    input_part, shift_one_grad, scale_one_grad = norm_back(normed_one_grad, normal_one, inverse_one, scale_one)
    latents_grad = middle_grad + input_part

    mod_grad = jnp.stack(
        [shift_one_grad, scale_one_grad, gate_one_grad, shift_two_grad, scale_two_grad, gate_two_grad], axis=0)
    mod_grad = lax.all_gather(mod_grad, ("row", "col"), axis=0, tiled=False)
    mod_grad = mod_grad.reshape(groups, plan.share, 6, width).sum(axis=1)
    mod_mine = lax.dynamic_slice(mod_grad, (0, 0, col * hc), (groups, 6, hc))
    ada_bsum = jnp.sum(mod_mine, axis=0)
    mod_low = mod_mine.astype(bf16).reshape(groups, 6 * hc)
    ada_wsum = tn(cond_mine, mod_low).reshape(depth, 6, hc)
    cond_part = lax.dynamic_update_slice(jnp.zeros((groups, width), f32), nt(mod_low, ada_flat), (0, row * depth))
    parts = [cond_part, proj_bias_part, fc2_bias_part, q_bias_part, v_bias_part, fc1_bias_part]
    totals = lax.psum(jnp.concatenate([part.reshape(-1) for part in parts]), ("row", "col"))
    ends, spot = [], 0
    for part in parts:
        ends.append(totals[spot:spot + part.size])
        spot += part.size

    def mine(flat):
        size = flat.size // cols
        return lax.dynamic_slice(flat, (col * size,), (size,))

    cond_summed = lax.dynamic_slice(ends[0].reshape(groups, width), (row * plan.lats, 0), (plan.lats, width))
    silu_value, silu_pull = jax.vjp(jax.nn.silu, condition.astype(f32))
    condition_grad = silu_pull(cond_summed)[0]
    qv_bsum = jnp.stack([mine(ends[3]), mine(ends[4])], axis=0)
    return (
        output, latents_grad, condition_grad, ada_wsum, ada_bsum, qkv_sum.reshape(depth, 3, hc), qv_bsum,
        proj_sum.T, mine(ends[1]), fc1_sum, mine(ends[5]), fc2_sum.T, mine(ends[2]))


def solution(mesh):
    token, grid, turned = P(("row", "col"), None), P("row", "col"), P("col", "row")
    cube, wide, flat = P("row", None, "col"), P(None, "col"), P("col")
    return jax.shard_map(
        shards,
        mesh=mesh,
        in_specs=(token, P("row", None), cube, wide, cube, wide, turned, flat, grid, flat, turned, flat, token),
        out_specs=(token, token, P("row", None), cube, wide, cube, wide, turned, flat, grid, flat, turned, flat),
        check_vma=False,
    )
```

time: 883 us -> 440 us (0.50)
  matrix products: 114 us -> 0 us
  waiting for transfers between devices: 100 us -> 0 us
  blocking collectives: 83.6 us -> 0 us
  local copies, waits for them, and re-layouts: 101 us -> 29.9 us
  other arithmetic: 72.8 us -> 3.71 us
  Pallas kernels: 384 us -> 402 us
  between operations: 15.4 us -> 0.96 us
    dot_general x38 -> x0, matrix products: 114 us -> none  [the longest x13 46.4 us: nt(): lax.dot_general(a, b, (((1,), (1,)), ((), ())), preferred_element_type=f32)]
    psum x1 -> x0, waiting for transfers between devices: 100 us -> none  [finish(): lax.psum(jnp.concatenate([part.reshape(-1) for part in parts]), ('row', '...]
    all_gather x2 -> x0, blocking collectives: 83.6 us -> none  [the longest x1 78.4 us: finish(): mod_grad = lax.all_gather(mod_grad, ('row', 'col'), axis=0, tiled=False)]
    another operation x6 -> x0, other arithmetic: 23.2 us -> none  [the longest x1 12 us: shards_near(): fc1_grad = jnp.stack([tn(normed_two, u).astype(bf16) for u in pre_low])]
    unnamed x188 -> x24, local copies, waits for them, and re-layouts: 27.4 us -> 7.08 us
    reduce_sum x8 -> x0, other arithmetic: 18.9 us -> none  [the longest x1 10.5 us: shards_near(): jnp.sum(value_grad, axis=1)]
    pallas_call x2 -> x1, Pallas kernels: 187 us -> 205 us  [backward(): pl.pallas_call(backward_kernel, out_shape=outs, in_specs=[ANY] * 16 + [vm...]
    concatenate x10 -> x0, local copies, waits for them, and re-layouts: 14.9 us -> none  [the longest x6 6.83 us: shards_near(): jnp.concatenate([got[:, :qm], proj_grads[z][:, :pm], got[:, qm:] + proj_g...]
  transfers between devices with their start and end apart: 4 -> 0, of which waited for: 1 -> 0; matrix products, arithmetic and copies ran while one was open for 9% -> 0% of each run, Pallas kernels for 0% -> 0%
where the time goes in v3:
time: 440 us; the launch traced here: 436 us
  Pallas kernels  402 us (91%)
  local copies, waits for them, and re-layouts  29.9 us (7%)
    pallas_call x1, Pallas kernels, backward(): pl.pallas_call(backward_kernel, out_shape=outs, in_specs=[ANY] * 16 + [vm...  205 us
    pallas_call x1, Pallas kernels, forward(): pl.pallas_call(forward_kernel, out_shape=outs, in_specs=[ANY, ANY, vmem,...  197 us

profile of v3, /device:TPU:0, one launch (start us, length us, event | category | flops | bytes accessed | tf_op | source)
XLA Modules:
  0.0 436.3 jit_solution(5442923125217850956)
XLA Ops:
  0.6 0.0 copy-start.8
  0.7 0.1 pad.22.clone
  0.7 0.7 concatenate.23
  1.4 0.7 concatenate.24
  2.1 0.8 reshape.106
  2.9 0.7 concatenate.22
  3.5 0.1 maximum_convert_fusion
  3.6 0.8 reshape.116
  4.4 0.7 maximum_maximum_fusion.refs_4_
  5.1 0.0 copy-start.6
  5.1 1.4 pad_convert_fusion.refs_2_.refs_20_
  6.5 0.8 slice.58
  7.2 0.9 slice.61
  8.1 0.1 copy.49
  8.2 0.7 reshape.113.refs_11_
  8.9 0.0 copy-start.7
  8.9 1.0 slice.47
  9.9 0.1 copy.50
  9.9 0.7 reshape.111.refs_9_
  10.6 1.0 copy.36
  11.6 0.0 copy-start.5
  11.7 0.6 slice.57.refs_6_
  12.3 0.1 copy.37
  12.4 0.1 reshape.108
  12.5 0.1 copy.38
  12.6 0.7 reshape.109.refs_7_
  13.4 0.0 copy-done.8
  13.4 0.8 copy.46.refs_5_
  14.2 0.0 copy-done.6
  14.2 0.7 slice.60.refs_10_
  15.0 0.0 copy-done.7
  15.0 0.7 slice.46.refs_8_
  15.7 0.0 copy-done.5
  15.7 1.0 copy.41.refs_3_.refs_19_
  16.8 197.2 %forward.1 = (bf16[1152,3072]{1,0:T(8,128)(2,1)}, bf16[1152,1024]{1,0:T(8,128)(2,1)}, bf16[576,1024]{1,0:T(8,128)(2,1)}, bf16[1152,4096]{1,0:T(8,128)(2,1)}, bf1...) custom-call(bf16[512,1152]{1,0:T(8,128)(2,1)} %refs_0_.1, ...), custom_call_target="tpu_custom_call" | custom-call | tf_op jit(solution)/shard_map/forward/pallas_call | solution.py:585
  214.0 204.5 %backward.1 = (bf16[512,1152]{1,0:T(8,128)(2,1)}, bf16[512,1152]{1,0:T(8,128)(2,1)}, bf16[4,512,896]{2,1,0:T(8,128)(2,1)}, f32[288,576]{1,0:T(8,128)}, f32[288,5...) custom-call(bf16[3,4,1152,1152]{3,2,1,0:T(8,128)(2,1)} %get-tuple-el, ...), custom_call_target="tpu_custom_call" | custom-call | tf_op jit(solution)/shard_map/backward/pallas_call | solution.py:1193
  418.5 0.0 copy-start.2
  418.5 0.8 slice_reduce_fusion.2
  419.3 0.7 reshape_squeeze.7
  420.0 1.4 fusion
  421.4 1.3 slice_reduce_fusion.1
  422.8 0.8 slice_reduce_fusion
  423.5 0.7 reshape_squeeze.6
  424.2 1.4 slice.50
  425.6 1.8 copy.45
  427.4 0.0 copy-start
  427.4 2.2 copy.44
  429.6 0.0 copy-done.2
  429.6 1.5 copy.43
  431.1 0.0 copy-done
  431.1 0.0 copy-start.1
  431.1 1.6 convert_element_type.21
  432.7 0.2 copy-done.1
  432.8 0.0 copy-start.4
  432.8 0.0 copy-start.3
  432.8 1.0 copy.54
  433.8 0.5 copy-done.4
  434.4 0.9 copy.55
  435.2 0.0 copy-done.3
  435.2 0.9 copy.56
  (5 shorter events, 0.1 us)
Async XLA Ops:
  0.6 12.7 %copy-start.8 = (bf16[288,3,144]{0,2,1:T(8,128)(2,1)S(1)}, bf16[288,3,144]{0,2,1:T(8,128)(2,1)}, u32[]{:S(2)}) copy-start(bf16[288,3,144]{0,2,1:T(8,128)(2,1)} %param.17) | copy-start | bytes 746500
  5.1 9.2 %copy-start.6 = (bf16[576,288]{0,1:T(8,128)(2,1)S(1)}, bf16[576,288]{0,1:T(8,128)(2,1)}, u32[]{:S(2)}) copy-start(bf16[576,288]{0,1:T(8,128)(2,1)} %param.23) | copy-start | bytes 995332
  8.9 6.1 %copy-start.7 = (bf16[288,576]{1,0:T(8,128)(2,1)S(1)}, bf16[288,576]{1,0:T(8,128)(2,1)}, u32[]{:S(2)}) copy-start(bf16[288,576]{1,0:T(8,128)(2,1)} %param.21) | copy-start | bytes 995332
  11.6 4.1 copy-start.5
  418.5 11.1 %copy-start.2 = (f32[288,864]{1,0:T(8,128)S(1)}, f32[288,864]{1,0:T(8,128)}, u32[]{:S(2)}) copy-start(f32[288,864]{1,0:T(8,128)} %get-tuple-element.63) | copy-start | bytes 2985988
  427.4 3.7 copy-start
  431.1 1.7 copy-start.1
  432.8 1.5 copy-start.4
  432.8 2.4 copy-start.3

commit v4 on v3

--- a/solution.py
+++ b/solution.py
@@ -56,22 +56,21 @@
 
 
 class Gather:
-    sems = (1, 2, 2, 4, 8)
-
     def __init__(self, place, ins, outs, sems):
         self.at, self.ins, self.outs = place, ins, outs
-        self.local, self.zs, self.qs, self.ps, self.ks = sems
+        self.local, self.zs, self.zzs, self.qs, self.ps, self.ks = sems
+        self.early = place.h == 0
 
     @staticmethod
     def scratch(count, depth):
         dma = pltpu.SemaphoreType.DMA
-        return [dma((count,)), dma((count, 2, depth)), dma((count, 2, depth)), dma((count, 2, depth, 2)), dma((count, 2, depth, 4))]
-
-    def block(self, a, p, q, z, h=None):
+        return [dma((count,)), dma((count, 2, depth)), dma((count, 2, depth)), dma((count, 2, depth)), dma((count, 2, depth, 2)),
+                dma((count, 2, depth, 4))]
+
+    def block(self, a, p, q, z):
         y, x = self.at.yx(p, q)
         rows, lanes = self.ins[a].shape
-        h = self.at.h if h is None else h
-        return block_at(self.outs[a], rows, lanes, 2 * y + h, 2 * z + x)
+        return block_at(self.outs[a], rows, lanes, 2 * y + self.at.h, 2 * z + x)
 
     def zc(self, t):
         return (self.at.z + self.at.depth - t) % self.at.depth
@@ -81,54 +80,62 @@
             src_ref=src, dst_ref=dst, send_sem=sems.at[(index[0], 0) + index[1:]], recv_sem=sems.at[(index[0], 1) + index[1:]],
             device_id=to, device_id_type=MESH)
 
-    def own(self, a):
-        return self.block(a, self.at.p, self.at.q, self.at.z)
+    def spot(self, a, t, j=0):
+        p, q = self.at.p, self.at.q
+        return self.block(a, p if j < 2 else 1 - p, q if j % 2 == 0 else 1 - q, self.zc(t))
+
+    def source(self, a, t, j=0):
+        return self.ins[a] if t == 0 and j == 0 else self.spot(a, t, j)
 
     def c_local(self, a):
-        return pltpu.make_async_copy(self.ins[a], self.own(a), self.local.at[a])
-
-    def c_z(self, a, k):
-        place = self.at
+        return pltpu.make_async_copy(self.ins[a], self.spot(a, 0), self.local.at[a])
+
+    def c_z(self, a, k, j):
+        place, sems = self.at, (self.zs, self.zzs)[j]
         return pltpu.make_async_remote_copy(
-            src_ref=self.ins[a], dst_ref=self.own(a), send_sem=self.zs.at[a, 0, k], recv_sem=self.zs.at[a, 1, place.z],
+            src_ref=self.source(a, 0, j), dst_ref=self.spot(a, 0, j), send_sem=sems.at[a, 0, k], recv_sem=sems.at[a, 1, place.z],
             device_id=place.to_z((place.z + k) % place.depth), device_id_type=MESH)
 
-    def r_z(self, a, t):
-        place = self.at
-        here = self.block(a, place.p, place.q, self.zc(t))
+    def r_z(self, a, t, j):
+        place, sems = self.at, (self.zs, self.zzs)[j]
         return pltpu.make_async_remote_copy(
-            src_ref=self.ins[a], dst_ref=here, send_sem=self.zs.at[a, 0, 0], recv_sem=self.zs.at[a, 1, self.zc(t)],
-            device_id=place.to_z(place.z), device_id_type=MESH)
+            src_ref=self.source(a, 0, j), dst_ref=self.spot(a, t, j), send_sem=sems.at[a, 0, 0], recv_sem=sems.at[a, 1, self.zc(t)],
+            device_id=place.to_q, device_id_type=MESH)
 
     def c_q(self, a, t):
-        place = self.at
-        spot = self.block(a, place.p, place.q, self.zc(t))
-        return self.copy(self.ins[a] if t == 0 else spot, spot, self.qs, (a, self.zc(t)), place.to_q)
+        return self.copy(self.source(a, t), self.spot(a, t), self.qs, (a, self.zc(t)), self.at.to_q)
 
     def c_p(self, a, t, j):
-        place = self.at
-        spot = self.block(a, place.p, place.q if j == 0 else 1 - place.q, self.zc(t))
-        return self.copy(self.ins[a] if t == 0 and j == 0 else spot, spot, self.ps, (a, self.zc(t), j), place.to_p)
+        return self.copy(self.source(a, t, j), self.spot(a, t, j), self.ps, (a, self.zc(t), j), self.at.to_p)
 
     def c_k(self, a, t, j):
-        place = self.at
-        spot = self.block(a, place.p if j < 2 else 1 - place.p, place.q if j % 2 == 0 else 1 - place.q, self.zc(t))
-        return self.copy(self.ins[a] if t == 0 and j == 0 else spot, spot, self.ks, (a, self.zc(t), j), place.to_core)
+        return self.copy(self.source(a, t, j), self.spot(a, t, j), self.ks, (a, self.zc(t), j), self.at.to_core)
 
     def start(self, a):
+        self.c_q(a, 0).start()
         for k in range(1, self.at.depth):
-            self.c_z(a, k).start()
+            self.c_z(a, k, 0).start()
         self.c_local(a).start()
 
+    def forward(self, a):
+        @pl.when(self.early)
+        def _():
+            self.c_q(a, 0).wait_recv()
+            for k in range(1, self.at.depth):
+                self.c_z(a, k, 1).start()
+
     def stage(self, a, t, n):
+        late = jnp.logical_not(self.early)
         if n == 0:
             if t > 0:
-                self.r_z(a, t).wait_recv()
-            self.c_q(a, t).start()
+                self.r_z(a, t, 0).wait_recv()
+                pl.when(late)(self.c_q(a, t).start)
             self.c_p(a, t, 0).start()
             self.c_k(a, t, 0).start()
         elif n == 1:
-            self.c_q(a, t).wait_recv()
+            pl.when(late)(self.c_q(a, t).wait_recv)
+            if t > 0:
+                pl.when(self.early)(self.r_z(a, t, 1).wait_recv)
             self.c_p(a, t, 1).start()
             self.c_k(a, t, 1).start()
         elif n == 2:
@@ -144,10 +151,132 @@
                 self.c_k(a, t, j).wait_recv()
 
     def finish(self, a):
+        self.c_q(a, 0).wait_send()
         for k in range(1, self.at.depth):
-            self.c_z(a, k).wait_send()
+            self.c_z(a, k, 0).wait_send()
+
+        @pl.when(self.early)
+        def _():
+            for k in range(1, self.at.depth):
+                self.c_z(a, k, 1).wait_send()
+
+        @pl.when(jnp.logical_not(self.early))
+        def _():
+            for t in range(1, self.at.depth):
+                self.c_q(a, t).wait_send()
+
         for t in range(self.at.depth):
-            self.c_q(a, t).wait_send()
+            for j in range(2):
+                self.c_p(a, t, j).wait_send()
+            for j in range(4):
+                self.c_k(a, t, j).wait_send()
+
+
+class LineGather(Gather):
+    def __init__(self, place, ins, outs, sems, mid=()):
+        super().__init__(place, ins, outs, sems)
+        z = place.z
+        self.core0, self.mid = place.h == 0, mid
+        self.middle = jnp.logical_and(z > 0, z < place.depth - 1)
+        low = z < 2
+        self.inner = place.to_z(jnp.where(low, z + 1, z - 1))
+        self.outer = place.to_z(jnp.where(low, jnp.maximum(z - 1, 0), jnp.minimum(z + 1, place.depth - 1)))
+        self.order = [z, z + 1 - 2 * (z % 2), jnp.where(low, 2, 1), jnp.where(low, 3, 0)]
+
+    @staticmethod
+    def scratch(count, depth):
+        dma = pltpu.SemaphoreType.DMA
+        return [dma((count,)), dma((count, 2, 5)), dma((count, 2, 5)), dma((count, 2, depth)), dma((count, 2, depth, 2)),
+                dma((count, 2, depth, 4))]
+
+    def early(self, a):
+        return self.core0 if a in self.mid else jnp.logical_and(self.core0, False)
+
+    def zc(self, t):
+        return self.order[t]
+
+    def c_z(self, a, t, j, n):
+        sems = (self.zs, self.zzs)[j]
+        return pltpu.make_async_remote_copy(
+            src_ref=self.source(a, t, j), dst_ref=self.spot(a, t, j), send_sem=sems.at[a, 0, n], recv_sem=sems.at[a, 1, self.zc(t)],
+            device_id=self.inner if n in (0, 2) else self.outer, device_id_type=MESH)
+
+    def z_start(self, a, j):
+        self.c_z(a, 0, j, 0).start()
+        pl.when(self.middle)(self.c_z(a, 0, j, 1).start)
+
+    def z_got(self, a, t, j):
+        self.c_z(a, t, j, 0).wait_recv()
+        pl.when(self.middle)(self.c_z(a, t, j, 1 + t).start)
+
+    def z_sent(self, a, j):
+        self.c_z(a, 0, j, 0).wait_send()
+
+        @pl.when(self.middle)
+        def _():
+            self.c_z(a, 0, j, 1).wait_send()
+            for t in range(1, self.at.depth):
+                self.c_z(a, t, j, 1 + t).wait_send()
+
+    def start(self, a):
+        self.c_q(a, 0).start()
+        self.z_start(a, 0)
+        self.c_local(a).start()
+
+    def forward(self, a):
+        if a in self.mid:
+            @pl.when(self.core0)
+            def _():
+                self.c_q(a, 0).wait_recv()
+                self.z_start(a, 1)
+
+    def stage(self, a, t, n):
+        mid, early = a in self.mid, self.core0
+        late = jnp.logical_not(early)
+        if n == 0:
+            if t > 0:
+                self.z_got(a, t, 0)
+                if mid:
+                    pl.when(late)(self.c_q(a, t).start)
+                else:
+                    self.c_q(a, t).start()
+            self.c_p(a, t, 0).start()
+            self.c_k(a, t, 0).start()
+        elif n == 1:
+            if not mid:
+                self.c_q(a, t).wait_recv()
+            else:
+                pl.when(late)(self.c_q(a, t).wait_recv)
+                if t > 0:
+                    pl.when(early)(lambda: self.z_got(a, t, 1))
+            self.c_p(a, t, 1).start()
+            self.c_k(a, t, 1).start()
+        elif n == 2:
+            self.c_p(a, t, 0).wait_recv()
+            self.c_k(a, t, 2).start()
+        elif n == 3:
+            self.c_p(a, t, 1).wait_recv()
+            self.c_k(a, t, 3).start()
+        else:
+            if t == 0:
+                self.c_local(a).wait()
+            for j in range(4):
+                self.c_k(a, t, j).wait_recv()
+
+    def finish(self, a):
+        self.c_q(a, 0).wait_send()
+        self.z_sent(a, 0)
+
+        def rest():
+            for t in range(1, self.at.depth):
+                self.c_q(a, t).wait_send()
+
+        if a in self.mid:
+            pl.when(self.core0)(lambda: self.z_sent(a, 1))
+            pl.when(jnp.logical_not(self.core0))(rest)
+        else:
+            rest()
+        for t in range(self.at.depth):
             for j in range(2):
                 self.c_p(a, t, j).wait_send()
             for j in range(4):
@@ -232,7 +361,7 @@
     (o_w, o_cot, o_x, o_n1, o_q, o_k, o_v, o_k2, o_v2, o_lse, o_att, o_ba, o_mid, o_n2, o_hid, o_slo, o_out, o_vec, o_act), refs = refs[:19], refs[19:]
     (x_v, n1, q_v, k_v, v_v, k2_v, v2_v, lse_v, ot, att, ba, mid, n2, hid, slo, acc, wbuf, lbuf, out_v, cot_v, vec,
      c_send, c_recv, s_send, s_recv, m_own, m_oth), refs = refs[:27], refs[27:]
-    ag_sems, (swap_sems, c_sems, s_sems, m_sems, o_sems, kv_sems, w_sems, save_sems, wsave_sems) = refs[:5], refs[5:]
+    ag_sems, (swap_sems, c_sems, s_sems, m_sems, o_sems, kv_sems, w_sems, save_sems, wsave_sems) = refs[:6], refs[6:]
 
     place = Place()
     depth, rows_n = place.depth, 4
@@ -270,7 +399,7 @@
     swap_x = Swap(place, lat, x_v, swap_sems, 0)
     swap_x.start()
 
-    work = Gather(place, blocks, fulls, ag_sems)
+    work = LineGather(place, blocks, fulls, ag_sems, range(7))
     for a in range(3):
         work.start(a)
 
@@ -279,14 +408,21 @@
         members.append(list(range(first, first + size)))
         first += size
     chunks = [(g, t) for g in range(len(GROUPS)) for t in range(depth)]
-    events = [(s - n, n) for s in range(len(chunks) + 4) for n in range(5) if 0 <= s - n < len(chunks)]
+    events = []
+    for s in range(len(chunks) + 4):
+        if s % depth == 2 and s < 2 * depth:
+            events.append((s // depth + 1, "start"))
+        if s in (1, 3, depth + 3):
+            events.append(((s + 1) // depth, "forward"))
+        events += [(s - n, n) for n in range(5) if 0 <= s - n < len(chunks)]
     at = [0]
 
     def pump(count):
         for s, n in events[at[0]:at[0] + count]:
-            if n == 0 and s in (2, depth + 2):
-                for a in members[1 if s == 2 else 2]:
-                    work.start(a)
+            if n in ("start", "forward"):
+                for a in members[s]:
+                    (work.start if n == "start" else work.forward)(a)
+                continue
             g, t = chunks[s]
             for a in members[g]:
                 work.stage(a, t, n)
@@ -578,7 +714,7 @@
         vm((depth, tokens, lanes), bf16), vm((tokens, width), f32), vm((depth, width, lanes), bf16), vm((2, width // 2, 256), bf16),
         t16, t16, vm((VECS, width), f32), vm((rows, 8, drows), f32), vm((rows, 8, drows), f32), vm((rows, 8, hc6), f32),
         vm((rows, 8, hc6), f32), vm((cols, 8, hc6), f32), vm((cols, 8, hc6), f32)]
-    scratch += Gather.scratch(len(blocks), depth)
+    scratch += LineGather.scratch(len(blocks), depth)
     scratch += [dma((2, 2)), dma((2, rows)), dma((2, rows)), dma((2, cols)), dma((2,)), dma((2, 2, heads)), dma((2, 3)), dma((32,)),
                 dma((3 * depth,))]
     vmem = pl.BlockSpec(memory_space=pltpu.VMEM)
@@ -594,14 +730,17 @@
     return got[len(blocks):]
 
 
+SLOTS = 4
+
+
 def backward_kernel(*refs):
     (w, dy_h, x_h, n1_h, q_h, k_h, v_h, k2_h, v2_h, att_h, ba_h, mid_h, n2_h, hid_h, slo_h, out_h), refs = refs[:16], refs[16:]
     (lse, vec, act, ada, cond), refs = refs[:5], refs[5:]
     (o_out, o_lat, o_pq, o_fc2, o_fc1, o_qkv, o_proj, o_ada, o_rows, o_cond), refs = refs[:10], refs[10:]
     (acc, give, r0, r1, r1l, r2, r2l, r3, r3l, lf, lx), refs = refs[:11], refs[11:]
-    (wbuf, hs, pre, pq, turn, tmp, ml, gm, gx, slo, att, heads, grad_o, delta, kv_give, kv_got, own, gv), refs = refs[:18], refs[18:]
+    (wbuf, hs, pre, pq, turn, tmp, ml, gm, gx, att, heads, grad_o, delta, kv_give, kv_got, own, gv, att_w), refs = refs[:18], refs[18:]
     (tt, tc, um, vm_, modl, cp, cr, cf), refs = refs[:8], refs[8:]
-    (swap_sems, s0, s1, s2, s3, lx_sems, w_sems, hs_sems, slo_sems, tmp_sems, head_sems, kv_sems, pq_sems, t_sems, u_sems, v_sems, cr_sems, cf_sems) = refs
+    (swap_sems, s0, s1, s2, s3, lx_sems, w_sems, hs_sems, slo_sems, tmp_sems, head_sems, kv_sems, pq_sems, t_sems, u_sems, v_sems, cr_sems, cf_sems, att_sems) = refs
 
     place = Place()
     depth, rows_n = place.depth, 4
@@ -633,8 +772,14 @@
         def _(i):
             body(pl.ds(pl.multiple_of(i * half, half), half))
 
+    low = place.z < 2
+    middle = jnp.logical_and(place.z > 0, place.z < depth - 1)
+    inner = place.to_z(jnp.where(low, place.z + 1, place.z - 1))
+    outer = place.to_z(jnp.where(low, jnp.maximum(place.z - 1, 0), jnp.minimum(place.z + 1, depth - 1)))
+    far = [jnp.where(low, 3, 0), jnp.where(low, 2, 1), place.z + 1 - 2 * (place.z % 2), place.z]
+
     def zc(t):
-        return lax.rem(place.z + 1 + t, depth)
+        return far[t]
 
     def load(src, i):
         copy = pltpu.make_async_copy(src, tmp.at[i], tmp_sems.at[i])
@@ -645,7 +790,7 @@
         return pltpu.make_async_copy(w.at[2 - u // depth, zc(u % depth)], wbuf.at[u % 2], w_sems.at[u % 2])
 
     def slope_load(u):
-        return pltpu.make_async_copy(slo_h.at[zc(u)], slo.at[u % 2], slo_sems.at[u % 2])
+        return pltpu.make_async_copy(slo_h.at[zc(u)], pre.at[zc(u)], slo_sems.at[u])
 
     def weight_use(u):
         weight_load(u).wait()
@@ -660,13 +805,22 @@
         if g == 1:
             return []
         return [pltpu.make_async_copy(o_pq.at[zc(t)], hs.at[s % 2, :, :896], hs_sems.at[s % 2, 0]),
-                pltpu.make_async_copy(att_h.at[zc(t)], att.at[s % 2], hs_sems.at[s % 2, 1])]
+                pltpu.make_async_copy(att_h.at[zc(t)], att_w.at[s % 2], hs_sems.at[s % 2, 1])]
 
     def tick_prefetch(s):
         if s < 3 * depth:
+            if s // depth == 2:
+                pq_wait(s % depth)
             for copy in tick_loads(s):
                 copy.start()
 
+    saved = set()
+
+    def pq_wait(t):
+        if t not in saved:
+            saved.add(t)
+            pq_save(t).wait()
+
     def pq_save(t):
         return pltpu.make_async_copy(pq, o_pq.at[zc(t)], pq_sems.at[t])
 
@@ -674,8 +828,8 @@
         return send(give.at[s % 2, y], r0.at[s % 2, y], s0.at[0, s % 2, y], s0.at[1, s % 2, y], place.to_core)
 
     def spots(s, y, x):
-        return (acc.at[s % 4, y, :, pl.ds(pl.multiple_of(x * 512, 512), 512)],
-                acc.at[s % 4, y, pl.ds(pl.multiple_of(x * lrows, 16), lrows), 1024:1152])
+        return (acc.at[s % SLOTS, y, :, pl.ds(pl.multiple_of(x * 512, 512), 512)],
+                acc.at[s % SLOTS, y, pl.ds(pl.multiple_of(x * lrows, 16), lrows), 1024:1152])
 
     def c1(s, j):
         main, left = spots(s, *place.yx(1 - place.p, j))
@@ -683,18 +837,84 @@
         return [send(main, r1.at[k, j], s1.at[0, k, j, 0], s1.at[1, k, j, 0], place.to_p),
                 send(left, r1l.at[k, j], s1.at[0, k, j, 1], s1.at[1, k, j, 1], place.to_p)]
 
+    zq = h == 0
+    qz = jnp.logical_not(zq)
+
     def c2(s):
         main, left = spots(s, *place.yx(place.p, 1 - place.q))
-        k = s % 4
+        k = jnp.where(zq, s // depth, s % 4) if s % depth == depth - 1 else s % 4
         return [send(main, r2.at[k], s2.at[0, k, 0], s2.at[1, k, 0], place.to_q),
                 send(left, r2l.at[k], s2.at[0, k, 1], s2.at[1, k, 1], place.to_q)]
 
-    def c3(s):
+    def z_copy(s, j, inward, slot):
         g, t = s // depth, s % depth
-        main, left = spots(s, *place.yx(place.p, place.q))
-        to = place.to_z(zc(t))
-        return [send(main, r3.at[g, t], s3.at[0, g, t, 0], s3.at[1, g, t, 0], to),
-                send(left, r3l.at[g, t], s3.at[0, g, t, 1], s3.at[1, g, t, 1], to)]
+        main, left = spots(s, *place.yx(place.p, place.q if j == 0 else 1 - place.q))
+        to = inner if inward else outer
+        return [send(main, r3.at[j, slot], s3.at[0, j, g, t, 0], s3.at[1, j, slot, 0, 0], to),
+                send(left, r3l.at[j, slot], s3.at[0, j, g, t, 1], s3.at[1, j, slot, 0, 1], to)]
+
+    def z_stage(s, j, inside):
+        g, t = s // depth, s % depth
+        par = g % 2
+        if t == depth - 1:
+            return
+        if inside:
+            slot = (par, 2, 3 + par)[t]
+            for copy in z_copy(s, j, True, slot):
+                copy.wait_recv()
+            for into, other in zip(spots(s, *place.yx(place.p, place.q if j == 0 else 1 - place.q)), (r3.at[j, slot], r3l.at[j, slot])):
+                add_into(into, other)
+            copies = z_copy(s, j, t < 2, (3 + par, 5 + par, 5 + par)[t])
+        else:
+            copies = z_copy(s, j, True, (par, 2, 7 + par)[t])
+        for copy in copies:
+            copy.start()
+
+    def z_stages(s, twice, inside):
+        where = jnp.logical_and(zq if twice else qz, middle if inside else jnp.logical_not(middle))
+
+        @pl.when(where)
+        def _():
+            z_stage(s, 0, inside)
+            if twice:
+                z_stage(s, 1, inside)
+
+    def z_got(g, j):
+        par = g % 2
+        last = (g + 1) * depth - 1
+        for copy in z_copy(last, j, True, 5 + par):
+            copy.wait_recv()
+
+        @pl.when(middle)
+        def _():
+            for copy in z_copy(last, j, True, 7 + par):
+                copy.wait_recv()
+
+    def z_sum(g, j, value, refs, index):
+        par = g % 2
+        value = value + refs[(j, 5 + par) + index].astype(f32)
+        return jnp.where(middle, value + refs[(j, 7 + par) + index].astype(f32), value)
+
+    def sent(s):
+        for j in range(2):
+            for copy in c1(s, j):
+                copy.wait_send()
+        if s % depth < depth - 1:
+            for copy in z_copy(s, 0, True, 0):
+                copy.wait_send()
+
+            @pl.when(zq)
+            def _():
+                for copy in z_copy(s, 1, True, 0):
+                    copy.wait_send()
+
+            @pl.when(qz)
+            def _():
+                for copy in c2(s):
+                    copy.wait_send()
+        else:
+            for copy in c2(s):
+                copy.wait_send()
 
     def add_into(into, other):
         n = into.shape[0]
@@ -706,16 +926,9 @@
 
     def tick_a(s):
         g, t = s // depth, s % depth
-        k = s % 4
-        if s >= 4:
-            for j in range(2):
-                for copy in c1(s - 4, j):
-                    copy.wait_send()
-            for copy in c2(s - 4):
-                copy.wait_send()
-            if (s - 4) % depth < depth - 1:
-                for copy in c3(s - 4):
-                    copy.wait_send()
+        k = s % SLOTS
+        if s >= SLOTS:
+            sent(s - SLOTS)
         if s >= 2:
             for y in range(2):
                 c0(s - 2, y).wait_send()
@@ -729,7 +942,7 @@
             if g == 1:
                 return nn(turn[0, at_rows, :], pre[zc(t)]).astype(bf16)
             one = nn(turn[1, at_rows, :], hs[s % 2, :, :896])
-            two = nn(turn[0, at_rows, :], att[s % 2])
+            two = nn(turn[0, at_rows, :], att_w[s % 2])
             return jnp.concatenate(
                 [one[:, :q_main], two[:, :p_main], one[:, q_main:2 * q_main], two[:, p_main:2 * p_main],
                  one[:, 2 * q_main:] + two[:, 2 * p_main:]], axis=1).astype(bf16)
@@ -741,9 +954,18 @@
 
         for y in range(2):
             c0(s, y).start()
-        tick_prefetch(s + 1)
+        if s + 1 < 3 * depth - 1:
+            tick_prefetch(s + 1)
 
     def tick_b(s):
+        if s < 3 * depth:
+            for y in range(2):
+                c0(s, y).wait_recv()
+            for y in range(2):
+                add_into(acc.at[s % SLOTS, y], r0.at[s % 2, y])
+            for j in range(2):
+                for copy in c1(s, j):
+                    copy.start()
         if 0 <= s - 1 < 3 * depth:
             n = s - 1
             for j in range(2):
@@ -751,58 +973,80 @@
                     copy.wait_recv()
             for into, other in zip(spots(n, *place.yx(place.p, 1 - place.q)), (r1.at[n % 4, 1 - place.q], r1l.at[n % 4, 1 - place.q])):
                 add_into(into, other)
-            for copy in c2(n):
-                copy.start()
+
+            @pl.when(qz)
+            def _():
+                for copy in c2(n):
+                    copy.start()
+
             for into, other in zip(spots(n, *place.yx(place.p, place.q)), (r1.at[n % 4, place.q], r1l.at[n % 4, place.q])):
                 add_into(into, other)
-        if s < 3 * depth:
-            for y in range(2):
-                c0(s, y).wait_recv()
-            for y in range(2):
-                add_into(acc.at[s % 4, y], r0.at[s % 2, y])
-            for j in range(2):
-                for copy in c1(s, j):
-                    copy.start()
+            z_stages(n, True, False)
         if 0 <= s - 2 < 3 * depth:
             n = s - 2
-            for copy in c2(n):
-                copy.wait_recv()
-            for into, other in zip(spots(n, *place.yx(place.p, place.q)), (r2.at[n % 4], r2l.at[n % 4])):
-                add_into(into, other)
-            if n % depth < depth - 1:
-                for copy in c3(n):
-                    copy.start()
-        if 0 <= s - 3 < 3 * depth and (s - 3) % depth == depth - 1:
-            total((s - 3) // depth)
-
-    def left_copy(g):
-        return send(lf.at[g], lx.at[g], lx_sems.at[0, g], lx_sems.at[1, g], flip_x)
-
-    def total(g):
-        last = (g + 1) * depth - 1
-        for t in range(depth - 1):
-            for copy in c3(g * depth + t):
-                copy.wait_recv()
-        main, left = spots(last, *place.yx(place.p, place.q))
+
+            @pl.when(qz)
+            def _():
+                for copy in c2(n):
+                    copy.wait_recv()
+                for into, other in zip(spots(n, *place.yx(place.p, place.q)), (r2.at[n % 4], r2l.at[n % 4])):
+                    add_into(into, other)
+
+            z_stages(n, False, False)
+            z_stages(n, True, True)
+            if n % depth == depth - 1:
+                pl.when(zq)(lambda: hand_over(n))
+        if 0 <= s - 3 < 3 * depth:
+            z_stages(s - 3, False, True)
+            if (s - 3) % depth == depth - 1:
+                total((s - 3) // depth)
+
+    def hand_over(n):
+        g = n // depth
+        z_got(g, 1)
+        main, left = spots(n, *place.yx(place.p, 1 - place.q))
 
         @pl.loop(0, drows // 48)
         def _(i):
             at_rows = pl.ds(pl.multiple_of(i * 48, 16), 48)
-            value = main[at_rows, :].astype(f32)
-            for t in range(depth - 1):
-                value = value + r3[g, t, at_rows, :].astype(f32)
-            if g == 0:
-                o_fc2[at_rows, :512] = value
-            elif g == 1:
-                o_fc1[at_rows, :512] = value
-            else:
-                o_qkv[at_rows, :q_main] = value[:, :q_main]
-                o_proj[at_rows, :p_main] = value[:, q_main:]
-
-        value = left[...].astype(f32)
-        for t in range(depth - 1):
-            value = value + r3l[g, t].astype(f32)
-        lf[g] = value
+            main[at_rows, :] = z_sum(g, 1, main[at_rows, :].astype(f32), r3, (at_rows,)).astype(bf16)
+
+        left[...] = z_sum(g, 1, left[...].astype(f32), r3l, ()).astype(bf16)
+        for copy in c2(n):
+            copy.start()
+
+    def left_copy(g):
+        return send(lf.at[g], lx.at[g], lx_sems.at[0, g], lx_sems.at[1, g], flip_x)
+
+    def total(g):
+        last = (g + 1) * depth - 1
+        z_got(g, 0)
+        main, left = spots(last, *place.yx(place.p, place.q))
+
+        def write(handed):
+            if handed:
+                for copy in c2(last):
+                    copy.wait_recv()
+
+            @pl.loop(0, drows // 48)
+            def _(i):
+                at_rows = pl.ds(pl.multiple_of(i * 48, 16), 48)
+                value = z_sum(g, 0, main[at_rows, :].astype(f32), r3, (at_rows,))
+                if handed:
+                    value = value + r2[g, at_rows, :].astype(f32)
+                if g == 0:
+                    o_fc2[at_rows, :512] = value
+                elif g == 1:
+                    o_fc1[at_rows, :512] = value
+                else:
+                    o_qkv[at_rows, :q_main] = value[:, :q_main]
+                    o_proj[at_rows, :p_main] = value[:, q_main:]
+
+            value = z_sum(g, 0, left[...].astype(f32), r3l, ())
+            lf[g] = value + r2l[g].astype(f32) if handed else value
+
+        pl.when(zq)(lambda: write(True))
+        pl.when(qz)(lambda: write(False))
         left_copy(g).start()
 
     def left_finish(g):
@@ -829,7 +1073,8 @@
     swap_out = Swap(place, out_h, o_out, swap_sems, 0)
     load_dy = load(dy_h, 0)
     weight_load(0).start()
-    slope_load(0).start()
+    for u in range(depth):
+        slope_load(u).start()
     tick_prefetch(0)
     swap_out.start()
     gv[...] = jnp.zeros_like(gv)
@@ -849,13 +1094,11 @@
         z = zc(u)
         weight_use(u)
         slope_load(u).wait()
-        if u + 1 < depth:
-            slope_load(u + 1).start()
         sums = gv.at[8:9, :]
         sums[...] = jnp.zeros((1, width), f32)
 
         def body(at_rows):
-            grad = nn(ml[at_rows, :], wbuf[u % 2]) * slo[u % 2, at_rows, :].astype(f32)
+            grad = nn(ml[at_rows, :], wbuf[u % 2]) * pre[z, at_rows, :].astype(f32)
             sums[...] += jnp.sum(grad, axis=0, keepdims=True)
             pre[z, at_rows, :] = grad.astype(bf16)
 
@@ -881,16 +1124,16 @@
     hidden_back(0)
     tick_b(0)
     hidden_back(1)
+    hidden_back(2)
     tick_a(1)
-    hidden_back(2)
+    hidden_back(3)
     tick_b(1)
-    hidden_back(3)
-    for u in range(depth, 2 * depth):
-        if u == depth + 1:
-            tick_a(2)
-        if u == depth + 3:
-            tick_b(2)
-        normed_back(u)
+    normed_back(depth)
+    normed_back(depth + 1)
+    tick_a(2)
+    normed_back(depth + 2)
+    tick_b(2)
+    normed_back(depth + 3)
 
     load_mid = pltpu.make_async_copy(mid_h, gm, tmp_sems.at[2])
     load_mid.start()
@@ -924,7 +1167,7 @@
                 for i, src in enumerate((q_h, k_h, v_h, k2_h, v2_h))]
 
     def att_load(t):
-        return pltpu.make_async_copy(att_h.at[zc(t)], att.at[t % 2], hs_sems.at[t % 2, 1])
+        return pltpu.make_async_copy(att_h.at[zc(t)], att, att_sems.at[0])
 
     def kv_swap(t, kind, i):
         return send(kv_give.at[kind, i], kv_got.at[t % 2, kind, i], kv_sems.at[0, 0, kind, i], kv_sems.at[1, t % 2, kind, i], place.to_core)
@@ -940,7 +1183,7 @@
 
         def body(at_rows):
             grads = nn(ml[at_rows, :], wbuf[u % 2, :, 2 * q_main:])
-            results = att[t % 2, at_rows, :].astype(f32)
+            results = att[at_rows, :].astype(f32)
             for j in range(2):
                 grad = pair_of(grads, j).astype(bf16)
                 product = (grad.astype(f32) * pair_of(results, j)).T
@@ -985,7 +1228,7 @@
             for i in range(4):
                 kv_swap(t, kind, i).wait()
         if t > 0:
-            pq_save(t - 1).wait()
+            pq_wait(t - 1)
 
         def body(at_rows):
             for j in range(2):
@@ -1021,29 +1264,29 @@
     tick_a(3)
     load_n2.wait()
     turn_into(0, tmp.at[0])
+    load_x, load_n1 = load(x_h, 0), load(n1_h, 1)
+    tick_b(3)
     attention_open(0)
-    tick_b(3)
     attention_heads(0, [(1, lambda: tick_a(4)), (3, lambda: tick_b(4))])
     attention_close(0)
     attention_open(1)
     tick_a(5)
-    attention_heads(1, [(0, lambda: tick_b(5)), (2, lambda: tick_a(6))])
+    attention_heads(1, [(0, lambda: tick_b(5)), (2, lambda: tick_a(6)), (3, lambda: tick_b(6))])
     attention_close(1)
-    tick_b(6)
-    attention_open(2)
-    attention_heads(2, [(1, lambda: tick_a(7))])
-    load_x, load_n1 = load(x_h, 0), load(n1_h, 1)
-    tick_b(7)
+    tick_a(7)
     load_n1.wait()
     turn_into(1, tmp.at[1])
     turn_into(0, ml)
+    attention_open(2)
+    attention_heads(2, [(0, lambda: tick_b(7)), (2, lambda: tick_a(8))])
+    tick_b(8)
     attention_close(2)
     attention_open(3)
-    tick_a(8)
-    attention_heads(3, [(1, lambda: tick_b(8))])
+    tick_a(9)
+    attention_heads(3, [(0, lambda: tick_b(9)), (2, lambda: tick_a(10))])
+    tick_b(10)
     attention_close(3)
-    pq_save(3).wait()
-    tick_a(9)
+    tick_prefetch(11)
     load_x.wait()
 
     def third(at_rows):
@@ -1053,6 +1296,7 @@
     row_parts(third)
     swap_lat = Swap(place, tmp.at[1], o_lat, swap_sems, 1)
     swap_lat.start()
+    tick_a(11)
 
     for c in range(cols_n):
         spot = slice(c * hc, (c + 1) * hc)
@@ -1062,7 +1306,7 @@
         tt[c, 1:2, 576 + hc:] = gv[7:8, spot]
     copy_t = send(tt, tc, t_sems.at[0], t_sems.at[1], place.to_core)
     copy_t.start()
-    tick_b(9)
+    tick_b(11)
     copy_t.wait()
     tt[...] = tt[...] + tc[...]
 
@@ -1077,12 +1321,12 @@
     for k in range(1, cols_n):
         u_copy(k).start()
     um[col] = tt[col]
-    tick_a(10)
+    tick_b(12)
     for k in range(1, cols_n):
         u_got(k).wait_recv()
     copy_v = send(um, vm_, v_sems.at[0], v_sems.at[1], flip_y)
     copy_v.start()
-    tick_b(10)
+    tick_b(13)
     copy_v.wait_recv()
     modl[...] = jnp.zeros_like(modl)
     sums = um[0] + vm_[0]
@@ -1105,8 +1349,9 @@
 
     for k in range(1, cols_n):
         cr_copy(k).start()
-    tick_a(11)
-    tick_b(11)
+    tick_b(14)
+    left_finish(0)
+    left_finish(1)
     for k in range(1, cols_n):
         cr_got(k).wait_recv()
         cr_copy(k).wait_send()
@@ -1124,7 +1369,7 @@
     for k in range(1, rows_n):
         cf_copy(k).start()
     cf[row] = cp[row]
-    tick_b(12)
+    left_finish(2)
     for k in range(1, rows_n):
         cf_got(k).wait_recv()
     cond_value = cond[...]
@@ -1133,21 +1378,9 @@
     for r in range(rows_n):
         spot = slice(r * drows, (r + 1) * drows)
         o_cond[:, spot] = cf[r] * slope[:, spot]
-    tick_b(13)
-    left_finish(0)
-    left_finish(1)
-    tick_b(14)
-    left_finish(2)
-
-    for s in range(3 * depth - 4, 3 * depth):
-        for j in range(2):
-            for copy in c1(s, j):
-                copy.wait_send()
-        for copy in c2(s):
-            copy.wait_send()
-        if s % depth < depth - 1:
-            for copy in c3(s):
-                copy.wait_send()
+
+    for s in range(3 * depth - SLOTS, 3 * depth):
+        sent(s)
     for s in range(3 * depth - 2, 3 * depth):
         for y in range(2):
             c0(s, y).wait_send()
@@ -1175,20 +1408,20 @@
             shape((8, width), f32)]
     head = (tokens, HEAD_DIM)
     scratch = [
-        vm((4, 2, drows, lanes), bf16), vm((2, 2, drows, lanes), bf16), vm((2, 2, drows, lanes), bf16),
+        vm((SLOTS, 2, drows, lanes), bf16), vm((2, 2, drows, lanes), bf16), vm((2, 2, drows, lanes), bf16),
         vm((4, 2, drows, 512), bf16), vm((4, 2, lrows, 128), bf16), vm((4, drows, 512), bf16), vm((4, lrows, 128), bf16),
-        vm((3, depth - 1, drows, 512), bf16), vm((3, depth - 1, lrows, 128), bf16), vm((3, lrows, 128), f32), vm((3, lrows, 128), f32),
+        vm((2, 9, drows, 512), bf16), vm((2, 9, lrows, 128), bf16), vm((3, lrows, 128), f32), vm((3, lrows, 128), f32),
         vm((2, width, lanes), bf16), vm((2, tokens, lanes), bf16), vm((depth, tokens, lanes), bf16), vm((tokens, 896), bf16),
         vm((2, width, tokens), bf16), vm((2, tokens, width), bf16), vm((tokens, width), bf16), vm((tokens, width), f32),
-        vm((tokens, width), f32), vm((2, tokens, lanes), bf16), vm((2, tokens, 384), bf16), vm((5, 4) + head, bf16),
+        vm((tokens, width), f32), vm((tokens, 384), bf16), vm((5, 4) + head, bf16),
         vm((4,) + head, bf16), vm((4, 1, tokens), f32), vm((2, 4) + head, bf16), vm((2, 2, 4) + head, bf16), vm((3, 4) + head, f32),
-        vm((16, width), f32),
+        vm((16, width), f32), vm((2, tokens, 384), bf16),
         vm((cols, 8, hc6), f32), vm((cols, 8, hc6), f32), vm((cols, 8, hc6), f32), vm((cols, 8, hc6), f32), vm((rows, 8, hc6), f32),
         vm((rows, 8, drows), f32), vm((cols, rows, 8, drows), f32), vm((rows, 8, drows), f32)]
     scratch += [
-        dma((2, 2)), dma((2, 2, 2)), dma((2, 4, 2, 2)), dma((2, 4, 2)), dma((2, 3, depth, 2)), dma((2, 3)), dma((2,)), dma((2, 2)),
-        dma((2,)), dma((3,)), dma((5,)), dma((2, 2, 2, 4)), dma((depth,)), dma((2,)), dma((2, cols)), dma((2,)), dma((2, cols)),
-        dma((2, rows))]
+        dma((2, 2)), dma((2, 2, 2)), dma((2, 4, 2, 2)), dma((2, 4, 2)), dma((2, 2, 9, depth, 2)), dma((2, 3)), dma((2,)), dma((2, 2)),
+        dma((depth,)), dma((3,)), dma((5,)), dma((2, 2, 2, 4)), dma((depth,)), dma((2,)), dma((2, cols)), dma((2,)), dma((2, cols)),
+        dma((2, rows)), dma((2,))]
     vmem = pl.BlockSpec(memory_space=pltpu.VMEM)
     return pl.pallas_call(
         backward_kernel,

time: 440 us -> 411 us (0.934)
  Pallas kernels: 402 us -> 371 us
    pallas_call x1, Pallas kernels: 205 us -> 188 us  [backward(): pl.pallas_call(backward_kernel, out_shape=outs, in_specs=[ANY] * 16 + [vm...]
    pallas_call x1, Pallas kernels: 197 us -> 183 us  [forward(): pl.pallas_call(forward_kernel, out_shape=outs, in_specs=[ANY, ANY, vmem,...]
where the time goes in v4:
time: 411 us; the launch traced here: 406 us
  Pallas kernels  371 us (90%)
  local copies, waits for them, and re-layouts  29.9 us (7%)
    pallas_call x1, Pallas kernels, backward(): pl.pallas_call(backward_kernel, out_shape=outs, in_specs=[ANY] * 16 + [vm...  188 us
    pallas_call x1, Pallas kernels, forward(): pl.pallas_call(forward_kernel, out_shape=outs, in_specs=[ANY, ANY, vmem,...  183 us

profile of v4, /device:TPU:0, one launch (start us, length us, event | category | flops | bytes accessed | tf_op | source)
XLA Modules:
  0.0 405.7 jit_solution(17209082081751636375)
XLA Ops:
  0.6 0.0 copy-start.8
  0.7 0.1 pad.22.clone
  0.7 0.7 concatenate.23
  1.4 0.7 concatenate.24
  2.1 0.8 reshape.106
  2.9 0.7 concatenate.22
  3.5 0.1 maximum_convert_fusion
  3.6 0.8 reshape.116
  4.4 0.7 maximum_maximum_fusion.refs_4_
  5.1 0.0 copy-start.6
  5.1 1.4 pad_convert_fusion.refs_2_.refs_20_
  6.5 0.8 slice.58
  7.2 0.9 slice.61
  8.1 0.1 copy.49
  8.2 0.7 reshape.113.refs_11_
  8.9 0.0 copy-start.7
  8.9 1.0 slice.47
  9.9 0.1 copy.50
  9.9 0.7 reshape.111.refs_9_
  10.6 1.0 copy.36
  11.6 0.0 copy-start.5
  11.7 0.6 slice.57.refs_6_
  12.3 0.1 copy.37
  12.4 0.1 reshape.108
  12.5 0.1 copy.38
  12.6 0.7 reshape.109.refs_7_
  13.4 0.0 copy-done.8
  13.4 0.8 copy.46.refs_5_
  14.2 0.0 copy-done.6
  14.2 0.7 slice.60.refs_10_
  15.0 0.0 copy-done.7
  15.0 0.7 slice.46.refs_8_
  15.7 0.0 copy-done.5
  15.7 1.0 copy.41.refs_3_.refs_19_
  16.8 183.3 %forward.1 = (bf16[1152,3072]{1,0:T(8,128)(2,1)}, bf16[1152,1024]{1,0:T(8,128)(2,1)}, bf16[576,1024]{1,0:T(8,128)(2,1)}, bf16[1152,4096]{1,0:T(8,128)(2,1)}, bf1...) custom-call(bf16[512,1152]{1,0:T(8,128)(2,1)} %refs_0_.1, ...), custom_call_target="tpu_custom_call" | custom-call | tf_op jit(solution)/shard_map/forward/pallas_call | solution.py:721
  200.1 187.9 %backward.1 = (bf16[512,1152]{1,0:T(8,128)(2,1)}, bf16[512,1152]{1,0:T(8,128)(2,1)}, bf16[4,512,896]{2,1,0:T(8,128)(2,1)}, f32[288,576]{1,0:T(8,128)}, f32[288,5...) custom-call(bf16[3,4,1152,1152]{3,2,1,0:T(8,128)(2,1)} %get-tuple-el, ...), custom_call_target="tpu_custom_call" | custom-call | tf_op jit(solution)/shard_map/backward/pallas_call | solution.py:1426
  387.9 0.0 copy-start.2
  388.0 0.8 slice_reduce_fusion.2
  388.8 0.7 reshape_squeeze.7
  389.4 1.4 fusion
  390.9 1.3 slice_reduce_fusion.1
  392.2 0.8 slice_reduce_fusion
  392.9 0.7 reshape_squeeze.6
  393.6 1.4 slice.50
  395.0 1.8 copy.45
  396.8 0.0 copy-start
  396.8 2.2 copy.44
  399.0 0.0 copy-done.2
  399.0 1.5 copy.43
  400.5 0.0 copy-done
  400.5 0.0 copy-start.1
  400.5 1.6 convert_element_type.21
  402.1 0.2 copy-done.1
  402.2 0.0 copy-start.4
  402.3 0.0 copy-start.3
  402.3 1.0 copy.54
  403.3 0.5 copy-done.4
  403.8 0.9 copy.55
  404.7 0.0 copy-done.3
  404.7 0.9 copy.56
  (5 shorter events, 0.1 us)
Async XLA Ops:
  0.6 12.7 %copy-start.8 = (bf16[288,3,144]{0,2,1:T(8,128)(2,1)S(1)}, bf16[288,3,144]{0,2,1:T(8,128)(2,1)}, u32[]{:S(2)}) copy-start(bf16[288,3,144]{0,2,1:T(8,128)(2,1)} %param.17) | copy-start | bytes 746500
  5.1 9.2 %copy-start.6 = (bf16[576,288]{0,1:T(8,128)(2,1)S(1)}, bf16[576,288]{0,1:T(8,128)(2,1)}, u32[]{:S(2)}) copy-start(bf16[576,288]{0,1:T(8,128)(2,1)} %param.23) | copy-start | bytes 995332
  8.9 6.1 %copy-start.7 = (bf16[288,576]{1,0:T(8,128)(2,1)S(1)}, bf16[288,576]{1,0:T(8,128)(2,1)}, u32[]{:S(2)}) copy-start(bf16[288,576]{1,0:T(8,128)(2,1)} %param.21) | copy-start | bytes 995332
  11.6 4.1 %copy-start.5 = (bf16[288,6,144]{0,2,1:T(8,128)(2,1)S(1)}, bf16[288,6,144]{0,2,1:T(8,128)(2,1)}, u32[]{:S(2)}) copy-start(bf16[288,6,144]{0,2,1:T(8,128)(2,1)} %param.15) | copy-start | bytes 1492996
  387.9 11.1 %copy-start.2 = (f32[288,864]{1,0:T(8,128)S(1)}, f32[288,864]{1,0:T(8,128)}, u32[]{:S(2)}) copy-start(f32[288,864]{1,0:T(8,128)} %get-tuple-element.63) | copy-start | bytes 2985988
  396.8 3.7 copy-start
  400.5 1.7 copy-start.1
  402.2 1.5 copy-start.4
  402.3 2.4 copy-start.3

commit v5 on v4

--- a/solution.py
+++ b/solution.py
@@ -65,7 +65,7 @@
     def scratch(count, depth):
         dma = pltpu.SemaphoreType.DMA
         return [dma((count,)), dma((count, 2, depth)), dma((count, 2, depth)), dma((count, 2, depth)), dma((count, 2, depth, 2)),
-                dma((count, 2, depth, 4))]
+                dma((count, 2, depth, 2))]
 
     def block(self, a, p, q, z):
         y, x = self.at.yx(p, q)
@@ -109,7 +109,10 @@
         return self.copy(self.source(a, t, j), self.spot(a, t, j), self.ps, (a, self.zc(t), j), self.at.to_p)
 
     def c_k(self, a, t, j):
-        return self.copy(self.source(a, t, j), self.spot(a, t, j), self.ks, (a, self.zc(t), j), self.at.to_core)
+        rows, lanes = self.ins[a].shape
+        r = 2 * j + self.at.h
+        spot = block_at(self.outs[a], rows, 2 * lanes, r, self.zc(t))
+        return self.copy(spot, spot, self.ks, (a, self.zc(t), j), self.at.to_core)
 
     def start(self, a):
         self.c_q(a, 0).start()
@@ -131,23 +134,21 @@
                 self.r_z(a, t, 0).wait_recv()
                 pl.when(late)(self.c_q(a, t).start)
             self.c_p(a, t, 0).start()
-            self.c_k(a, t, 0).start()
         elif n == 1:
             pl.when(late)(self.c_q(a, t).wait_recv)
             if t > 0:
                 pl.when(self.early)(self.r_z(a, t, 1).wait_recv)
             self.c_p(a, t, 1).start()
-            self.c_k(a, t, 1).start()
         elif n == 2:
             self.c_p(a, t, 0).wait_recv()
-            self.c_k(a, t, 2).start()
+            if t == 0:
+                self.c_local(a).wait()
         elif n == 3:
             self.c_p(a, t, 1).wait_recv()
-            self.c_k(a, t, 3).start()
+            for j in range(2):
+                self.c_k(a, t, j).start()
         else:
-            if t == 0:
-                self.c_local(a).wait()
-            for j in range(4):
+            for j in range(2):
                 self.c_k(a, t, j).wait_recv()
 
     def finish(self, a):
@@ -168,7 +169,7 @@
         for t in range(self.at.depth):
             for j in range(2):
                 self.c_p(a, t, j).wait_send()
-            for j in range(4):
+            for j in range(2):
                 self.c_k(a, t, j).wait_send()
 
 
@@ -187,7 +188,7 @@
     def scratch(count, depth):
         dma = pltpu.SemaphoreType.DMA
         return [dma((count,)), dma((count, 2, 5)), dma((count, 2, 5)), dma((count, 2, depth)), dma((count, 2, depth, 2)),
-                dma((count, 2, depth, 4))]
+                dma((count, 2, depth, 2))]
 
     def early(self, a):
         return self.core0 if a in self.mid else jnp.logical_and(self.core0, False)
@@ -241,7 +242,6 @@
                 else:
                     self.c_q(a, t).start()
             self.c_p(a, t, 0).start()
-            self.c_k(a, t, 0).start()
         elif n == 1:
             if not mid:
                 self.c_q(a, t).wait_recv()
@@ -250,17 +250,16 @@
                 if t > 0:
                     pl.when(early)(lambda: self.z_got(a, t, 1))
             self.c_p(a, t, 1).start()
-            self.c_k(a, t, 1).start()
         elif n == 2:
             self.c_p(a, t, 0).wait_recv()
-            self.c_k(a, t, 2).start()
+            if t == 0:
+                self.c_local(a).wait()
         elif n == 3:
             self.c_p(a, t, 1).wait_recv()
-            self.c_k(a, t, 3).start()
+            for j in range(2):
+                self.c_k(a, t, j).start()
         else:
-            if t == 0:
-                self.c_local(a).wait()
-            for j in range(4):
+            for j in range(2):
                 self.c_k(a, t, j).wait_recv()
 
     def finish(self, a):
@@ -279,7 +278,7 @@
         for t in range(self.at.depth):
             for j in range(2):
                 self.c_p(a, t, j).wait_send()
-            for j in range(4):
+            for j in range(2):
                 self.c_k(a, t, j).wait_send()
 
 
@@ -351,13 +350,13 @@
         target[r * rows + half:(r + 1) * rows, :] = jnp.concatenate([tile[:, 64:128], tile[:, 192:]], axis=1).astype(bf16)
 
 
-GROUPS = (3, 2, 2)
+GROUPS = (2, 1, 1)
 
 
 def forward_kernel(*refs):
     lat, cot, cond, ada, bias = refs[:5]
-    blocks, refs = refs[5:12], refs[12:]
-    fulls, refs = refs[:7], refs[7:]
+    blocks, refs = refs[5:9], refs[9:]
+    fulls, refs = refs[:4], refs[4:]
     (o_w, o_cot, o_x, o_n1, o_q, o_k, o_v, o_k2, o_v2, o_lse, o_att, o_ba, o_mid, o_n2, o_hid, o_slo, o_out, o_vec, o_act), refs = refs[:19], refs[19:]
     (x_v, n1, q_v, k_v, v_v, k2_v, v2_v, lse_v, ot, att, ba, mid, n2, hid, slo, acc, wbuf, lbuf, out_v, cot_v, vec,
      c_send, c_recv, s_send, s_recv, m_own, m_oth), refs = refs[:27], refs[27:]
@@ -370,7 +369,7 @@
     tokens, width = x_v.shape
     hc = width // cols_n
     drows = ada.shape[0]
-    q_main, p_main = blocks[0].shape[1], blocks[1].shape[1]
+    q_main, p_main = 384, 128
     half = tokens // 2
 
     row_peers = [((row + k) % rows_n, col) for k in range(1, rows_n)]
@@ -399,8 +398,8 @@
     swap_x = Swap(place, lat, x_v, swap_sems, 0)
     swap_x.start()
 
-    work = LineGather(place, blocks, fulls, ag_sems, range(7))
-    for a in range(3):
+    work = LineGather(place, blocks, fulls, ag_sems, range(4))
+    for a in range(2):
         work.start(a)
 
     members, first = [], 0
@@ -512,14 +511,18 @@
     def fetch(s):
         g, t = chunks[s]
         zc, slot = work.zc(t), s % depth
-        lanes = [q_main, p_main] if g == 0 else [blocks[members[g][0]].shape[1]]
-        spot, copies = 0, []
-        for i, n in enumerate(lanes):
-            src = fulls[members[g][i]].at[:, pl.ds(pl.multiple_of(zc * 2 * n, 128), 2 * n)]
-            copies.append(pltpu.make_async_copy(src, wbuf.at[slot, :, spot:spot + 2 * n], w_sems.at[s % 2, i]))
-            spot += 2 * n
-        src = fulls[members[g][-1]].at[:, pl.ds(pl.multiple_of(zc * 256, 128), 256)]
-        copies.append(pltpu.make_async_copy(src, lbuf.at[s % 2], w_sems.at[s % 2, 2]))
+        main = fulls[members[g][0]]
+        if g == 0:
+            cuts = [(512 * i, q_main, q_main * i) for i in range(2)] + [(512 * i + q_main, p_main, 2 * q_main + p_main * i) for i in range(2)]
+        else:
+            cuts = [(256 * i, 256, 256 * i) for i in range(4)]
+        copies = []
+        for n, (spot, size, to) in enumerate(cuts):
+            src = main.at[:, pl.ds(pl.multiple_of(zc * 1024 + spot, 128), size)]
+            copies.append(pltpu.make_async_copy(src, wbuf.at[slot, :, to:to + size], w_sems.at[s % 2, n]))
+        for i in range(2):
+            src = fulls[1].at[:, pl.ds(pl.multiple_of(zc * 768 + 384 * i + 128 * g, 128), 128)]
+            copies.append(pltpu.make_async_copy(src, lbuf.at[s % 2, :, 128 * i:128 * (i + 1)], w_sems.at[s % 2, 4 + i]))
         return copies
 
     def fetch_start(s):
@@ -606,10 +609,11 @@
             else:
                 acc[at_rows, :] += term
 
+    fetch_start(0)
     for s in range(depth):
-        fetch_start(s)
         fetch_wait(s)
         project(s)
+        fetch_start(s + 1)
         if s > 0:
             attention(s - 1)
     attention(depth - 1)
@@ -629,8 +633,8 @@
         save(src, dst)
 
     for s in range(depth, 2 * depth):
-        fetch_start(s)
         fetch_wait(s)
+        fetch_start(s + 1)
         zc = work.zc(chunks[s][1])
 
         def up(at_rows):
@@ -643,8 +647,9 @@
     save(hid, o_hid)
     save(slo, o_slo)
     for s in range(2 * depth, 3 * depth):
-        fetch_start(s)
         fetch_wait(s)
+        if s + 1 < 3 * depth:
+            fetch_start(s + 1)
         zc = work.zc(chunks[s][1])
 
         def down(at_rows):
@@ -671,7 +676,7 @@
     save(out_v, o_out)
     save(vec, o_vec)
 
-    for a in range(7):
+    for a in range(4):
         work.finish(a)
     for k in range(1, rows_n):
         cond_copy(k).wait_send()
@@ -715,7 +720,7 @@
         t16, t16, vm((VECS, width), f32), vm((rows, 8, drows), f32), vm((rows, 8, drows), f32), vm((rows, 8, hc6), f32),
         vm((rows, 8, hc6), f32), vm((cols, 8, hc6), f32), vm((cols, 8, hc6), f32)]
     scratch += LineGather.scratch(len(blocks), depth)
-    scratch += [dma((2, 2)), dma((2, rows)), dma((2, rows)), dma((2, cols)), dma((2,)), dma((2, 2, heads)), dma((2, 3)), dma((32,)),
+    scratch += [dma((2, 2)), dma((2, rows)), dma((2, rows)), dma((2, cols)), dma((2,)), dma((2, 2, heads)), dma((2, 6)), dma((32,)),
                 dma((3 * depth,))]
     vmem = pl.BlockSpec(memory_space=pltpu.VMEM)
     got = pl.pallas_call(
@@ -1287,6 +1292,7 @@
     tick_b(10)
     attention_close(3)
     tick_prefetch(11)
+    tick_a(11)
     load_x.wait()
 
     def third(at_rows):
@@ -1296,7 +1302,6 @@
     row_parts(third)
     swap_lat = Swap(place, tmp.at[1], o_lat, swap_sems, 1)
     swap_lat.start()
-    tick_a(11)
 
     for c in range(cols_n):
         spot = slice(c * hc, (c + 1) * hc)
@@ -1514,9 +1519,10 @@
     q_main, p_main, f_main = 384, 128, 512
     qkv_flat = qkv_weight.reshape(depth, 3 * hc)
     proj_t, fc2_t = proj_weight.T, fc2_weight.T
-    left_a = fold(jnp.concatenate([qkv_flat[:, q_main:], proj_t[:, p_main:]], axis=1))
-    blocks = [qkv_flat[:, :q_main], proj_t[:, :p_main], left_a,
-              fc1_weight[:, :f_main], fold(fc1_weight[:, f_main:]), fc2_t[:, :f_main], fold(fc2_t[:, f_main:])]
+    main_a = jnp.concatenate([qkv_flat[:, :q_main], proj_t[:, :p_main]], axis=1)
+    left = jnp.concatenate([fold(jnp.concatenate([qkv_flat[:, q_main:], proj_t[:, p_main:]], axis=1)),
+                            fold(fc1_weight[:, f_main:]), fold(fc2_t[:, f_main:])], axis=1)
+    blocks = [main_a, left, fc1_weight[:, :f_main], fc2_t[:, :f_main]]
     cond = jnp.pad(condition.astype(f32), ((0, 8 - plan.lats), (0, 0)))
     ada = ada_weight.reshape(depth, 6 * hc)
     line = jnp.concatenate([fc1_bias, proj_bias, fc2_bias]).astype(f32).reshape(1, 6 * hc)

time: 411 us -> 397 us (0.966)
  Pallas kernels: 371 us -> 360 us
    pallas_call x1, Pallas kernels: 183 us -> 174 us  [forward(): pl.pallas_call(forward_kernel, out_shape=outs, in_specs=[ANY, ANY, vmem,...]
where the time goes in v5:
time: 397 us; the launch traced here: 392 us
  Pallas kernels  360 us (91%)
  local copies, waits for them, and re-layouts  26.2 us (7%)
  other arithmetic  5.07 us (1%)
    pallas_call x1, Pallas kernels, backward(): pl.pallas_call(backward_kernel, out_shape=outs, in_specs=[ANY] * 16 + [vm...  186 us
    pallas_call x1, Pallas kernels, forward(): pl.pallas_call(forward_kernel, out_shape=outs, in_specs=[ANY, ANY, vmem,...  174 us

profile of v5, /device:TPU:0, one launch (start us, length us, event | category | flops | bytes accessed | tf_op | source)
XLA Modules:
  0.0 392.0 jit_solution(3523127713891388099)
XLA Ops:
  0.6 0.0 copy-start.6
  0.7 0.0 copy-start.8
  0.7 0.1 pad.27.clone
  0.8 0.7 concatenate.29
  1.5 0.7 concatenate.30
  2.1 0.8 reshape.106
  2.9 0.7 concatenate.28
  3.6 0.1 maximum_convert_fusion
  3.6 0.8 reshape.116
  4.4 0.7 maximum_maximum_fusion.refs_4_
  5.1 1.3 pad_convert_fusion.refs_2_.refs_20_
  6.4 0.8 slice.58
  7.2 0.9 slice.60
  8.1 0.1 copy.49
  8.2 0.0 copy-start.7
  8.2 0.1 reshape.113
  8.3 0.9 slice.46
  9.2 0.1 copy.50
  9.2 0.1 reshape.111
  9.3 0.0 copy-start.5
  9.3 1.1 copy.36
  10.5 0.1 copy.37
  10.6 0.1 reshape.108
  10.6 0.1 copy.38
  10.8 0.1 reshape.109
  10.9 0.7 pad_maximum_fusion.1.refs_6_
  11.6 0.0 copy-done.8
  11.6 0.2 copy.46
  11.8 0.7 pad_maximum_fusion.refs_5_
  12.5 0.0 copy-done.6
  12.5 0.7 slice.61.refs_8_
  13.3 0.0 copy-done.7
  13.3 0.7 slice.48.refs_7_
  14.0 0.0 copy-done.5
  14.0 1.1 copy.41.refs_3_.refs_19_
  15.1 173.8 %forward.1 = (bf16[1152,4096]{1,0:T(8,128)(2,1)}, bf16[576,3072]{1,0:T(8,128)(2,1)}, bf16[1152,4096]{1,0:T(8,128)(2,1)}, bf16[1152,4096]{1,0:T(8,128)(2,1)}, bf1...) custom-call(bf16[512,1152]{1,0:T(8,128)(2,1)} %refs_0_.1, ...), custom_call_target="tpu_custom_call" | custom-call | tf_op jit(solution)/shard_map/forward/pallas_call | solution.py:726
  188.9 185.9 %backward.1 = (bf16[512,1152]{1,0:T(8,128)(2,1)}, bf16[512,1152]{1,0:T(8,128)(2,1)}, bf16[4,512,896]{2,1,0:T(8,128)(2,1)}, f32[288,576]{1,0:T(8,128)}, f32[288,5...) custom-call(bf16[3,4,1152,1152]{3,2,1,0:T(8,128)(2,1)} %get-tuple-el, ...), custom_call_target="tpu_custom_call" | custom-call | tf_op jit(solution)/shard_map/backward/pallas_call | solution.py:1431
  374.8 0.0 copy-start.2
  374.8 0.8 slice_reduce_fusion.2
  375.6 0.7 reshape_squeeze.7
  376.3 1.4 fusion
  377.7 0.0 copy-start
  377.7 1.4 slice_reduce_fusion.1
  379.1 0.8 slice_reduce_fusion
  379.9 0.7 reshape_squeeze.6
  380.6 1.4 slice.50
  382.0 1.8 copy.45
  383.7 2.1 copy.44
  385.9 0.0 copy-done.2
  385.9 1.5 copy.43
  387.4 0.0 copy-start.1
  387.4 0.0 copy-done
  387.4 0.0 copy-start.4
  387.4 1.6 convert_element_type.21
  389.0 0.1 copy-done.1
  389.1 0.0 copy-start.3
  389.1 1.0 copy.54
  390.1 0.0 copy-done.4
  390.1 0.9 copy.55
  391.0 0.0 copy-done.3
  391.0 0.9 copy.56
  (6 shorter events, 0.1 us)
Async XLA Ops:
  0.6 11.9 %copy-start.6 = (bf16[576,288]{0,1:T(8,128)(2,1)S(1)}, bf16[576,288]{0,1:T(8,128)(2,1)}, u32[]{:S(2)}) copy-start(bf16[576,288]{0,1:T(8,128)(2,1)} %param.23) | copy-start | bytes 995332
  0.7 10.9 %copy-start.8 = (bf16[288,3,144]{0,2,1:T(8,128)(2,1)S(1)}, bf16[288,3,144]{0,2,1:T(8,128)(2,1)}, u32[]{:S(2)}) copy-start(bf16[288,3,144]{0,2,1:T(8,128)(2,1)} %param.17) | copy-start | bytes 746500
  8.2 5.1 %copy-start.7 = (bf16[288,576]{1,0:T(8,128)(2,1)S(1)}, bf16[288,576]{1,0:T(8,128)(2,1)}, u32[]{:S(2)}) copy-start(bf16[288,576]{1,0:T(8,128)(2,1)} %param.21) | copy-start | bytes 995332
  9.3 4.7 %copy-start.5 = (bf16[288,6,144]{0,2,1:T(8,128)(2,1)S(1)}, bf16[288,6,144]{0,2,1:T(8,128)(2,1)}, u32[]{:S(2)}) copy-start(bf16[288,6,144]{0,2,1:T(8,128)(2,1)} %param.15) | copy-start | bytes 1492996
  374.8 11.1 %copy-start.2 = (f32[288,864]{1,0:T(8,128)S(1)}, f32[288,864]{1,0:T(8,128)}, u32[]{:S(2)}) copy-start(f32[288,864]{1,0:T(8,128)} %get-tuple-element.63) | copy-start | bytes 2985988
  377.7 9.7 %copy-start = (bf16[512,1152]{1,0:T(8,128)(2,1)S(1)}, bf16[512,1152]{1,0:T(8,128)(2,1)}, u32[]{:S(2)}) copy-start(bf16[512,1152]{1,0:T(8,128)(2,1)} %get-tuple-element.61) | copy-start | bytes 3538948
  387.4 1.7 copy-start.1
  387.4 2.7 copy-start.4
  389.1 1.9 copy-start.3

commit v6 on v5

--- a/solution.py
+++ b/solution.py
@@ -174,10 +174,10 @@
 
 
 class LineGather(Gather):
-    def __init__(self, place, ins, outs, sems, mid=()):
+    def __init__(self, place, ins, outs, sems, mid=(), both=()):
         super().__init__(place, ins, outs, sems)
         z = place.z
-        self.core0, self.mid = place.h == 0, mid
+        self.core0, self.mid, self.both = place.h == 0, mid, both
         self.middle = jnp.logical_and(z > 0, z < place.depth - 1)
         low = z < 2
         self.inner = place.to_z(jnp.where(low, z + 1, z - 1))
@@ -190,8 +190,8 @@
         return [dma((count,)), dma((count, 2, 5)), dma((count, 2, 5)), dma((count, 2, depth)), dma((count, 2, depth, 2)),
                 dma((count, 2, depth, 2))]
 
-    def early(self, a):
-        return self.core0 if a in self.mid else jnp.logical_and(self.core0, False)
+    def z_first(self, a):
+        return self.at.h < 2 if a in self.both else self.core0
 
     def zc(self, t):
         return self.order[t]
@@ -226,13 +226,13 @@
 
     def forward(self, a):
         if a in self.mid:
-            @pl.when(self.core0)
+            @pl.when(self.z_first(a))
             def _():
                 self.c_q(a, 0).wait_recv()
                 self.z_start(a, 1)
 
     def stage(self, a, t, n):
-        mid, early = a in self.mid, self.core0
+        mid, early = a in self.mid, self.z_first(a)
         late = jnp.logical_not(early)
         if n == 0:
             if t > 0:
@@ -271,8 +271,8 @@
                 self.c_q(a, t).wait_send()
 
         if a in self.mid:
-            pl.when(self.core0)(lambda: self.z_sent(a, 1))
-            pl.when(jnp.logical_not(self.core0))(rest)
+            pl.when(self.z_first(a))(lambda: self.z_sent(a, 1))
+            pl.when(jnp.logical_not(self.z_first(a)))(rest)
         else:
             rest()
         for t in range(self.at.depth):
@@ -398,7 +398,7 @@
     swap_x = Swap(place, lat, x_v, swap_sems, 0)
     swap_x.start()
 
-    work = LineGather(place, blocks, fulls, ag_sems, range(4))
+    work = LineGather(place, blocks, fulls, ag_sems, range(4), (2,))
     for a in range(2):
         work.start(a)
 
@@ -1130,15 +1130,15 @@
     tick_b(0)
     hidden_back(1)
     hidden_back(2)
+    hidden_back(3)
     tick_a(1)
-    hidden_back(3)
+    normed_back(depth)
     tick_b(1)
-    normed_back(depth)
     normed_back(depth + 1)
+    normed_back(depth + 2)
     tick_a(2)
-    normed_back(depth + 2)
+    normed_back(depth + 3)
     tick_b(2)
-    normed_back(depth + 3)
 
     load_mid = pltpu.make_async_copy(mid_h, gm, tmp_sems.at[2])
     load_mid.start()
@@ -1270,25 +1270,27 @@
     load_n2.wait()
     turn_into(0, tmp.at[0])
     load_x, load_n1 = load(x_h, 0), load(n1_h, 1)
+    attention_open(0)
     tick_b(3)
-    attention_open(0)
-    attention_heads(0, [(1, lambda: tick_a(4)), (3, lambda: tick_b(4))])
+    attention_heads(0, [(2, lambda: tick_a(4))])
+    tick_b(4)
     attention_close(0)
     attention_open(1)
     tick_a(5)
-    attention_heads(1, [(0, lambda: tick_b(5)), (2, lambda: tick_a(6)), (3, lambda: tick_b(6))])
+    attention_heads(1, [(1, lambda: tick_b(5)), (3, lambda: tick_a(6))])
     attention_close(1)
+    tick_b(6)
     tick_a(7)
     load_n1.wait()
     turn_into(1, tmp.at[1])
     turn_into(0, ml)
     attention_open(2)
-    attention_heads(2, [(0, lambda: tick_b(7)), (2, lambda: tick_a(8))])
+    attention_heads(2, [(1, lambda: tick_b(7)), (3, lambda: tick_a(8))])
+    attention_close(2)
     tick_b(8)
-    attention_close(2)
     attention_open(3)
     tick_a(9)
-    attention_heads(3, [(0, lambda: tick_b(9)), (2, lambda: tick_a(10))])
+    attention_heads(3, [(1, lambda: tick_b(9)), (2, lambda: tick_a(10))])
     tick_b(10)
     attention_close(3)
     tick_prefetch(11)
@@ -1299,9 +1301,15 @@
         grad = norm_grad(tmp[0, at_rows, :].astype(f32), gx[at_rows, :], 0, 1, vec[1:2, :]) + gm[at_rows, :]
         tmp[1, at_rows, :] = grad.astype(bf16)
 
-    row_parts(third)
-    swap_lat = Swap(place, tmp.at[1], o_lat, swap_sems, 1)
-    swap_lat.start()
+    def swap_lat(i):
+        at_rows = pl.ds(pl.multiple_of(i * part, part), part)
+        return Swap(place, tmp.at[1, at_rows], o_lat.at[at_rows], swap_sems, 1 + i)
+
+    @pl.loop(0, tokens // part)
+    def _(i):
+        third(pl.ds(pl.multiple_of(i * part, part), part))
+        swap_lat(i).start()
+
 
     for c in range(cols_n):
         spot = slice(c * hc, (c + 1) * hc)
@@ -1396,7 +1404,8 @@
     copy_v.wait_send()
     for k in range(1, rows_n):
         cf_copy(k).wait_send()
-    swap_lat.wait()
+    for i in range(tokens // part):
+        swap_lat(i).wait()
     swap_out.wait()
 
 
@@ -1424,7 +1433,7 @@
         vm((cols, 8, hc6), f32), vm((cols, 8, hc6), f32), vm((cols, 8, hc6), f32), vm((cols, 8, hc6), f32), vm((rows, 8, hc6), f32),
         vm((rows, 8, drows), f32), vm((cols, rows, 8, drows), f32), vm((rows, 8, drows), f32)]
     scratch += [
-        dma((2, 2)), dma((2, 2, 2)), dma((2, 4, 2, 2)), dma((2, 4, 2)), dma((2, 2, 9, depth, 2)), dma((2, 3)), dma((2,)), dma((2, 2)),
+        dma((1 + tokens // 128, 2)), dma((2, 2, 2)), dma((2, 4, 2, 2)), dma((2, 4, 2)), dma((2, 2, 9, depth, 2)), dma((2, 3)), dma((2,)), dma((2, 2)),
         dma((depth,)), dma((3,)), dma((5,)), dma((2, 2, 2, 4)), dma((depth,)), dma((2,)), dma((2, cols)), dma((2,)), dma((2, cols)),
         dma((2, rows)), dma((2,))]
     vmem = pl.BlockSpec(memory_space=pltpu.VMEM)
@@ -1525,8 +1534,9 @@
     blocks = [main_a, left, fc1_weight[:, :f_main], fc2_t[:, :f_main]]
     cond = jnp.pad(condition.astype(f32), ((0, 8 - plan.lats), (0, 0)))
     ada = ada_weight.reshape(depth, 6 * hc)
-    line = jnp.concatenate([fc1_bias, proj_bias, fc2_bias]).astype(f32).reshape(1, 6 * hc)
-    tail = jnp.pad(qv_bias.astype(f32).reshape(1, 2 * hc), ((0, 0), (0, 4 * hc)))
+    flat = lax.optimization_barrier(jnp.concatenate([fc1_bias, proj_bias, fc2_bias, qv_bias.reshape(-1)]).astype(f32))
+    line = flat[:6 * hc].reshape(1, 6 * hc)
+    tail = jnp.pad(flat[6 * hc:].reshape(1, 2 * hc), ((0, 0), (0, 4 * hc)))
     bias = jnp.concatenate([jnp.broadcast_to(ada_bias.astype(f32).reshape(1, 6 * hc), (plan.lats, 6 * hc)), line, tail,
                             jnp.zeros((8 - plan.lats - 2, 6 * hc), f32)], axis=0)
     (w, dy, x, n1, q, k, v, k2, v2, lse, att, ba, mid, n2, hid, slo, out, vec, act) = forward(

time: 397 us -> 396 us (level)
  no operation moved by 1% of the time
where the time goes in v6:
time: 396 us; the launch traced here: 390 us
  Pallas kernels  358 us (90%)
  local copies, waits for them, and re-layouts  26.4 us (7%)
  other arithmetic  5 us (1%)
    pallas_call x1, Pallas kernels, backward(): pl.pallas_call(backward_kernel, out_shape=outs, in_specs=[ANY] * 16 + [vm...  186 us
    pallas_call x1, Pallas kernels, forward(): pl.pallas_call(forward_kernel, out_shape=outs, in_specs=[ANY, ANY, vmem,...  172 us

profile of v6, /device:TPU:0, one launch (start us, length us, event | category | flops | bytes accessed | tf_op | source)
XLA Modules:
  0.0 390.2 jit_solution(4956193624406910744)
XLA Ops:
  0.6 0.0 copy-start.6
  0.7 0.0 copy-start.8
  0.7 0.1 pad.23.clone
  0.8 0.8 reshape.68
  1.6 2.1 concatenate.15
  3.7 0.1 slice.65
  3.8 0.8 reshape.80
  4.5 0.7 fusion.refs_4_
  5.2 1.3 pad_convert_fusion.refs_2_.refs_20_
  6.6 0.8 slice.68
  7.3 0.9 slice.70
  8.2 0.1 copy.49
  8.3 0.0 copy-start.7
  8.3 0.1 reshape.77
  8.4 0.9 slice.54
  9.3 0.1 copy.50
  9.3 0.1 reshape.75
  9.4 0.0 copy-start.5
  9.5 1.1 copy.36
  10.6 0.1 copy.37
  10.7 0.1 reshape.72
  10.8 0.1 copy.38
  10.9 0.1 reshape.73
  11.0 0.7 pad_maximum_fusion.1.refs_6_
  11.7 0.0 copy-done.8
  11.7 0.2 copy.46
  11.9 0.7 pad_maximum_fusion.refs_5_
  12.6 0.0 copy-done.6
  12.6 0.7 slice.71.refs_8_
  13.4 0.0 copy-done.7
  13.4 0.7 slice.56.refs_7_
  14.1 0.0 copy-done.5
  14.1 1.1 copy.41.refs_3_.refs_19_
  15.2 172.2 %forward.1 = (bf16[1152,4096]{1,0:T(8,128)(2,1)}, bf16[576,3072]{1,0:T(8,128)(2,1)}, bf16[1152,4096]{1,0:T(8,128)(2,1)}, bf16[1152,4096]{1,0:T(8,128)(2,1)}, bf1...) custom-call(bf16[512,1152]{1,0:T(8,128)(2,1)} %refs_0_.1, ...), custom_call_target="tpu_custom_call" | custom-call | tf_op jit(solution)/shard_map/forward/pallas_call | solution.py:726
  187.4 185.6 %backward.1 = (bf16[512,1152]{1,0:T(8,128)(2,1)}, bf16[512,1152]{1,0:T(8,128)(2,1)}, bf16[4,512,896]{2,1,0:T(8,128)(2,1)}, f32[288,576]{1,0:T(8,128)}, f32[288,5...) custom-call(bf16[3,4,1152,1152]{3,2,1,0:T(8,128)(2,1)} %get-tuple-el, ...), custom_call_target="tpu_custom_call" | custom-call | tf_op jit(solution)/shard_map/backward/pallas_call | solution.py:1440
  373.0 0.0 copy-start.2
  373.0 0.8 slice_reduce_fusion.2
  373.8 0.7 reshape_squeeze.7
  374.4 1.4 fusion.2
  375.9 0.0 copy-start
  375.9 1.4 slice_reduce_fusion.1
  377.3 0.8 slice_reduce_fusion
  378.1 0.7 reshape_squeeze.6
  378.7 1.4 slice.58
  380.1 1.8 copy.45
  381.9 2.1 copy.44
  384.0 0.0 copy-done.2
  384.1 1.5 copy.43
  385.5 0.0 copy-start.1
  385.5 0.0 copy-done
  385.5 0.0 copy-start.4
  385.5 1.6 convert_element_type.13
  387.1 0.1 copy-done.1
  387.2 0.0 copy-start.3
  387.2 1.0 copy.54
  388.3 0.0 copy-done.4
  388.3 0.9 copy.55
  389.1 0.0 copy-done.3
  389.1 0.9 copy.56
  (10 shorter events, 0.1 us)
Async XLA Ops:
  0.6 12.0 %copy-start.6 = (bf16[576,288]{0,1:T(8,128)(2,1)S(1)}, bf16[576,288]{0,1:T(8,128)(2,1)}, u32[]{:S(2)}) copy-start(bf16[576,288]{0,1:T(8,128)(2,1)} %param.23) | copy-start | bytes 995332
  0.7 11.0 %copy-start.8 = (bf16[288,3,144]{0,2,1:T(8,128)(2,1)S(1)}, bf16[288,3,144]{0,2,1:T(8,128)(2,1)}, u32[]{:S(2)}) copy-start(bf16[288,3,144]{0,2,1:T(8,128)(2,1)} %param.17) | copy-start | bytes 746500
  8.3 5.1 %copy-start.7 = (bf16[288,576]{1,0:T(8,128)(2,1)S(1)}, bf16[288,576]{1,0:T(8,128)(2,1)}, u32[]{:S(2)}) copy-start(bf16[288,576]{1,0:T(8,128)(2,1)} %param.21) | copy-start | bytes 995332
  9.4 4.7 %copy-start.5 = (bf16[288,6,144]{0,2,1:T(8,128)(2,1)S(1)}, bf16[288,6,144]{0,2,1:T(8,128)(2,1)}, u32[]{:S(2)}) copy-start(bf16[288,6,144]{0,2,1:T(8,128)(2,1)} %param.15) | copy-start | bytes 1492996
  373.0 11.1 %copy-start.2 = (f32[288,864]{1,0:T(8,128)S(1)}, f32[288,864]{1,0:T(8,128)}, u32[]{:S(2)}) copy-start(f32[288,864]{1,0:T(8,128)} %get-tuple-element.63) | copy-start | bytes 2985988
  375.9 9.7 %copy-start = (bf16[512,1152]{1,0:T(8,128)(2,1)S(1)}, bf16[512,1152]{1,0:T(8,128)(2,1)}, u32[]{:S(2)}) copy-start(bf16[512,1152]{1,0:T(8,128)(2,1)} %get-tuple-element.61) | copy-start | bytes 3538948
  385.5 1.7 copy-start.1
  385.5 2.7 copy-start.4
  387.2 1.9 copy-start.3
